TPU v7x, 128 devices: a whole 4x4x4 slice. The times are simulated.
128 devices in a mesh: blk: 8 (over x_lo, y), head: 16 (over z, x_hi, core).
Axes of the slice: x: 4 (x_hi: 2, x_lo: 2; x = x_hi * 2 + x_lo), y: 4, z: 4, core: 2. Of those that a mesh axis runs over, the one named last changes fastest.
Arguments:
- queries: bfloat16 [16384, 4096], P(('blk', 'head')), may hold values from -13 to 13
- keys: bfloat16 [16384, 512], P(('blk', 'head')), may hold values from -13 to 13
- values: bfloat16 [16384, 512], P(('blk', 'head')), may hold values from -6 to 6
- positions: int32 [3, 16384], P(None, ('blk', 'head')), may hold values from 0 to 63
- block_order: int32 [16], replicated, may hold values from 0 to 15, each once
Outputs:
- attended: bfloat16 [16384, 4096], P(('blk', 'head'))
All inputs are finite; a program needn't handle non-finite values.
Results may differ from a plain program's by a relative error of at most 0.006.
Values may be sent and summed in bfloat16 or wider, within the bound.
No kernel may reach another device: no remote copies, remote signals or barrier semaphores. Data moves between devices by JAX's collectives and lax.ppermute only.
A program may use at most 64 MiB of HBM per device.

v0:
```python
import math

import jax
import jax.numpy as jnp
from jax import lax
from jax.sharding import PartitionSpec as P

HD = 128


rope_base = 1000000.0


def rotate_heads(tensor, positions):
    head_dim = tensor.shape[-1]
    half_dim = head_dim // 2
    pair_index = jnp.arange(half_dim, dtype=jnp.int32)
    inverse = jnp.exp(pair_index.astype(jnp.float32) * (-2.0 * math.log(rope_base) / head_dim))
    first_end = head_dim // 8
    second_end = first_end + 3 * head_dim // 16
    picked = jnp.where(
        pair_index[None, :] < first_end,
        positions[0][:, None],
        jnp.where(pair_index[None, :] < second_end, positions[1][:, None], positions[2][:, None]),
    )
    angles = picked.astype(jnp.float32) * inverse[None, :]
    cosine_table = jnp.cos(angles)[:, None, :]
    sine_table = jnp.sin(angles)[:, None, :]
    lower_half = tensor[..., :half_dim]
    upper_half = tensor[..., half_dim:]
    return jnp.concatenate(
        [
            lower_half * cosine_table - upper_half * sine_table,
            upper_half * cosine_table + lower_half * sine_table,
        ],
        axis=-1,
    )


def update_part(state_part, query_tile, query_pos, key_tile, value_tile, key_pos, scale):
    peaks, totals, sums = state_part
    scores = (
        jnp.einsum("hqd,kd->hqk", query_tile, key_tile, preferred_element_type=jnp.float32) * scale
    )
    allowed = key_pos[None, None, :] <= query_pos[None, :, None]
    scores = jnp.where(allowed, scores, -1e30)
    new_peaks = jnp.maximum(peaks, jnp.max(scores, axis=-1))
    weights = jnp.where(allowed, jnp.exp(scores - new_peaks[..., None]), 0.0)
    factor = jnp.exp(peaks - new_peaks)
    new_totals = totals * factor + jnp.sum(weights, axis=-1)
    new_sums = sums * factor[..., None] + jnp.einsum(
        "hqk,kd->hqd", weights.astype(jnp.bfloat16), value_tile, preferred_element_type=jnp.float32
    )
    return (new_peaks, new_totals, new_sums)


def attend_piece(state, piece, query_tiles, query_pos, block_order, half_rows, scale):
    key_piece, value_piece = piece
    piece_rows = key_piece.shape[0]
    step_rows = math.gcd(piece_rows, half_rows)
    labels = jnp.arange(block_order.shape[0], dtype=jnp.int32)

    def advance(step_index, carried):
        offset = step_index * step_rows
        key_tile = lax.dynamic_slice_in_dim(key_piece, offset, step_rows, 0)
        value_tile = lax.dynamic_slice_in_dim(value_piece, offset, step_rows, 0)
        row_ids = offset + jnp.arange(step_rows, dtype=jnp.int32)
        owner = row_ids // half_rows
        mapped = jnp.sum(
            jnp.where(owner[:, None] == labels[None, :], block_order[None, :], 0), axis=1
        )
        key_pos = mapped * half_rows + row_ids % half_rows
        peaks, totals, sums = carried
        new_peaks, new_totals, new_sums = ([], [], [])
        for part_index in range(2):
            state_part = (peaks[part_index], totals[part_index], sums[part_index])

            def compute(
                operand,
                part_index=part_index,
                key_tile=key_tile,
                value_tile=value_tile,
                key_pos=key_pos,
            ):
                return update_part(
                    operand,
                    query_tiles[part_index],
                    query_pos[part_index],
                    key_tile,
                    value_tile,
                    key_pos,
                    scale,
                )

            def keep_state(operand):
                return operand

            result = lax.cond(
                jnp.min(key_pos) <= jnp.max(query_pos[part_index]), compute, keep_state, state_part
            )
            new_peaks.append(result[0])
            new_totals.append(result[1])
            new_sums.append(result[2])
        return (jnp.stack(new_peaks), jnp.stack(new_totals), jnp.stack(new_sums))

    return lax.fori_loop(0, piece_rows // step_rows, advance, state)


def per_device(queries, keys, values, positions, block_order):
    head_count = lax.axis_size("head")
    count_rows = queries.shape[0]
    query_heads = queries.shape[1] // HD
    value_heads = keys.shape[1] // HD
    copies_each = head_count // value_heads
    local_heads = query_heads // head_count
    scale = 1.0 / math.sqrt(HD)

    def widen(tensor):
        shaped = tensor.reshape(count_rows, value_heads, HD)
        return jnp.repeat(shaped, copies_each, axis=1).reshape(count_rows, head_count * HD)

    rot_queries = rotate_heads(
        queries.reshape(count_rows, query_heads, HD).astype(jnp.float32), positions
    )
    rot_queries = rot_queries.astype(jnp.bfloat16).reshape(count_rows, query_heads * HD)
    rot_keys = rotate_heads(
        keys.reshape(count_rows, value_heads, HD).astype(jnp.float32), positions
    )
    rot_keys = rot_keys.astype(jnp.bfloat16).reshape(count_rows, value_heads * HD)
    query_local, key_local, value_local = (
        lax.all_to_all(rot_queries, "head", split_axis=1, concat_axis=0, tiled=True),
        lax.all_to_all(widen(rot_keys), "head", split_axis=1, concat_axis=0, tiled=True),
        lax.all_to_all(widen(values), "head", split_axis=1, concat_axis=0, tiled=True),
    )
    block_rows = query_local.shape[0]
    query_local = query_local.reshape(block_rows, local_heads, HD)
    half_rows = block_rows // 2
    blk_index = lax.axis_index("blk")
    query_tiles = jnp.transpose(query_local.reshape(2, half_rows, local_heads, HD), (0, 2, 1, 3))
    offsets = jnp.arange(half_rows, dtype=jnp.int32)
    query_pos = [
        lax.dynamic_index_in_dim(block_order, 2 * blk_index + part_index, 0, keepdims=False)
        * half_rows
        + offsets
        for part_index in range(2)
    ]
    initial = (
        jnp.full((2, local_heads, half_rows), -1e30, jnp.float32),
        jnp.zeros((2, local_heads, half_rows), jnp.float32),
        jnp.zeros((2, local_heads, half_rows, HD), jnp.float32),
    )
    final_state = attend_piece(
        initial,
        (
            lax.all_gather(key_local, "blk", axis=0, tiled=True),
            lax.all_gather(value_local, "blk", axis=0, tiled=True),
        ),
        query_tiles,
        query_pos,
        block_order,
        half_rows,
        scale,
    )
    peaks, totals, sums = final_state
    mixed = (sums / totals[..., None]).astype(jnp.bfloat16)
    mixed = jnp.transpose(mixed, (0, 2, 1, 3)).reshape(block_rows, local_heads * HD)
    return lax.all_to_all(mixed, "head", split_axis=0, concat_axis=1, tiled=True)


def solution(mesh):
    return jax.shard_map(
        per_device,
        mesh=mesh,
        in_specs=(
            P(("blk", "head"), None),
            P(("blk", "head"), None),
            P(("blk", "head"), None),
            P(None, ("blk", "head")),
            P(),
        ),
        out_specs=P(("blk", "head"), None),
        check_vma=False,
    )
```

profile of v0, /device:TPU:24, one launch (start us, length us, event | category | flops | bytes accessed | tf_op | source)
XLA Modules:
  0.0 694.2 jit_solution(16523836798982500714)
XLA Ops:
  9.4 20.1 %all_to_all.70 = bf16[128,16,128]{2,0,1:T(8,128)(2,1)} all-to-all(bf16[128,16,128]{2,0,1:T(8,128)(2,1)S(1)} %bitcast.94), channel_id=1, replica_groups=mesh['blk'=8,'head'=16] {'head'}, dimensions={1} | all-to-all | bytes 1048576 | tf_op jit(solution)/shard_map/all_to_all | solution.py:132
  29.8 20.8 %all_to_all.71 = bf16[128,16,128]{2,0,1:T(8,128)(2,1)} all-to-all(bf16[128,16,128]{2,0,1:T(8,128)(2,1)S(1)} %bitcast.95), channel_id=1, replica_groups=mesh['blk'=8,'head'=16] {'head'}, dimensions={1} | all-to-all | bytes 1048576 | tf_op jit(solution)/shard_map/all_to_all | solution.py:133
  59.8 26.8 %all-to-all-done.2 = bf16[128,16,256]{0,2,1:T(8,128)(2,1)S(1)} async-done(((bf16[128,16,256]{0,2,1:T(8,128)(2,1)}), bf16[128,16,256]{0,2,1:T(8,128)(2,1)S(1)}, u32[]{:S(2)}, u32[]{:S(2)}) %all-to-all-start.2) | async-done | bytes 1048608 | tf_op jit(solution)/shard_map/all_to_all | solution.py:131
  92.4 53.1 %all-gather.5.cloned.1.call-done = bf16[16384,128]{1,0:T(8,128)(2,1)} async-done(((bf16[2048,128]{1,0:T(8,128)(2,1)}), bf16[16384,128]{1,0:T(8,128)(2,1)}) %all-gather.5.cloned.1.call-update) | async-done | bytes 4194320 | tf_op jit(solution)/shard_map/all_gather | solution.py:156
  147.0 509.9 %while.20 = (s32[]{:T(128)}, f32[2,2,1024]{2,1,0:T(2,128)S(1)}, f32[2,2,1024]{2,1,0:T(2,128)S(1)}, f32[2,2,1024,128]{3,2,1,0:T(8,128)}, s32[16]{0:T(128)S(1)}, /...) while((s32[]{:T(128)}, f32[2,2,1024]{2,1,0:T(2,128)S(1)}, ...), condition=%wide.region_13.14_spmd.clone, body=%wide.region_2.13_spmd.clone.sunk | while | flops 2205777920 | bytes 74904104 | solution.py:106
  153.1 11.9 %conditional.6 = (f32[1,2,1024]{2,1,0:T(2,128)}, f32[1,2,1024]{2,1,0:T(2,128)S(1)}, f32[1,2,1024,128]{3,2,1,0:T(8,128)S(1)}) conditional(s32[]{:T(128)} %convert_element_type.102, (f32[2,1024]{1,0:T(2,128)}, f32[2,1024]{1,0:T(2,128)S(1)}, f32[2,1024,128]{2,1,0:T(8,128)S(1)}) %tuple.150, (s32[1024]{0:T(1024)S(1)}, s32[]{:T(128)}, ...), branch_computations={%region_9.9_spmd, %region_10.12_spmd} | conditional | flops 1102582784 | bytes 32636956 | solution.py:98
  166.9 11.9 %conditional.7 = (f32[1,2,1024]{2,1,0:T(2,128)}, f32[1,2,1024]{2,1,0:T(2,128)S(1)}, f32[1,2,1024,128]{3,2,1,0:T(8,128)S(1)}) conditional(s32[]{:T(128)} %convert_element_type.103, (f32[2,1024]{1,0:T(2,128)}, f32[2,1024]{1,0:T(2,128)S(1)}, f32[2,1024,128]{2,1,0:T(8,128)S(1)}) %tuple.152, (s32[1024]{0:T(1024)S(1)}, s32[]{:T(128)}, ...), branch_computations={%region_5.5_spmd, %region_6.8_spmd} | conditional | flops 1102582784 | bytes 32636956 | solution.py:98
  187.2 11.9 %conditional.6 = (f32[1,2,1024]{2,1,0:T(2,128)}, f32[1,2,1024]{2,1,0:T(2,128)S(1)}, f32[1,2,1024,128]{3,2,1,0:T(8,128)S(1)}) conditional(s32[]{:T(128)} %convert_element_type.102, (f32[2,1024]{1,0:T(2,128)}, f32[2,1024]{1,0:T(2,128)S(1)}, f32[2,1024,128]{2,1,0:T(8,128)S(1)}) %tuple.150, (s32[1024]{0:T(1024)S(1)}, s32[]{:T(128)}, ...), branch_computations={%region_9.9_spmd, %region_10.12_spmd} | conditional | flops 1102582784 | bytes 32636956 | solution.py:98
  201.0 11.9 %conditional.7 = (f32[1,2,1024]{2,1,0:T(2,128)}, f32[1,2,1024]{2,1,0:T(2,128)S(1)}, f32[1,2,1024,128]{3,2,1,0:T(8,128)S(1)}) conditional(s32[]{:T(128)} %convert_element_type.103, (f32[2,1024]{1,0:T(2,128)}, f32[2,1024]{1,0:T(2,128)S(1)}, f32[2,1024,128]{2,1,0:T(8,128)S(1)}) %tuple.152, (s32[1024]{0:T(1024)S(1)}, s32[]{:T(128)}, ...), branch_computations={%region_5.5_spmd, %region_6.8_spmd} | conditional | flops 1102582784 | bytes 32636956 | solution.py:98
  221.3 11.9 %conditional.6 = (f32[1,2,1024]{2,1,0:T(2,128)}, f32[1,2,1024]{2,1,0:T(2,128)S(1)}, f32[1,2,1024,128]{3,2,1,0:T(8,128)S(1)}) conditional(s32[]{:T(128)} %convert_element_type.102, (f32[2,1024]{1,0:T(2,128)}, f32[2,1024]{1,0:T(2,128)S(1)}, f32[2,1024,128]{2,1,0:T(8,128)S(1)}) %tuple.150, (s32[1024]{0:T(1024)S(1)}, s32[]{:T(128)}, ...), branch_computations={%region_9.9_spmd, %region_10.12_spmd} | conditional | flops 1102582784 | bytes 32636956 | solution.py:98
  255.4 11.9 %conditional.6 = (f32[1,2,1024]{2,1,0:T(2,128)}, f32[1,2,1024]{2,1,0:T(2,128)S(1)}, f32[1,2,1024,128]{3,2,1,0:T(8,128)S(1)}) conditional(s32[]{:T(128)} %convert_element_type.102, (f32[2,1024]{1,0:T(2,128)}, f32[2,1024]{1,0:T(2,128)S(1)}, f32[2,1024,128]{2,1,0:T(8,128)S(1)}) %tuple.150, (s32[1024]{0:T(1024)S(1)}, s32[]{:T(128)}, ...), branch_computations={%region_9.9_spmd, %region_10.12_spmd} | conditional | flops 1102582784 | bytes 32636956 | solution.py:98
  289.5 11.9 %conditional.6 = (f32[1,2,1024]{2,1,0:T(2,128)}, f32[1,2,1024]{2,1,0:T(2,128)S(1)}, f32[1,2,1024,128]{3,2,1,0:T(8,128)S(1)}) conditional(s32[]{:T(128)} %convert_element_type.102, (f32[2,1024]{1,0:T(2,128)}, f32[2,1024]{1,0:T(2,128)S(1)}, f32[2,1024,128]{2,1,0:T(8,128)S(1)}) %tuple.150, (s32[1024]{0:T(1024)S(1)}, s32[]{:T(128)}, ...), branch_computations={%region_9.9_spmd, %region_10.12_spmd} | conditional | flops 1102582784 | bytes 32636956 | solution.py:98
  323.6 11.9 %conditional.6 = (f32[1,2,1024]{2,1,0:T(2,128)}, f32[1,2,1024]{2,1,0:T(2,128)S(1)}, f32[1,2,1024,128]{3,2,1,0:T(8,128)S(1)}) conditional(s32[]{:T(128)} %convert_element_type.102, (f32[2,1024]{1,0:T(2,128)}, f32[2,1024]{1,0:T(2,128)S(1)}, f32[2,1024,128]{2,1,0:T(8,128)S(1)}) %tuple.150, (s32[1024]{0:T(1024)S(1)}, s32[]{:T(128)}, ...), branch_computations={%region_9.9_spmd, %region_10.12_spmd} | conditional | flops 1102582784 | bytes 32636956 | solution.py:98
  357.7 11.9 %conditional.6 = (f32[1,2,1024]{2,1,0:T(2,128)}, f32[1,2,1024]{2,1,0:T(2,128)S(1)}, f32[1,2,1024,128]{3,2,1,0:T(8,128)S(1)}) conditional(s32[]{:T(128)} %convert_element_type.102, (f32[2,1024]{1,0:T(2,128)}, f32[2,1024]{1,0:T(2,128)S(1)}, f32[2,1024,128]{2,1,0:T(8,128)S(1)}) %tuple.150, (s32[1024]{0:T(1024)S(1)}, s32[]{:T(128)}, ...), branch_computations={%region_9.9_spmd, %region_10.12_spmd} | conditional | flops 1102582784 | bytes 32636956 | solution.py:98
  391.8 11.9 %conditional.6 = (f32[1,2,1024]{2,1,0:T(2,128)}, f32[1,2,1024]{2,1,0:T(2,128)S(1)}, f32[1,2,1024,128]{3,2,1,0:T(8,128)S(1)}) conditional(s32[]{:T(128)} %convert_element_type.102, (f32[2,1024]{1,0:T(2,128)}, f32[2,1024]{1,0:T(2,128)S(1)}, f32[2,1024,128]{2,1,0:T(8,128)S(1)}) %tuple.150, (s32[1024]{0:T(1024)S(1)}, s32[]{:T(128)}, ...), branch_computations={%region_9.9_spmd, %region_10.12_spmd} | conditional | flops 1102582784 | bytes 32636956 | solution.py:98
  414.0 11.9 %conditional.6 = (f32[1,2,1024]{2,1,0:T(2,128)}, f32[1,2,1024]{2,1,0:T(2,128)S(1)}, f32[1,2,1024,128]{3,2,1,0:T(8,128)S(1)}) conditional(s32[]{:T(128)} %convert_element_type.102, (f32[2,1024]{1,0:T(2,128)}, f32[2,1024]{1,0:T(2,128)S(1)}, f32[2,1024,128]{2,1,0:T(8,128)S(1)}) %tuple.150, (s32[1024]{0:T(1024)S(1)}, s32[]{:T(128)}, ...), branch_computations={%region_9.9_spmd, %region_10.12_spmd} | conditional | flops 1102582784 | bytes 32636956 | solution.py:98
  448.1 11.9 %conditional.6 = (f32[1,2,1024]{2,1,0:T(2,128)}, f32[1,2,1024]{2,1,0:T(2,128)S(1)}, f32[1,2,1024,128]{3,2,1,0:T(8,128)S(1)}) conditional(s32[]{:T(128)} %convert_element_type.102, (f32[2,1024]{1,0:T(2,128)}, f32[2,1024]{1,0:T(2,128)S(1)}, f32[2,1024,128]{2,1,0:T(8,128)S(1)}) %tuple.150, (s32[1024]{0:T(1024)S(1)}, s32[]{:T(128)}, ...), branch_computations={%region_9.9_spmd, %region_10.12_spmd} | conditional | flops 1102582784 | bytes 32636956 | solution.py:98
  482.2 11.9 %conditional.6 = (f32[1,2,1024]{2,1,0:T(2,128)}, f32[1,2,1024]{2,1,0:T(2,128)S(1)}, f32[1,2,1024,128]{3,2,1,0:T(8,128)S(1)}) conditional(s32[]{:T(128)} %convert_element_type.102, (f32[2,1024]{1,0:T(2,128)}, f32[2,1024]{1,0:T(2,128)S(1)}, f32[2,1024,128]{2,1,0:T(8,128)S(1)}) %tuple.150, (s32[1024]{0:T(1024)S(1)}, s32[]{:T(128)}, ...), branch_computations={%region_9.9_spmd, %region_10.12_spmd} | conditional | flops 1102582784 | bytes 32636956 | solution.py:98
  496.1 11.9 %conditional.7 = (f32[1,2,1024]{2,1,0:T(2,128)}, f32[1,2,1024]{2,1,0:T(2,128)S(1)}, f32[1,2,1024,128]{3,2,1,0:T(8,128)S(1)}) conditional(s32[]{:T(128)} %convert_element_type.103, (f32[2,1024]{1,0:T(2,128)}, f32[2,1024]{1,0:T(2,128)S(1)}, f32[2,1024,128]{2,1,0:T(8,128)S(1)}) %tuple.152, (s32[1024]{0:T(1024)S(1)}, s32[]{:T(128)}, ...), branch_computations={%region_5.5_spmd, %region_6.8_spmd} | conditional | flops 1102582784 | bytes 32636956 | solution.py:98
  516.3 11.9 %conditional.6 = (f32[1,2,1024]{2,1,0:T(2,128)}, f32[1,2,1024]{2,1,0:T(2,128)S(1)}, f32[1,2,1024,128]{3,2,1,0:T(8,128)S(1)}) conditional(s32[]{:T(128)} %convert_element_type.102, (f32[2,1024]{1,0:T(2,128)}, f32[2,1024]{1,0:T(2,128)S(1)}, f32[2,1024,128]{2,1,0:T(8,128)S(1)}) %tuple.150, (s32[1024]{0:T(1024)S(1)}, s32[]{:T(128)}, ...), branch_computations={%region_9.9_spmd, %region_10.12_spmd} | conditional | flops 1102582784 | bytes 32636956 | solution.py:98
  550.4 11.9 %conditional.6 = (f32[1,2,1024]{2,1,0:T(2,128)}, f32[1,2,1024]{2,1,0:T(2,128)S(1)}, f32[1,2,1024,128]{3,2,1,0:T(8,128)S(1)}) conditional(s32[]{:T(128)} %convert_element_type.102, (f32[2,1024]{1,0:T(2,128)}, f32[2,1024]{1,0:T(2,128)S(1)}, f32[2,1024,128]{2,1,0:T(8,128)S(1)}) %tuple.150, (s32[1024]{0:T(1024)S(1)}, s32[]{:T(128)}, ...), branch_computations={%region_9.9_spmd, %region_10.12_spmd} | conditional | flops 1102582784 | bytes 32636956 | solution.py:98
  594.8 11.9 %conditional.6 = (f32[1,2,1024]{2,1,0:T(2,128)}, f32[1,2,1024]{2,1,0:T(2,128)S(1)}, f32[1,2,1024,128]{3,2,1,0:T(8,128)S(1)}) conditional(s32[]{:T(128)} %convert_element_type.102, (f32[2,1024]{1,0:T(2,128)}, f32[2,1024]{1,0:T(2,128)S(1)}, f32[2,1024,128]{2,1,0:T(8,128)S(1)}) %tuple.150, (s32[1024]{0:T(1024)S(1)}, s32[]{:T(128)}, ...), branch_computations={%region_9.9_spmd, %region_10.12_spmd} | conditional | flops 1102582784 | bytes 32636956 | solution.py:98
  628.9 11.9 %conditional.6 = (f32[1,2,1024]{2,1,0:T(2,128)}, f32[1,2,1024]{2,1,0:T(2,128)S(1)}, f32[1,2,1024,128]{3,2,1,0:T(8,128)S(1)}) conditional(s32[]{:T(128)} %convert_element_type.102, (f32[2,1024]{1,0:T(2,128)}, f32[2,1024]{1,0:T(2,128)S(1)}, f32[2,1024,128]{2,1,0:T(8,128)S(1)}) %tuple.150, (s32[1024]{0:T(1024)S(1)}, s32[]{:T(128)}, ...), branch_computations={%region_9.9_spmd, %region_10.12_spmd} | conditional | flops 1102582784 | bytes 32636956 | solution.py:98
  660.7 24.7 %all_to_all.72 = bf16[16,128,256]{2,1,0:T(8,128)(2,1)S(1)} all-to-all(bf16[16,128,256]{2,1,0:T(8,128)(2,1)S(1)} %all_to_all.62), channel_id=1, replica_groups=mesh['blk'=8,'head'=16] {'head'}, dimensions={0} | all-to-all | bytes 2097152 | tf_op jit(solution)/shard_map/all_to_all | solution.py:167
  (464 shorter events, 624.3 us)
Async XLA Ops:
  6.5 23.1 %copy-start = (bf16[128,512]{1,0:T(8,128)(2,1)S(1)}, bf16[128,512]{1,0:T(8,128)(2,1)}, u32[]{:S(2)}) copy-start(bf16[128,512]{1,0:T(8,128)(2,1)} %param.13) | copy-start | bytes 393220
  6.5 85.9 %all-gather.3.cloned.1.call-start = ((), (), s32[]{:S(2)}) async-start(), calls=%async_computation.4 | async-start | bytes 4718592 | tf_op jit(solution)/shard_map/all_gather | solution.py:155
  8.8 48.5 %copy-start.1 = (s32[16]{0:T(128)S(1)}, s32[16]{0:T(128)}, u32[]{:S(2)}) copy-start(s32[16]{0:T(128)} %param.15) | copy-start | bytes 196
  29.6 115.9 %all-gather.5.cloned.1.call-start = ((), (), s32[]{:S(2)}) async-start(), calls=%async_computation.5 | async-start | bytes 4718592 | tf_op jit(solution)/shard_map/all_gather | solution.py:156
  53.5 33.2 %all-to-all-start.2 = ((bf16[128,16,256]{0,2,1:T(8,128)(2,1)}), bf16[128,16,256]{0,2,1:T(8,128)(2,1)S(1)}, u32[]{:S(2)}, u32[]{:S(2)}) async-start(bf16[128,16,256]{0,2,1:T(8,128)(2,1)} %bitcast.29), calls=%async_computation.2 | async-start | bytes 2097152 | tf_op jit(solution)/shard_map/all_to_all | solution.py:131
Sparse Core Ops, SparseCore 0:
  29.7 62.6 all-gather.2
  94.1 51.3 all-gather.4
where the time goes:
time: 702 us; the launch traced here: 694 us
  matrix products  203 us (29%)
  other arithmetic  195 us (28%)
  local copies, waits for them, and re-layouts  87.6 us (12%)
  waiting for transfers between devices  83.8 us (12%)
  blocking collectives  65.6 us (9%)
  loops' own time  40.6 us (6%)
  between operations  14.8 us (2%)
    dot_general x29, matrix products, update_part(): jnp.einsum('hqk,kd->hqd', weights.astype(jnp.bfloat16), value_tile, prefe...  120 us
    reduce_sum x29, other arithmetic, update_part(): new_totals = totals * factor + jnp.sum(weights, axis=-1)  84.7 us
    dot_general x29, matrix products, update_part(): jnp.einsum('hqd,kd->hqk', query_tile, key_tile, preferred_element_type=jn...  83.4 us
    another operation x77, other arithmetic, advance(): return (jnp.stack(new_peaks), jnp.stack(new_totals), jnp.stack(new_sums))  56.6 us
    all_gather x1, waiting for transfers between devices, per_device(): lax.all_gather(value_local, 'blk', axis=0, tiled=True)  53.1 us
    another operation x1, loops' own time, attend_piece(): return lax.fori_loop(0, piece_rows // step_rows, advance, state)  40 us
    squeeze x32, local copies, waits for them, and re-layouts, advance(): state_part = (peaks[part_index], totals[part_index], sums[part_index])  36.5 us
    all_to_all x1, waiting for transfers between devices, per_device(): lax.all_to_all(rot_queries, 'head', split_axis=1, concat_axis=0, tiled=True)  26.8 us
  transfers between devices with their start and end apart: 3, of which 3 were waited for; matrix products, arithmetic and copies ran while one was open for 1% of the time, Pallas kernels for 0%

commit v1 on v0

v1 whole, which is shorter than its diff:
```python
import functools
import math

import jax
import jax.numpy as jnp
from jax import lax
from jax.experimental import pallas as pl
from jax.experimental.pallas import tpu as pltpu
from jax.sharding import PartitionSpec as P

HD = 128
ROPE_BASE = 1000000.0
bf16 = jnp.bfloat16
f32 = jnp.float32
AXES = ("blk", "head")
NT = (((1,), (1,)), ((), ()))
NEG = -1e30
TILES = 4


def device_id(x, y, z, core):
    return ((x % 2) * 4 + y) * 16 + z * 4 + (x // 2) * 2 + core


COORDS = [(x, y, z, c) for x in range(4) for y in range(4) for z in range(4) for c in range(2)]
SPREAD_GROUPS = [
    [device_id(xh * 2 + b // 4, b % 4, z, c) for b in range(8) for z in range(4)]
    for xh in range(2)
    for c in range(2)
]


def ring_perm(first_axis_core, shift):
    pairs = []
    for x, y, z, c in COORDS:
        if c == first_axis_core:
            target = device_id(x, (y + shift) % 4, z, c)
        else:
            target = device_id((x + shift) % 4, y, z, c)
        pairs.append((device_id(x, y, z, c), target))
    return pairs


SWAP = [(device_id(x, y, z, c), device_id(x, y, z, 1 - c)) for x, y, z, c in COORDS]


def rope_tables(positions):
    pair = jnp.arange(HD // 2, dtype=jnp.int32)
    inverse = jnp.exp(pair.astype(f32) * (-2.0 * math.log(ROPE_BASE) / HD))
    picked = jnp.where(
        pair[None, :] < 16,
        positions[0][:, None],
        jnp.where(pair[None, :] < 40, positions[1][:, None], positions[2][:, None]),
    )
    angles = picked.astype(f32) * inverse[None, :]
    cos, sin = jnp.cos(angles), jnp.sin(angles)
    return jnp.concatenate([cos, cos], axis=1), jnp.concatenate([-sin, sin], axis=1)


def pack_kernel(q_ref, k_ref, v_ref, cos_ref, sin_ref, qo_ref, kvo_ref):
    cos, sin = cos_ref[...], sin_ref[...]
    fold = math.log2(math.e) / math.sqrt(HD)
    qcos, qsin = cos * fold, sin * fold

    def rotate(x, c, s):
        x = x.astype(f32)
        return (x * c + pltpu.roll(x, HD // 2, 1) * s).astype(bf16).reshape(8, 16, HD)

    for z in range(4):
        for h in range(8):
            col = (z * 8 + h) * HD
            qo_ref[:, z, :, h * HD : (h + 1) * HD] = rotate(q_ref[:, col : col + HD], qcos, qsin)
        kvo_ref[:, z, :, :HD] = rotate(k_ref[:, z * HD : (z + 1) * HD], cos, sin)
        kvo_ref[:, z, :, HD:] = v_ref[:, z * HD : (z + 1) * HD].reshape(8, 16, HD)


def pack(q, k, v, cos, sin):
    vmem = pl.BlockSpec(memory_space=pltpu.VMEM)
    return pl.pallas_call(
        pack_kernel,
        out_shape=(
            jax.ShapeDtypeStruct((8, 4, 16, 8 * HD), bf16),
            jax.ShapeDtypeStruct((8, 4, 16, 2 * HD), bf16),
        ),
        in_specs=[vmem] * 5,
        out_specs=(vmem, vmem),
        compiler_params=pltpu.CompilerParams(vmem_limit_bytes=24 * 2**20),
        name="pack",
    )(q, k, v, cos, sin)


def attend_kernel(inv, *refs, n_kv, first, last):
    refs = list(refs)
    q_ref = refs.pop(0)
    kv_refs = [refs.pop(0) for _ in range(n_kv)]
    kpos_ref, qpos_ref = refs.pop(0), refs.pop(0)
    if not first:
        acc_in, ml_in = refs.pop(0), refs.pop(0)
    if last:
        o_ref = refs.pop(0)
    else:
        acc_out, ml_out = refs.pop(0), refs.pop(0)
    m_ref, a_ref = refs
    pieces = sum(r.shape[0] for r in kv_refs)
    keys = pieces * 32
    per_unit = max(1, 1024 // keys)
    units = 2 if per_unit <= 2 else 1
    per_body = per_unit * units
    step = pl.program_id(0)
    base = step * TILES

    def query_tile(block):
        x = q_ref[block]
        return jnp.concatenate([x[:, h * HD : (h + 1) * HD] for h in range(8)], axis=0)

    def key_tile(orders):
        ks, vs = [], []
        for order in orders:
            block = inv[order]
            for r in kv_refs:
                kv = r[:, block].reshape(r.shape[0] * 32, 2 * HD)
                ks.append(kv[:, :HD])
                vs.append(kv[:, HD:])
        k = jnp.concatenate(ks, axis=0) if len(ks) > 1 else ks[0]
        v = jnp.concatenate(vs, axis=0) if len(vs) > 1 else vs[0]
        return k, jnp.concatenate([v, jnp.ones_like(v)], axis=1)

    rows = [pl.ds(w * 256, 256) for w in range(TILES)]
    for w in range(TILES):
        if first:
            m_ref[rows[w], :] = jnp.full((256, HD), NEG, f32)
            a_ref[rows[w], :] = jnp.zeros((256, 2 * HD), f32)
        else:
            ml = ml_in[w]
            m_ref[rows[w], :] = jnp.broadcast_to(ml[:, :1], (256, HD))
            a_ref[rows[w], :HD] = acc_in[w]
            a_ref[rows[w], HD:] = jnp.broadcast_to(ml[:, HD - 1 :], (256, HD))
    queries = [query_tile(inv[base + w]) for w in range(TILES)]

    def scores(w, tile, masked):
        s = lax.dot_general(queries[w], tile[0], NT, preferred_element_type=f32)
        if masked:
            allowed = jnp.tile(kpos_ref[...], (256, 1)) <= jnp.tile(qpos_ref[...], (1, keys // HD))
            own = jnp.where(allowed, s[:, s.shape[1] - keys :], NEG)
            s = jnp.concatenate([s[:, : s.shape[1] - keys], own], axis=1) if s.shape[1] > keys else own
        return s

    def weigh(w, s):
        before = m_ref[rows[w], :]
        peak = jnp.maximum(before, jnp.max(s, axis=1, keepdims=True))
        p = jnp.exp2(s - jnp.tile(peak, (1, s.shape[1] // HD))).astype(bf16)
        m_ref[rows[w], :] = peak
        return p, jnp.exp2(before - peak)

    def add(w, p, factor, vext):
        o = jnp.dot(p, vext, preferred_element_type=f32)
        a_ref[rows[w], :] = a_ref[rows[w], :] * jnp.tile(factor, (1, 2)) + o

    def run(todo):
        ahead = scores(*todo[0])
        pending = None
        for i, (w, tile, _) in enumerate(todo):
            s = ahead
            if i + 1 < len(todo):
                ahead = scores(*todo[i + 1])
            p, factor = weigh(w, s)
            if pending is not None:
                add(*pending)
            pending = (w, p, factor, tile[1])
        add(*pending)

    def body(j, carry):
        tiles = [
            key_tile([j * per_body + u * per_unit + i for i in range(per_unit)])
            for u in range(units)
        ]
        run([(w, t, False) for t in tiles for w in range(TILES)])
        return carry

    lax.fori_loop(0, base // per_body, body, 0)

    todo = []
    for w in range(TILES):
        for start in range(0, w + 1, per_unit):
            stop = min(start + per_unit, w + 1)
            todo.append((w, key_tile([base + i for i in range(start, stop)]), stop == w + 1))
    run(todo)

    for w in range(TILES):
        a = a_ref[rows[w], :]
        if last:
            o = (a[:, :HD] / a[:, HD:]).astype(bf16)
            block = inv[base + w]
            for h in range(8):
                o_ref[block, :, h * HD : (h + 1) * HD] = o[h * 32 : (h + 1) * 32]
        else:
            acc_out[w] = a[:, :HD]
            lane = lax.broadcasted_iota(jnp.int32, (256, HD), 1)
            ml_out[w] = jnp.where(lane < HD // 2, m_ref[rows[w], :], a[:, HD:])


def attend(inv, q, kvs, kpos, qpos, state, last, name):
    first = state is None

    def whole(x):
        return pl.BlockSpec(x.shape, lambda i, inv: (0,) * x.ndim, pipeline_mode=pl.Buffered(1))

    part = pl.BlockSpec((TILES, 256, HD), lambda i, inv: (i, 0, 0))
    operands = [q, *kvs, kpos, qpos]
    in_specs = [whole(x) for x in operands]
    if not first:
        operands += list(state)
        in_specs += [part, part]
    full = jax.ShapeDtypeStruct((16, 256, HD), f32)
    pieces = sum(x.shape[0] for x in kvs)
    work = 17 * 16 // 2 * 256 * 32 * pieces
    return pl.pallas_call(
        functools.partial(attend_kernel, n_kv=len(kvs), first=first, last=last),
        out_shape=jax.ShapeDtypeStruct(q.shape, bf16) if last else (full, full),
        grid_spec=pltpu.PrefetchScalarGridSpec(
            num_scalar_prefetch=1,
            grid=(16 // TILES,),
            in_specs=in_specs,
            out_specs=whole(q) if last else (part, part),
            scratch_shapes=[
                pltpu.VMEM((TILES * 256, HD), f32),
                pltpu.VMEM((TILES * 256, 2 * HD), f32),
            ],
        ),
        compiler_params=pltpu.CompilerParams(vmem_limit_bytes=48 * 2**20),
        cost_estimate=pl.CostEstimate(
            flops=work * 1024, bytes_accessed=8 * 2**20, transcendentals=work
        ),
        name=name,
    )(inv, *operands)


def per_device(queries, keys, values, positions, block_order):
    blk, head = lax.axis_index("blk"), lax.axis_index("head")
    core = head % 2
    x = (head // 2) % 2 * 2 + blk // 4
    y = blk % 4

    def offsets(px, py, pc):
        start = ((px // 2) * 2 + pc) * 128 + ((px % 2) * 4 + py) * 16
        return jnp.concatenate([start + jnp.arange(16), start + 512 + jnp.arange(16)]).astype(jnp.int32)

    cos, sin = rope_tables(positions)
    q_send, kv_send = pack(queries, keys, values, cos, sin)
    inv = jnp.sum(
        jnp.where(
            block_order[None, :] == jnp.arange(16, dtype=jnp.int32)[:, None],
            jnp.arange(16, dtype=jnp.int32)[None, :],
            0,
        ),
        axis=1,
    ).astype(jnp.int32)

    def spread(t):
        return lax.all_to_all(t, AXES, 0, 0, axis_index_groups=SPREAD_GROUPS)

    own = spread(kv_send.reshape(32, 16, 2 * HD)).reshape(16, 32, 2 * HD)
    q = spread(q_send.reshape(32, 16, 8 * HD)).reshape(16, 32, 8 * HD)
    qpos = jnp.broadcast_to(jnp.tile(offsets(x, y, core), 8)[:, None], (256, HD))

    send = lambda t, perm: lax.ppermute(t, AXES, perm)
    plus1, minus1 = ring_perm(0, 1), ring_perm(0, -1)
    plus2, minus2 = ring_perm(1, 1), ring_perm(1, -1)

    from_minus = send(own, plus1)
    from_plus = send(own, minus1)
    far = jnp.concatenate(
        [send(from_minus[:, :16], plus1), send(from_plus[:, 16:], minus1)], axis=1
    )
    line = jnp.stack([own, from_minus, from_plus, far])
    line_other = send(line, SWAP)
    shifts = [0, -1, 1, 2]

    def line_offsets(dx, dy, c):
        return jnp.concatenate(
            [
                offsets(
                    (x + dx + jnp.where(c == 0, 0, s)) % 4,
                    (y + dy + jnp.where(c == 0, s, 0)) % 4,
                    c,
                )
                for s in shifts
            ]
        )

    def moved_offsets(shift, c):
        return line_offsets(jnp.where(c == 0, shift, 0), jnp.where(c == 0, 0, shift), c)

    line_minus = send(line, plus2)
    line_plus = send(line, minus2)
    far_a = send(line_minus[:2], plus2)
    far_b = send(line_plus[2:], minus2)
    minus_other, plus_other = send(line_minus, SWAP), send(line_plus, SWAP)
    far_a_other, far_b_other = send(far_a, SWAP), send(far_b, SWAP)

    other = 1 - core
    kpos1 = jnp.concatenate([moved_offsets(0, core), moved_offsets(0, other)])[None]
    kpos2 = jnp.concatenate([moved_offsets(-1, core), moved_offsets(1, core)])[None]
    far_own, far_other = moved_offsets(2, core), moved_offsets(2, other)
    kpos3 = jnp.concatenate(
        [moved_offsets(-1, other), moved_offsets(1, other), far_own, far_other]
    )[None]

    state = attend(inv, q, [line, line_other], kpos1, qpos, None, False, "attend_near")
    state = attend(inv, q, [line_minus, line_plus], kpos2, qpos, state, False, "attend_next")
    mixed = attend(
        inv,
        q,
        [minus_other, plus_other, far_a, far_b, far_a_other, far_b_other],
        kpos3,
        qpos,
        state,
        True,
        "attend_far",
    )
    back = spread(mixed.reshape(32, 16, 8 * HD)).reshape(8, 4, 16, 8 * HD)
    return jnp.transpose(back, (0, 2, 1, 3)).reshape(128, 32 * HD)


def solution(mesh):
    return jax.shard_map(
        per_device,
        mesh=mesh,
        in_specs=(P(AXES, None), P(AXES, None), P(AXES, None), P(None, AXES), P()),
        out_specs=P(AXES, None),
        check_vma=False,
    )
```

time: 702 us -> 167 us (0.24)
  matrix products: 203 us -> 0 us
  other arithmetic: 195 us -> 0.97 us
  local copies, waits for them, and re-layouts: 87.6 us -> 11.8 us
  Pallas kernels: 0 us -> 64.4 us
  waiting for transfers between devices: 83.8 us -> 35.3 us
  blocking collectives: 65.6 us -> 23 us
  loops' own time: 40.6 us -> 0 us
  starting transfers between devices: 3.88 us -> 27.1 us
  between operations: 14.8 us -> 2.57 us
    dot_general x58 -> x0, matrix products: 203 us -> none  [the longest x29 120 us: update_part(): jnp.einsum('hqk,kd->hqd', weights.astype(jnp.bfloat16), value_tile, prefe...]
    reduce_sum x45 -> x1, other arithmetic: 86.1 us -> 0.11 us  [per_device(): jnp.sum(jnp.where(block_order[None, :] == jnp.arange(16, dtype=jnp.int32)...]
    pallas_call x0 -> x4, Pallas kernels: none -> 64.4 us  [the longest x3 62.6 us: attend(): pl.pallas_call(functools.partial(attend_kernel, n_kv=len(kvs), first=firs...]
    another operation x79 -> x2, other arithmetic: 57.2 us -> 0.15 us  [per_device(): line = jnp.stack([own, from_minus, from_plus, far])]
    all_gather x2 -> x0, waiting for transfers between devices: 56.9 us -> none  [the longest x1 53.1 us: per_device(): lax.all_gather(value_local, 'blk', axis=0, tiled=True)]
    all_to_all x3 -> x1, blocking collectives: 65.6 us -> 23 us  [spread(): return lax.all_to_all(t, AXES, 0, 0, axis_index_groups=SPREAD_GROUPS)]
    another operation x33 -> x0, loops' own time: 40.6 us -> none  [the longest x1 40 us: attend_piece(): return lax.fori_loop(0, piece_rows // step_rows, advance, state)]
    squeeze x32 -> x0, local copies, waits for them, and re-layouts: 36.5 us -> none  [advance(): state_part = (peaks[part_index], totals[part_index], sums[part_index])]
  transfers between devices with their start and end apart: 3 -> 15, of which waited for: 3 -> 5; matrix products, arithmetic and copies ran while one was open for 1% -> 2% of each run, Pallas kernels for 0% -> 21%
where the time goes in v1:
time: 167 us; the launch traced here: 165 us
  Pallas kernels  64.4 us (39%)
  waiting for transfers between devices  35.3 us (21%)
  starting transfers between devices  27.1 us (16%)
  blocking collectives  23 us (14%)
  local copies, waits for them, and re-layouts  11.8 us (7%)
  between operations  2.57 us (2%)
    pallas_call x3, Pallas kernels, attend(): pl.pallas_call(functools.partial(attend_kernel, n_kv=len(kvs), first=firs...  62.6 us
    ppermute x13, waiting for transfers between devices, per_device(): send = lambda t, perm: lax.ppermute(t, AXES, perm)  30 us
    all_to_all x1, blocking collectives, spread(): return lax.all_to_all(t, AXES, 0, 0, axis_index_groups=SPREAD_GROUPS)  23 us
    all_to_all x2, starting transfers between devices, spread(): return lax.all_to_all(t, AXES, 0, 0, axis_index_groups=SPREAD_GROUPS)  14.8 us
    ppermute x13, starting transfers between devices, per_device(): send = lambda t, perm: lax.ppermute(t, AXES, perm)  12.3 us
    unnamed x13, local copies, waits for them, and re-layouts  7.07 us
    all_to_all x2, waiting for transfers between devices, spread(): return lax.all_to_all(t, AXES, 0, 0, axis_index_groups=SPREAD_GROUPS)  5.37 us
  transfers between devices with their start and end apart: 15, of which 5 were waited for; matrix products, arithmetic and copies ran while one was open for 2% of the time, Pallas kernels for 21%

profile of v1, /device:TPU:24, one launch (start us, length us, event | category | flops | bytes accessed | tf_op | source)
XLA Modules:
  0.0 165.2 jit_solution(1276568855546137979)
XLA Ops:
  1.3 1.2 copy-done
  2.5 0.9 copy-done.1
  3.4 0.9 copy-done.2
  4.3 1.8 %pack.1 = (bf16[8,4,16,1024]{3,2,1,0:T(8,128)(2,1)}, bf16[8,4,16,256]{3,2,1,0:T(8,128)(2,1)}) custom-call(bf16[128,4096]{1,0:T(8,128)(2,1)S(1)} %copy-done, bf16[128,512]{1,0:T(8,128)(2,1)S(1)} %copy-done.1, bf16[128,512]{1,0:T(8,128)(2,1)S(1)} %copy-done.2, f32[128,128]{1,0:T(8,128)S(1)} %get-tuple-element.23.cos_ref, f32[128,128]{1,0:T(8,128)S(1)} %get-tuple-element.24.sin_ref), custom_call_target="tpu_custom_call" | custom-call | tf_op jit(solution)/shard_map/pack/pallas_call | solution.py:79
  6.1 9.3 %all-to-all-start.1 = ((bf16[32,16,256]{2,1,0:T(8,128)(2,1)}), bf16[32,16,256]{2,1,0:T(8,128)(2,1)S(1)}, u32[]{:S(2)}, u32[]{:S(2)}) async-start(bf16[32,16,256]{2,1,0:T(8,128)(2,1)} %bitcast.5), calls=%async_computation.1 | async-start | bytes 524288 | tf_op jit(solution)/shard_map/all_to_all | solution.py:260
  17.4 5.4 %all-to-all-done.1 = bf16[32,16,256]{2,1,0:T(8,128)(2,1)S(1)} async-done(((bf16[32,16,256]{2,1,0:T(8,128)(2,1)}), bf16[32,16,256]{2,1,0:T(8,128)(2,1)S(1)}, u32[]{:S(2)}, u32[]{:S(2)}) %all-to-all-start.1) | async-done | bytes 262176 | tf_op jit(solution)/shard_map/all_to_all | solution.py:260
  22.8 5.6 %all-to-all-start = ((bf16[32,16,1024]{2,1,0:T(8,128)(2,1)}), bf16[32,16,1024]{2,1,0:T(8,128)(2,1)S(1)}, u32[]{:S(2)}, u32[]{:S(2)}) async-start(bf16[32,16,1024]{2,1,0:T(8,128)(2,1)} %bitcast.3), calls=%async_computation | async-start | bytes 2097152 | tf_op jit(solution)/shard_map/all_to_all | solution.py:260
  28.7 1.8 %collective-permute-start.1 = (bf16[16,32,256]{2,1,0:T(8,128)(2,1)S(1)}, bf16[16,32,256]{2,1,0:T(8,128)(2,1)S(1)}, u32[]{:S(2)}, u32[]{:S(2)}) collective-permute-start(bf16[16,32,256]{2,1,0:T(8,128)(2,1)S(1)} %bitcast.34), channel_id=1, source_target_pairs={{0,48},{1,67},{4,52},{5,71},{8,56},{9,75},{12,60},{13,79},{16,0},{... | collective-permute-start | bytes 786440 | tf_op jit(solution)/shard_map/ppermute | solution.py:266
  30.5 12.0 %collective-permute-done = bf16[16,32,256]{2,1,0:T(8,128)(2,1)S(1)} collective-permute-done((bf16[16,32,256]{2,1,0:T(8,128)(2,1)S(1)}, bf16[16,32,256]{2,1,0:T(8,128)(2,1)S(1)}, u32[]{:S(2)}, u32[]{:S(2)}) %collective-permute-start) | collective-permute-done | bytes 262176 | tf_op jit(solution)/shard_map/ppermute | solution.py:266
  42.6 2.5 %collective-permute-start.2 = (bf16[16,16,256]{2,1,0:T(8,128)(2,1)S(1)}, bf16[16,16,256]{2,1,0:T(8,128)(2,1)S(1)}, u32[]{:S(2)}, u32[]{:S(2)}) collective-permute-start(bf16[16,16,256]{2,1,0:T(8,128)(2,1)S(1)} %slice.28), channel_id=1, source_target_pairs={{0,16},{1,65},{4,20},{5,69},{8,24},{9,73},{12,28},{13,77},{16,32},... | collective-permute-start | bytes 393224 | tf_op jit(solution)/shard_map/ppermute | solution.py:266
  45.2 2.4 %collective-permute-done.2 = bf16[16,16,256]{2,1,0:T(8,128)(2,1)S(1)} collective-permute-done((bf16[16,16,256]{2,1,0:T(8,128)(2,1)S(1)}, bf16[16,16,256]{2,1,0:T(8,128)(2,1)S(1)}, u32[]{:S(2)}, u32[]{:S(2)}) %collective-permute-start.2) | collective-permute-done | bytes 131104 | tf_op jit(solution)/shard_map/ppermute | solution.py:266
  47.6 3.7 %collective-permute-done.3 = bf16[16,16,256]{2,1,0:T(8,128)(2,1)S(1)} collective-permute-done((bf16[16,16,256]{2,1,0:T(8,128)(2,1)S(1)}, bf16[16,16,256]{2,1,0:T(8,128)(2,1)S(1)}, u32[]{:S(2)}, u32[]{:S(2)}) %collective-permute-start.3) | collective-permute-done | bytes 131104 | tf_op jit(solution)/shard_map/ppermute | solution.py:266
  51.5 1.6 collective-permute-start.4
  53.1 1.7 %collective-permute-start.6 = (bf16[4,16,32,256]{3,2,1,0:T(8,128)(2,1)S(1)}, bf16[4,16,32,256]{3,2,1,0:T(8,128)(2,1)}, u32[]{:S(2)}, u32[]{:S(2)}) collective-permute-start(bf16[4,16,32,256]{3,2,1,0:T(8,128)(2,1)S(1)} %pad_maximum_fusion.refs_1_), channel_id=1, source_target_pairs={{0,66},{1,49},{4,70},{5,53},{8,74},{9,57},{12,78},{13,61},{16,82},... | collective-permute-start | bytes 3145736 | tf_op jit(solution)/shard_map/ppermute | solution.py:266
  55.8 11.8 %collective-permute-done.4.refs_1_ = bf16[4,16,32,256]{3,2,1,0:T(8,128)(2,1)S(1)} collective-permute-done((bf16[4,16,32,256]{3,2,1,0:T(8,128)(2,1)S(1)}, bf16[4,16,32,256]{3,2,1,0:T(8,128)(2,1)S(1)}, u32[]{:S(2)}, u32[]{:S(2)}) %collective-permute-start.4) | collective-permute-done | bytes 1048608 | tf_op jit(solution)/shard_map/ppermute | solution.py:266
  68.8 1.9 %slice.31 = bf16[2,16,32,256]{3,2,1,0:T(8,128)(2,1)} slice(bf16[4,16,32,256]{3,2,1,0:T(8,128)(2,1)} %collective-permute-done.6.refs_2_), slice={[2:4], [0:16], [0:32], [0:256]} | slice | bytes 1048576 | tf_op jit(solution)/shard_map/slice | solution.py:297
  70.6 2.9 %collective-permute-start.9 = (bf16[2,16,32,256]{3,2,1,0:T(8,128)(2,1)}, bf16[2,16,32,256]{3,2,1,0:T(8,128)(2,1)}, u32[]{:S(2)}, u32[]{:S(2)}) collective-permute-start(bf16[2,16,32,256]{3,2,1,0:T(8,128)(2,1)} %slice.31), channel_id=1, source_target_pairs={{0,66},{1,49},{4,70},{5,53},{8,74},{9,57},{12,78},{13,61},{16,82},... | collective-permute-start | bytes 1572872 | tf_op jit(solution)/shard_map/ppermute | solution.py:266
  74.2 16.6 %attend_near.1 = (f32[16,256,128]{2,1,0:T(8,128)S(1)}, f32[16,256,128]{2,1,0:T(8,128)}) custom-call(s32[16]{0:T(128)S(1)} %select_reduce_fusion.inv, bf16[16,32,1024]{2,1,0:T(8,128)(2,1)S(1)} %bitcast.24, bf16[4,16,32,256]{3,2,1,0:T(8,128)(2,1)S(1)} %pad_maximum_fusion.refs_1_, bf16[4,16,32,256]{3,2,1,0:T(8,128)(2,1)} %collective-permute-done.12.refs_2_, ...), custom_call_target="tpu_custom_call" | custom-call | flops 9126805504 | bytes 8388608 | tf_op jit(solution)/shard_map/attend_near/pallas_call | solution.py:217
  90.8 1.3 copy-done.4
  92.6 18.0 %attend_next.1 = (f32[16,256,128]{2,1,0:T(8,128)S(1)}, f32[16,256,128]{2,1,0:T(8,128)}) custom-call(s32[16]{0:T(128)S(1)} %select_reduce_fusion.inv, bf16[16,32,1024]{2,1,0:T(8,128)(2,1)S(1)} %bitcast.25, bf16[4,16,32,256]{3,2,1,0:T(8,128)(2,1)S(1)} %collective-permute-done.4.refs_1_, bf16[4,16,32,256]{3,2,1,0:T(8,128)(2,1)} %collective-permute-done.6.refs_2_, ...), custom_call_target="tpu_custom_call" | custom-call | flops 9126805504 | bytes 8388608 | tf_op jit(solution)/shard_map/attend_next/pallas_call | solution.py:217
  110.7 1.4 copy-done.3
  112.0 28.0 %attend_far.1 = bf16[16,32,1024]{2,1,0:T(8,128)(2,1)S(1)} custom-call(s32[16]{0:T(128)S(1)} %select_reduce_fusion.inv, bf16[16,32,1024]{2,1,0:T(8,128)(2,1)S(1)} %bitcast.26, bf16[4,16,32,256]{3,2,1,0:T(8,128)(2,1)} %collective-permute-done.5.refs_1_, bf16[4,16,32,256]{3,2,1,0:T(8,128)(2,1)} %collective-permute-done.7.refs_2_, ...), custom_call_target="tpu_custom_call" | custom-call | flops 18253611008 | bytes 8388608 | tf_op jit(solution)/shard_map/attend_far/pallas_call | solution.py:217
  140.1 23.0 %all_to_all.15 = bf16[32,16,1024]{2,1,0:T(8,128)(2,1)S(1)} all-to-all(bf16[32,16,1024]{2,1,0:T(8,128)(2,1)S(1)} %bitcast.27), channel_id=1, replica_groups={{0,4,8,12,16,20,24,28,32,36,40,44,48,52,56,60,64,68,72,76,80,84,88,92,9..., dimensions={0} | all-to-all | bytes 2097152 | tf_op jit(solution)/shard_map/all_to_all | solution.py:260
  163.9 1.3 copy.8
  (78 shorter events, 5.7 us)
Async XLA Ops:
  1.3 1.2 copy-start
  2.5 0.9 copy-start.1
  3.4 0.9 copy-start.2
  6.1 16.7 %all-to-all-start.1 = ((bf16[32,16,256]{2,1,0:T(8,128)(2,1)}), bf16[32,16,256]{2,1,0:T(8,128)(2,1)S(1)}, u32[]{:S(2)}, u32[]{:S(2)}) async-start(bf16[32,16,256]{2,1,0:T(8,128)(2,1)} %bitcast.5), calls=%async_computation.1 | async-start | bytes 524288 | tf_op jit(solution)/shard_map/all_to_all | solution.py:260
  22.8 51.3 %all-to-all-start = ((bf16[32,16,1024]{2,1,0:T(8,128)(2,1)}), bf16[32,16,1024]{2,1,0:T(8,128)(2,1)S(1)}, u32[]{:S(2)}, u32[]{:S(2)}) async-start(bf16[32,16,1024]{2,1,0:T(8,128)(2,1)} %bitcast.3), calls=%async_computation | async-start | bytes 2097152 | tf_op jit(solution)/shard_map/all_to_all | solution.py:260
  28.4 14.2 %collective-permute-start = (bf16[16,32,256]{2,1,0:T(8,128)(2,1)S(1)}, bf16[16,32,256]{2,1,0:T(8,128)(2,1)S(1)}, u32[]{:S(2)}, u32[]{:S(2)}) collective-permute-start(bf16[16,32,256]{2,1,0:T(8,128)(2,1)S(1)} %bitcast.33), channel_id=1, source_target_pairs={{0,16},{1,65},{4,20},{5,69},{8,24},{9,73},{12,28},{13,77},{16,32},... | collective-permute-start | bytes 786440 | tf_op jit(solution)/shard_map/ppermute | solution.py:266
  28.7 16.3 %collective-permute-start.1 = (bf16[16,32,256]{2,1,0:T(8,128)(2,1)S(1)}, bf16[16,32,256]{2,1,0:T(8,128)(2,1)S(1)}, u32[]{:S(2)}, u32[]{:S(2)}) collective-permute-start(bf16[16,32,256]{2,1,0:T(8,128)(2,1)S(1)} %bitcast.34), channel_id=1, source_target_pairs={{0,48},{1,67},{4,52},{5,71},{8,56},{9,75},{12,60},{13,79},{16,0},{... | collective-permute-start | bytes 786440 | tf_op jit(solution)/shard_map/ppermute | solution.py:266
  30.5 25.2 %copy-start.5 = (s32[16]{0:T(128)S(1)}, s32[16]{0:T(128)}, u32[]{:S(2)}) copy-start(s32[16]{0:T(128)} %param.9) | copy-start | bytes 196
  42.6 5.0 %collective-permute-start.2 = (bf16[16,16,256]{2,1,0:T(8,128)(2,1)S(1)}, bf16[16,16,256]{2,1,0:T(8,128)(2,1)S(1)}, u32[]{:S(2)}, u32[]{:S(2)}) collective-permute-start(bf16[16,16,256]{2,1,0:T(8,128)(2,1)S(1)} %slice.28), channel_id=1, source_target_pairs={{0,16},{1,65},{4,20},{5,69},{8,24},{9,73},{12,28},{13,77},{16,32},... | collective-permute-start | bytes 393224 | tf_op jit(solution)/shard_map/ppermute | solution.py:266
  45.0 6.2 %collective-permute-start.3 = (bf16[16,16,256]{2,1,0:T(8,128)(2,1)S(1)}, bf16[16,16,256]{2,1,0:T(8,128)(2,1)S(1)}, u32[]{:S(2)}, u32[]{:S(2)}) collective-permute-start(bf16[16,16,256]{2,1,0:T(8,128)(2,1)S(1)} %slice.29), channel_id=1, source_target_pairs={{0,48},{1,67},{4,52},{5,71},{8,56},{9,75},{12,60},{13,79},{16,0},{... | collective-permute-start | bytes 393224 | tf_op jit(solution)/shard_map/ppermute | solution.py:266
  51.4 22.6 %collective-permute-start.12 = (bf16[4,16,32,256]{3,2,1,0:T(8,128)(2,1)S(1)}, bf16[4,16,32,256]{3,2,1,0:T(8,128)(2,1)}, u32[]{:S(2)}, u32[]{:S(2)}) collective-permute-start(bf16[4,16,32,256]{3,2,1,0:T(8,128)(2,1)S(1)} %pad_maximum_fusion.refs_1_), channel_id=1, source_target_pairs={{0,1},{1,0},{4,5},{5,4},{8,9},{9,8},{12,13},{13,12},{16,17},{17,16... | collective-permute-start | bytes 3145736 | tf_op jit(solution)/shard_map/ppermute | solution.py:266
  51.5 16.1 %collective-permute-start.4 = (bf16[4,16,32,256]{3,2,1,0:T(8,128)(2,1)S(1)}, bf16[4,16,32,256]{3,2,1,0:T(8,128)(2,1)S(1)}, u32[]{:S(2)}, u32[]{:S(2)}) collective-permute-start(bf16[4,16,32,256]{3,2,1,0:T(8,128)(2,1)S(1)} %pad_maximum_fusion.refs_1_), channel_id=1, source_target_pairs={{0,64},{1,17},{4,68},{5,21},{8,72},{9,25},{12,76},{13,29},{16,80},... | collective-permute-start | bytes 3145736 | tf_op jit(solution)/shard_map/ppermute | solution.py:266
  53.1 15.6 %collective-permute-start.6 = (bf16[4,16,32,256]{3,2,1,0:T(8,128)(2,1)S(1)}, bf16[4,16,32,256]{3,2,1,0:T(8,128)(2,1)}, u32[]{:S(2)}, u32[]{:S(2)}) collective-permute-start(bf16[4,16,32,256]{3,2,1,0:T(8,128)(2,1)S(1)} %pad_maximum_fusion.refs_1_), channel_id=1, source_target_pairs={{0,66},{1,49},{4,70},{5,53},{8,74},{9,57},{12,78},{13,61},{16,82},... | collective-permute-start | bytes 3145736 | tf_op jit(solution)/shard_map/ppermute | solution.py:266
  68.4 23.7 %collective-permute-start.8 = (bf16[2,16,32,256]{3,2,1,0:T(8,128)(2,1)}, bf16[2,16,32,256]{3,2,1,0:T(8,128)(2,1)}, u32[]{:S(2)}, u32[]{:S(2)}) collective-permute-start(bf16[2,16,32,256]{3,2,1,0:T(8,128)(2,1)} %slice.30), channel_id=1, source_target_pairs={{0,64},{1,17},{4,68},{5,21},{8,72},{9,25},{12,76},{13,29},{16,80},... | collective-permute-start | bytes 1572872 | tf_op jit(solution)/shard_map/ppermute | solution.py:266
  70.6 21.5 %collective-permute-start.9 = (bf16[2,16,32,256]{3,2,1,0:T(8,128)(2,1)}, bf16[2,16,32,256]{3,2,1,0:T(8,128)(2,1)}, u32[]{:S(2)}, u32[]{:S(2)}) collective-permute-start(bf16[2,16,32,256]{3,2,1,0:T(8,128)(2,1)} %slice.31), channel_id=1, source_target_pairs={{0,66},{1,49},{4,70},{5,53},{8,74},{9,57},{12,78},{13,61},{16,82},... | collective-permute-start | bytes 1572872 | tf_op jit(solution)/shard_map/ppermute | solution.py:266
  73.6 38.5 %collective-permute-start.5 = (bf16[4,16,32,256]{3,2,1,0:T(8,128)(2,1)S(1)}, bf16[4,16,32,256]{3,2,1,0:T(8,128)(2,1)}, u32[]{:S(2)}, u32[]{:S(2)}) collective-permute-start(bf16[4,16,32,256]{3,2,1,0:T(8,128)(2,1)S(1)} %collective-permute-done.4.refs_1_), channel_id=1, source_target_pairs={{0,1},{1,0},{4,5},{5,4},{8,9},{9,8},{12,13},{13,12},{16,17},{17,16... | collective-permute-start | bytes 3145736 | tf_op jit(solution)/shard_map/ppermute | solution.py:266
  73.6 38.5 %collective-permute-start.7 = (bf16[4,16,32,256]{3,2,1,0:T(8,128)(2,1)}, bf16[4,16,32,256]{3,2,1,0:T(8,128)(2,1)}, u32[]{:S(2)}, u32[]{:S(2)}) collective-permute-start(bf16[4,16,32,256]{3,2,1,0:T(8,128)(2,1)} %collective-permute-done.6.refs_2_), channel_id=1, source_target_pairs={{0,1},{1,0},{4,5},{5,4},{8,9},{9,8},{12,13},{13,12},{16,17},{17,16... | collective-permute-start | bytes 3145736 | tf_op jit(solution)/shard_map/ppermute | solution.py:266
  90.8 1.3 copy-start.4
  92.1 19.9 %collective-permute-start.10 = (bf16[2,16,32,256]{3,2,1,0:T(8,128)(2,1)}, bf16[2,16,32,256]{3,2,1,0:T(8,128)(2,1)S(1)}, u32[]{:S(2)}, u32[]{:S(2)}) collective-permute-start(bf16[2,16,32,256]{3,2,1,0:T(8,128)(2,1)} %collective-permute-done.8.refs_3_), channel_id=1, source_target_pairs={{0,1},{1,0},{4,5},{5,4},{8,9},{9,8},{12,13},{13,12},{16,17},{17,16... | collective-permute-start | bytes 1572872 | tf_op jit(solution)/shard_map/ppermute | solution.py:266
  92.1 19.9 %collective-permute-start.11 = (bf16[2,16,32,256]{3,2,1,0:T(8,128)(2,1)}, bf16[2,16,32,256]{3,2,1,0:T(8,128)(2,1)S(1)}, u32[]{:S(2)}, u32[]{:S(2)}) collective-permute-start(bf16[2,16,32,256]{3,2,1,0:T(8,128)(2,1)} %collective-permute-done.9.refs_4_), channel_id=1, source_target_pairs={{0,1},{1,0},{4,5},{5,4},{8,9},{9,8},{12,13},{13,12},{16,17},{17,16... | collective-permute-start | bytes 1572872 | tf_op jit(solution)/shard_map/ppermute | solution.py:266
  110.7 1.4 copy-start.3

commit v2 on v1

v2 whole, which is shorter than its diff:
```python
import functools
import math

import jax
import jax.numpy as jnp
import numpy as np
from jax import lax
from jax.experimental import pallas as pl
from jax.experimental.pallas import tpu as pltpu
from jax.sharding import PartitionSpec as P

HD = 128
ROPE_BASE = 1000000.0
bf16 = jnp.bfloat16
f32 = jnp.float32
AXES = ("blk", "head")
NT = (((1,), (1,)), ((), ()))
NEG = -1e30
TILES = 4
VMEM_LIMIT = 60 * 2**20


def device_id(x, y, z, core):
    return ((x % 2) * 4 + y) * 16 + z * 4 + (x // 2) * 2 + core


COORDS = [(x, y, z, c) for x in range(4) for y in range(4) for z in range(4) for c in range(2)]
SPREAD_GROUPS = [
    [device_id(xh * 2 + b // 4, b % 4, z, c) for b in range(8) for z in range(4)]
    for xh in range(2)
    for c in range(2)
]


def ring_perm(first_axis_core, shift):
    pairs = []
    for x, y, z, c in COORDS:
        if c == first_axis_core:
            target = device_id(x, (y + shift) % 4, z, c)
        else:
            target = device_id((x + shift) % 4, y, z, c)
        pairs.append((device_id(x, y, z, c), target))
    return pairs


SHIFTS = (0, -1, 1, 2)


def row_offsets(x, y, c):
    start = ((x % 4) // 2 * 2 + c) * 128 + ((x % 2) * 4 + y % 4) * 16
    return [start + half * 512 + r for half in range(2) for r in range(16)]


def line_offsets(x, y, c, shift):
    if c == 0:
        return [o for s in SHIFTS for o in row_offsets(x + shift, y + s, c)]
    return [o for s in SHIFTS for o in row_offsets(x + s, y + shift, c)]


def key_offsets(parts):
    table = np.zeros((128, 1, 128 * len(parts)), np.int32)
    for x, y, z, c in COORDS:
        row = [o for shift, own in parts for o in line_offsets(x, y, c if own else 1 - c, shift)]
        table[device_id(x, y, z, c), 0] = row
    return table


KEY_OFFSETS = [
    key_offsets([(0, True), (0, False)]),
    key_offsets([(-1, True), (1, True)]),
    key_offsets([(-1, False), (1, False), (2, True), (2, False)]),
]
SWAP = [(device_id(x, y, z, c), device_id(x, y, z, 1 - c)) for x, y, z, c in COORDS]


def rope_tables(positions):
    pair = jnp.arange(HD // 2, dtype=jnp.int32)
    inverse = jnp.exp(pair.astype(f32) * (-2.0 * math.log(ROPE_BASE) / HD))
    picked = jnp.where(
        pair[None, :] < 16,
        positions[0][:, None],
        jnp.where(pair[None, :] < 40, positions[1][:, None], positions[2][:, None]),
    )
    angles = picked.astype(f32) * inverse[None, :]
    cos, sin = jnp.cos(angles), jnp.sin(angles)
    return jnp.concatenate([cos, cos], axis=1), jnp.concatenate([-sin, sin], axis=1)


def pack_kernel(q_ref, k_ref, v_ref, cos_ref, sin_ref, out_ref):
    cos, sin = cos_ref[...], sin_ref[...]
    fold = math.log2(math.e) / math.sqrt(HD)
    qcos, qsin = cos * fold, sin * fold

    def rotate(x, c, s):
        x = x.astype(f32)
        return (x * c + pltpu.roll(x, HD // 2, 1) * s).astype(bf16).reshape(8, 16, HD)

    for h in range(8):
        cols = slice(h * HD, (h + 1) * HD)
        out_ref[:, 0, :, cols] = rotate(q_ref[:, cols], qcos, qsin)
    out_ref[:, 0, :, 8 * HD : 9 * HD] = rotate(k_ref[...], cos, sin)
    out_ref[:, 0, :, 9 * HD :] = v_ref[...].reshape(8, 16, HD)


def pack(q, k, v, cos, sin):
    table = pl.BlockSpec((128, HD), lambda z: (0, 0))
    small = pl.BlockSpec((128, HD), lambda z: (0, z))
    return pl.pallas_call(
        pack_kernel,
        out_shape=jax.ShapeDtypeStruct((8, 4, 16, 10 * HD), bf16),
        grid=(4,),
        in_specs=[pl.BlockSpec((128, 8 * HD), lambda z: (0, z)), small, small, table, table],
        out_specs=pl.BlockSpec((8, 1, 16, 10 * HD), lambda z: (0, z, 0, 0)),
        compiler_params=pltpu.CompilerParams(vmem_limit_bytes=VMEM_LIMIT),
        name="pack",
    )(q, k, v, cos, sin)


def unpack_kernel(x_ref, o_ref):
    o_ref[...] = x_ref[:, 0].reshape(128, 8 * HD)


def unpack(x):
    return pl.pallas_call(
        unpack_kernel,
        out_shape=jax.ShapeDtypeStruct((128, 32 * HD), bf16),
        grid=(4,),
        in_specs=[pl.BlockSpec((8, 1, 16, 8 * HD), lambda z: (0, z, 0, 0))],
        out_specs=pl.BlockSpec((128, 8 * HD), lambda z: (0, z)),
        compiler_params=pltpu.CompilerParams(vmem_limit_bytes=VMEM_LIMIT),
        name="unpack",
    )(x)


def attend_kernel(inv, *refs, n_kv, first, last):
    refs = list(refs)
    q_refs = [refs.pop(0) for _ in range(TILES)]
    kv_hbm = [refs.pop(0) for _ in range(n_kv)]
    kpos_ref = refs.pop(0)
    if not first:
        acc_in, ml_in = refs.pop(0), refs.pop(0)
    if last:
        o_hbm = refs.pop(0)
    else:
        acc_out, ml_out = refs.pop(0), refs.pop(0)
    m_ref, a_ref = refs.pop(0), refs.pop(0)
    kv_refs = [refs.pop(0) for _ in range(n_kv)]
    kv_sem = refs.pop(0)
    if last:
        o_ref, o_sem = refs
    pieces = sum(r.shape[0] for r in kv_refs)
    keys = pieces * 32
    per_unit = max(1, 1024 // keys)
    units = 2 if per_unit <= 2 else 1
    per_body = per_unit * units
    step = pl.program_id(0)
    base = step * TILES

    def fetch(i, order):
        block = inv[order]
        return pltpu.make_async_copy(
            kv_hbm[i].at[:, block], kv_refs[i].at[:, block], kv_sem.at[i, order]
        )

    def start_fetch(begin):
        for w in range(TILES):
            for i in range(n_kv):
                fetch(i, begin + w).start()

    @pl.when(step == 0)
    def _():
        start_fetch(0)

    @pl.when(step < 16 // TILES - 1)
    def _():
        start_fetch(base + TILES)

    def query_tile(ref):
        x = ref[0]
        return jnp.concatenate([x[:, h * HD : (h + 1) * HD] for h in range(8)], axis=0)

    def key_tile(orders):
        ks, vs = [], []
        for order in orders:
            block = inv[order]
            for r in kv_refs:
                kv = r[:, block].reshape(r.shape[0] * 32, 2 * HD)
                ks.append(kv[:, :HD])
                vs.append(kv[:, HD:])
        k = jnp.concatenate(ks, axis=0) if len(ks) > 1 else ks[0]
        v = jnp.concatenate(vs, axis=0) if len(vs) > 1 else vs[0]
        return k, jnp.concatenate([v, jnp.ones_like(v)], axis=1)

    rows = [pl.ds(w * 256, 256) for w in range(TILES)]
    for w in range(TILES):
        if first:
            m_ref[rows[w], :] = jnp.full((256, HD), NEG, f32)
            a_ref[rows[w], :] = jnp.zeros((256, 2 * HD), f32)
        else:
            ml = ml_in[w]
            m_ref[rows[w], :] = jnp.broadcast_to(ml[:, :1], (256, HD))
            a_ref[rows[w], :HD] = acc_in[w]
            a_ref[rows[w], HD:] = jnp.broadcast_to(ml[:, HD - 1 :], (256, HD))
    queries = [query_tile(r) for r in q_refs]

    def scores(w, tile, masked):
        s = lax.dot_general(queries[w], tile[0], NT, preferred_element_type=f32)
        if masked:
            row = lax.broadcasted_iota(jnp.int32, (256, HD), 0)
            device = inv[16]
            start = (device % 4) * 128 + (device // 16) * 16
            qpos = start + (row // 16 % 2) * 512 + row % 16
            allowed = jnp.tile(kpos_ref[0], (256, 1)) <= jnp.tile(qpos, (1, keys // HD))
            own = jnp.where(allowed, s[:, s.shape[1] - keys :], NEG)
            s = jnp.concatenate([s[:, : s.shape[1] - keys], own], axis=1) if s.shape[1] > keys else own
        return s

    def weigh(w, s):
        before = m_ref[rows[w], :]
        peak = jnp.maximum(before, jnp.max(s, axis=1, keepdims=True))
        p = jnp.exp2(s - jnp.tile(peak, (1, s.shape[1] // HD))).astype(bf16)
        m_ref[rows[w], :] = peak
        return p, jnp.exp2(before - peak)

    def add(w, p, factor, vext):
        o = jnp.dot(p, vext, preferred_element_type=f32)
        a_ref[rows[w], :] = a_ref[rows[w], :] * jnp.tile(factor, (1, 2)) + o

    def run(todo):
        ahead = scores(*todo[0])
        pending = None
        for i, (w, tile, _) in enumerate(todo):
            s = ahead
            if i + 1 < len(todo):
                ahead = scores(*todo[i + 1])
            p, factor = weigh(w, s)
            if pending is not None:
                add(*pending)
            pending = (w, p, factor, tile[1])
        add(*pending)

    def body(j, carry):
        tiles = [
            key_tile([j * per_body + u * per_unit + i for i in range(per_unit)])
            for u in range(units)
        ]
        run([(w, t, False) for t in tiles for w in range(TILES)])
        return carry

    lax.fori_loop(0, base // per_body, body, 0)

    for w in range(TILES):
        for i in range(n_kv):
            fetch(i, base + w).wait()
    todo = []
    for w in range(TILES):
        for start in range(0, w + 1, per_unit):
            stop = min(start + per_unit, w + 1)
            todo.append((w, key_tile([base + i for i in range(start, stop)]), stop == w + 1))
    run(todo)

    def store(order):
        block = inv[order]
        return pltpu.make_async_copy(o_ref.at[block], o_hbm.at[block], o_sem.at[order])

    for w in range(TILES):
        a = a_ref[rows[w], :]
        if last:
            o = (a[:, :HD] / a[:, HD:]).astype(bf16)
            block = inv[base + w]
            for h in range(8):
                o_ref[block, :, h * HD : (h + 1) * HD] = o[h * 32 : (h + 1) * 32]
            store(base + w).start()
        else:
            acc_out[w] = a[:, :HD]
            lane = lax.broadcasted_iota(jnp.int32, (256, HD), 1)
            ml_out[w] = jnp.where(lane < HD // 2, m_ref[rows[w], :], a[:, HD:])
    if last:

        @pl.when(step == 16 // TILES - 1)
        def _():
            for order in range(16):
                store(order).wait()


def attend(inv, q, kvs, kpos, state, last, name):
    first = state is None

    own_row = pl.BlockSpec((1, 1, kpos.shape[2]), lambda i, inv: (inv[16], 0, 0))

    def query_spec(w):
        return pl.BlockSpec((1, 32, 8 * HD), lambda i, inv: (inv[i * TILES + w], 0, 0))

    hbm = pl.BlockSpec(memory_space=pl.ANY)
    part = pl.BlockSpec((TILES, 256, HD), lambda i, inv: (i, 0, 0))
    operands = [q] * TILES + [*kvs, kpos]
    in_specs = [query_spec(w) for w in range(TILES)] + [hbm] * len(kvs) + [own_row]
    if not first:
        operands += list(state)
        in_specs += [part, part]
    full = jax.ShapeDtypeStruct((16, 256, HD), f32)
    mixed = jax.ShapeDtypeStruct((16, 32, 8 * HD), bf16)
    pieces = sum(x.shape[0] for x in kvs)
    work = 17 * 16 // 2 * 256 * 32 * pieces
    scratch = [
        pltpu.VMEM((TILES * 256, HD), f32),
        pltpu.VMEM((TILES * 256, 2 * HD), f32),
        *[pltpu.VMEM(x.shape, bf16) for x in kvs],
        pltpu.SemaphoreType.DMA((len(kvs), 16)),
    ]
    if last:
        scratch += [pltpu.VMEM(mixed.shape, bf16), pltpu.SemaphoreType.DMA((16,))]
    return pl.pallas_call(
        functools.partial(attend_kernel, n_kv=len(kvs), first=first, last=last),
        out_shape=mixed if last else (full, full),
        grid_spec=pltpu.PrefetchScalarGridSpec(
            num_scalar_prefetch=1,
            grid=(16 // TILES,),
            in_specs=in_specs,
            out_specs=hbm if last else (part, part),
            scratch_shapes=scratch,
        ),
        compiler_params=pltpu.CompilerParams(vmem_limit_bytes=VMEM_LIMIT),
        cost_estimate=pl.CostEstimate(
            flops=work * 1024, bytes_accessed=8 * 2**20, transcendentals=work
        ),
        name=name,
    )(inv, *operands)


def per_device(queries, keys, values, positions, block_order):
    cos, sin = rope_tables(positions)
    packed = pack(queries, keys, values, cos, sin)
    inv = jnp.sum(
        jnp.where(
            block_order[None, :] == jnp.arange(16, dtype=jnp.int32)[:, None],
            jnp.arange(16, dtype=jnp.int32)[None, :],
            0,
        ),
        axis=1,
    ).astype(jnp.int32)
    inv = jnp.concatenate([inv, lax.axis_index(AXES).astype(jnp.int32)[None]])

    def spread(t):
        return lax.all_to_all(t, AXES, 0, 0, axis_index_groups=SPREAD_GROUPS)

    q = spread(packed.reshape(32, 16, 10 * HD)).reshape(16, 32, 10 * HD)
    own = q[:, :, 8 * HD :]
    send = lambda t, perm: lax.ppermute(t, AXES, perm)
    plus1, minus1 = ring_perm(0, 1), ring_perm(0, -1)
    plus2, minus2 = ring_perm(1, 1), ring_perm(1, -1)

    from_minus = send(own, plus1)
    from_plus = send(own, minus1)
    far = jnp.concatenate(
        [send(from_minus[:, :16], plus1), send(from_plus[:, 16:], minus1)], axis=1
    )
    line = jnp.stack([own, from_minus, from_plus, far])
    line_other = send(line, SWAP)
    line_minus = send(line, plus2)
    line_plus = send(line, minus2)
    state = attend(inv, q, [line, line_other], KEY_OFFSETS[0], None, False, "attend_near")
    line_minus, line_plus, state = lax.optimization_barrier((line_minus, line_plus, state))
    far_a = send(line_minus[:2], plus2)
    far_b = send(line_plus[2:], minus2)
    minus_other, plus_other = send(line_minus, SWAP), send(line_plus, SWAP)
    state = attend(inv, q, [line_minus, line_plus], KEY_OFFSETS[1], state, False, "attend_next")
    far_a, far_b, state = lax.optimization_barrier((far_a, far_b, state))
    far_a_other, far_b_other = send(far_a, SWAP), send(far_b, SWAP)
    mixed = attend(
        inv,
        q,
        [minus_other, plus_other, far_a, far_b, far_a_other, far_b_other],
        KEY_OFFSETS[2],
        state,
        True,
        "attend_far",
    )
    back = spread(mixed.reshape(32, 16, 8 * HD)).reshape(8, 4, 16, 8 * HD)
    return unpack(back)


def solution(mesh):
    return jax.shard_map(
        per_device,
        mesh=mesh,
        in_specs=(P(AXES, None), P(AXES, None), P(AXES, None), P(None, AXES), P()),
        out_specs=P(AXES, None),
        check_vma=False,
    )
```

time: 167 us -> 159 us (0.952)
  blocking collectives: 23 us -> 49.8 us
  waiting for transfers between devices: 35.3 us -> 12.5 us
  starting transfers between devices: 27.1 us -> 12.3 us
  Pallas kernels: 64.4 us -> 75.6 us
  local copies, waits for them, and re-layouts: 11.8 us -> 3.5 us
  between operations: 2.57 us -> 0.19 us
    all_to_all x1 -> x2, blocking collectives: 23 us -> 49.8 us  [spread(): return lax.all_to_all(t, AXES, 0, 0, axis_index_groups=SPREAD_GROUPS)]
    ppermute x13, waiting for transfers between devices: 30 us -> 12.5 us  [per_device(): send = lambda t, perm: lax.ppermute(t, AXES, perm)]
    all_to_all x2 -> x0, starting transfers between devices: 14.8 us -> none  [spread(): return lax.all_to_all(t, AXES, 0, 0, axis_index_groups=SPREAD_GROUPS)]
    unnamed x13 -> x16, local copies, waits for them, and re-layouts: 7.07 us -> 1.15 us
    pallas_call x3, Pallas kernels: 62.6 us -> 68.3 us  [attend(): pl.pallas_call(functools.partial(attend_kernel, n_kv=len(kvs), first=firs...]
    pallas_call x1 -> x2, Pallas kernels: 1.76 us -> 7.28 us  [the longest x1 3.93 us: pack(): pl.pallas_call(pack_kernel, out_shape=jax.ShapeDtypeStruct((8, 4, 16, 10...]
    all_to_all x2 -> x0, waiting for transfers between devices: 5.37 us -> none  [spread(): return lax.all_to_all(t, AXES, 0, 0, axis_index_groups=SPREAD_GROUPS)]
    slice x1, local copies, waits for them, and re-layouts: 1.88 us -> 0.03 us  [per_device(): far_b = send(line_plus[2:], minus2)]
  transfers between devices with their start and end apart: 15 -> 13, of which waited for: 5 -> 5; matrix products, arithmetic and copies ran while one was open for 2% -> 0% of each run, Pallas kernels for 21% -> 24%
where the time goes in v2:
time: 159 us; the launch traced here: 156 us
  Pallas kernels  75.6 us (48%)
  blocking collectives  49.8 us (31%)
  waiting for transfers between devices  12.5 us (8%)
  starting transfers between devices  12.3 us (8%)
  local copies, waits for them, and re-layouts  3.5 us (2%)
  other arithmetic  1.94 us (1%)
    pallas_call x3, Pallas kernels, attend(): pl.pallas_call(functools.partial(attend_kernel, n_kv=len(kvs), first=firs...  68.3 us
    all_to_all x2, blocking collectives, spread(): return lax.all_to_all(t, AXES, 0, 0, axis_index_groups=SPREAD_GROUPS)  49.8 us
    ppermute x13, waiting for transfers between devices, per_device(): send = lambda t, perm: lax.ppermute(t, AXES, perm)  12.5 us
    ppermute x13, starting transfers between devices, per_device(): send = lambda t, perm: lax.ppermute(t, AXES, perm)  12.3 us
    pallas_call x1, Pallas kernels, pack(): pl.pallas_call(pack_kernel, out_shape=jax.ShapeDtypeStruct((8, 4, 16, 10...  3.93 us
    pallas_call x1, Pallas kernels, unpack(): pl.pallas_call(unpack_kernel, out_shape=jax.ShapeDtypeStruct((128, 32 * H...  3.36 us
  transfers between devices with their start and end apart: 13, of which 5 were waited for; matrix products, arithmetic and copies ran while one was open for 0% of the time, Pallas kernels for 24%

profile of v2, /device:TPU:24, one launch (start us, length us, event | category | flops | bytes accessed | tf_op | source)
XLA Modules:
  0.0 155.9 jit_solution(17628050757093265156)
XLA Ops:
  0.0 0.8 slice_bitcast_fusion.2
  0.8 0.3 fusion.2
  1.2 0.8 pad_maximum_fusion.1
  1.9 3.9 %pack.1 = bf16[8,4,16,1280]{3,2,1,0:T(8,128)(2,1)} custom-call(bf16[128,4096]{1,0:T(8,128)(2,1)} %q_ref.1, bf16[128,512]{1,0:T(8,128)(2,1)} %k_ref.1, bf16[128,512]{1,0:T(8,128)(2,1)} %v_ref.1, f32[128,128]{1,0:T(8,128)} %get-tuple-element.37.cos_ref, f32[128,128]{1,0:T(8,128)} %get-tuple-element.38.sin_ref), custom_call_target="tpu_custom_call" | custom-call | tf_op jit(solution)/shard_map/pack/pallas_call | solution.py:108
  5.9 28.0 %all_to_all.10 = bf16[32,16,1280]{2,1,0:T(8,128)(2,1)S(1)} all-to-all(bf16[32,16,1280]{2,1,0:T(8,128)(2,1)} %bitcast.17), channel_id=1, replica_groups={{0,4,8,12,16,20,24,28,32,36,40,44,48,52,56,60,64,68,72,76,80,84,88,92,9..., dimensions={0} | all-to-all | bytes 2621440 | tf_op jit(solution)/shard_map/all_to_all | solution.py:345
  33.9 2.0 %collective-permute-start = (bf16[16,32,256]{2,1,0:T(8,128)(2,1)S(1)}, bf16[16,32,256]{2,1,0:T(8,128)(2,1)S(1)}, u32[]{:S(2)}, u32[]{:S(2)}) collective-permute-start(bf16[16,32,256]{2,1,0:T(8,128)(2,1)S(1)} %get-tuple-element.30), channel_id=1, source_target_pairs={{0,16},{1,65},{4,20},{5,69},{8,24},{9,73},{12,28},{13,77},{16,32},... | collective-permute-start | bytes 786440 | tf_op jit(solution)/shard_map/ppermute | solution.py:349
  36.0 4.3 %collective-permute-done = bf16[16,32,256]{2,1,0:T(8,128)(2,1)S(1)} collective-permute-done((bf16[16,32,256]{2,1,0:T(8,128)(2,1)S(1)}, bf16[16,32,256]{2,1,0:T(8,128)(2,1)S(1)}, u32[]{:S(2)}, u32[]{:S(2)}) %collective-permute-start) | collective-permute-done | bytes 262176 | tf_op jit(solution)/shard_map/ppermute | solution.py:349
  40.3 3.2 %collective-permute-start.2 = (bf16[16,16,256]{2,1,0:T(8,128)(2,1)S(1)}, bf16[16,16,256]{2,1,0:T(8,128)(2,1)S(1)}, u32[]{:S(2)}, u32[]{:S(2)}) collective-permute-start(bf16[16,16,256]{2,1,0:T(8,128)(2,1)S(1)} %slice.33), channel_id=1, source_target_pairs={{0,16},{1,65},{4,20},{5,69},{8,24},{9,73},{12,28},{13,77},{16,32},... | collective-permute-start | bytes 393224 | tf_op jit(solution)/shard_map/ppermute | solution.py:349
  43.6 2.4 %collective-permute-done.2 = bf16[16,16,256]{2,1,0:T(8,128)(2,1)S(1)} collective-permute-done((bf16[16,16,256]{2,1,0:T(8,128)(2,1)S(1)}, bf16[16,16,256]{2,1,0:T(8,128)(2,1)S(1)}, u32[]{:S(2)}, u32[]{:S(2)}) %collective-permute-start.2) | collective-permute-done | bytes 131104 | tf_op jit(solution)/shard_map/ppermute | solution.py:349
  46.1 3.7 %collective-permute-done.3 = bf16[16,16,256]{2,1,0:T(8,128)(2,1)S(1)} collective-permute-done((bf16[16,16,256]{2,1,0:T(8,128)(2,1)S(1)}, bf16[16,16,256]{2,1,0:T(8,128)(2,1)S(1)}, u32[]{:S(2)}, u32[]{:S(2)}) %collective-permute-start.3) | collective-permute-done | bytes 131104 | tf_op jit(solution)/shard_map/ppermute | solution.py:349
  50.1 2.0 %collective-permute-start.5 = (bf16[4,16,32,256]{3,2,1,0:T(8,128)(2,1)S(1)}, bf16[4,16,32,256]{3,2,1,0:T(8,128)(2,1)S(1)}, u32[]{:S(2)}, u32[]{:S(2)}) collective-permute-start(bf16[4,16,32,256]{3,2,1,0:T(8,128)(2,1)S(1)} %pad_maximum_fusion.refs_4_), channel_id=1, source_target_pairs={{0,66},{1,49},{4,70},{5,53},{8,74},{9,57},{12,78},{13,61},{16,82},... | collective-permute-start | bytes 3145736 | tf_op jit(solution)/shard_map/ppermute | solution.py:349
  52.3 0.6 pad_add_fusion.inv
  52.9 18.5 %attend_near.1 = (f32[16,256,128]{2,1,0:T(8,128)}, f32[16,256,128]{2,1,0:T(8,128)}) custom-call(s32[17]{0:T(128)} %pad_add_fusion.inv, bf16[16,32,1280]{2,1,0:T(8,128)(2,1)} %bitcast.20, bf16[16,32,1280]{2,1,0:T(8,128)(2,1)} %bitcast.21, bf16[16,32,1280]{2,1,0:T(8,128)(2,1)} %bitcast.22, bf16[16,32,1280]{2,1,0:T(8,128)(2,1)} %bitcast.23, ...), custom_call_target="tpu_custom_call" | custom-call | flops 9126805504 | bytes 8388608 | tf_op jit(solution)/shard_map/attend_near/pallas_call | solution.py:313
  71.4 1.5 slice.30
  72.9 1.2 collective-permute-start.7
  74.2 2.6 %collective-permute-start.10 = (bf16[2,16,32,256]{3,2,1,0:T(8,128)(2,1)S(1)}, bf16[2,16,32,256]{3,2,1,0:T(8,128)(2,1)S(1)}, u32[]{:S(2)}, u32[]{:S(2)}) collective-permute-start(bf16[2,16,32,256]{3,2,1,0:T(8,128)(2,1)S(1)} %slice.31), channel_id=1, source_target_pairs={{0,66},{1,49},{4,70},{5,53},{8,74},{9,57},{12,78},{13,61},{16,82},... | collective-permute-start | bytes 1572872 | tf_op jit(solution)/shard_map/ppermute | solution.py:349
  76.8 19.7 %attend_next.1 = (f32[16,256,128]{2,1,0:T(8,128)}, f32[16,256,128]{2,1,0:T(8,128)}) custom-call(s32[17]{0:T(128)} %pad_add_fusion.inv, bf16[16,32,1280]{2,1,0:T(8,128)(2,1)} %bitcast.24, bf16[16,32,1280]{2,1,0:T(8,128)(2,1)} %bitcast.25, bf16[16,32,1280]{2,1,0:T(8,128)(2,1)} %bitcast.26, bf16[16,32,1280]{2,1,0:T(8,128)(2,1)} %bitcast.27, ...), custom_call_target="tpu_custom_call" | custom-call | flops 9126805504 | bytes 8388608 | tf_op jit(solution)/shard_map/attend_next/pallas_call | solution.py:313
  96.5 0.7 collective-permute-start.11
  97.4 1.5 collective-permute-done.11.refs_8_
  98.9 0.5 collective-permute-done.12.refs_9_
  99.7 0.5 copy-done.6
  100.6 30.1 %attend_far.1 = bf16[16,32,1024]{2,1,0:T(8,128)(2,1)} custom-call(s32[17]{0:T(128)} %pad_add_fusion.inv, bf16[16,32,1280]{2,1,0:T(8,128)(2,1)} %bitcast.28, bf16[16,32,1280]{2,1,0:T(8,128)(2,1)} %bitcast.29, bf16[16,32,1280]{2,1,0:T(8,128)(2,1)} %bitcast.30, bf16[16,32,1280]{2,1,0:T(8,128)(2,1)} %bitcast.31, bf16[4,16,32,256]{3,2,1,0:T(8,128)(2,1)} %copy-done.3, ...), custom_call_target="tpu_custom_call" | custom-call | flops 18253611008 | bytes 8388608 | tf_op jit(solution)/shard_map/attend_far/pallas_call | solution.py:313
  130.7 21.8 %all_to_all.11 = bf16[32,16,1024]{2,1,0:T(8,128)(2,1)} all-to-all(bf16[32,16,1024]{2,1,0:T(8,128)(2,1)} %bitcast.32), channel_id=1, replica_groups={{0,4,8,12,16,20,24,28,32,36,40,44,48,52,56,60,64,68,72,76,80,84,88,92,9..., dimensions={0} | all-to-all | bytes 2097152 | tf_op jit(solution)/shard_map/all_to_all | solution.py:345
  152.5 3.4 %unpack.1 = bf16[128,4096]{1,0:T(8,128)(2,1)} custom-call(bf16[8,4,16,1024]{3,2,1,0:T(8,128)(2,1)} %bitcast.18), custom_call_target="tpu_custom_call" | custom-call | tf_op jit(solution)/shard_map/unpack/pallas_call | solution.py:124
  (40 shorter events, 1.7 us)
Async XLA Ops:
  33.8 19.0 %copy-start = (bf16[32,16,1280]{2,1,0:T(8,128)(2,1)}, bf16[32,16,1280]{2,1,0:T(8,128)(2,1)S(1)}, u32[]{:S(2)}) copy-start(bf16[32,16,1280]{2,1,0:T(8,128)(2,1)S(1)} %all_to_all.10) | copy-start | bytes 3932164
  33.8 18.4 %copy-start.7 = (s32[16]{0:T(128)S(1)}, s32[16]{0:T(128)}, u32[]{:S(2)}) copy-start(s32[16]{0:T(128)} %param.12) | copy-start | bytes 196
  33.9 6.4 %collective-permute-start = (bf16[16,32,256]{2,1,0:T(8,128)(2,1)S(1)}, bf16[16,32,256]{2,1,0:T(8,128)(2,1)S(1)}, u32[]{:S(2)}, u32[]{:S(2)}) collective-permute-start(bf16[16,32,256]{2,1,0:T(8,128)(2,1)S(1)} %get-tuple-element.30), channel_id=1, source_target_pairs={{0,16},{1,65},{4,20},{5,69},{8,24},{9,73},{12,28},{13,77},{16,32},... | collective-permute-start | bytes 786440 | tf_op jit(solution)/shard_map/ppermute | solution.py:349
  35.9 7.7 %collective-permute-start.1 = (bf16[16,32,256]{2,1,0:T(8,128)(2,1)S(1)}, bf16[16,32,256]{2,1,0:T(8,128)(2,1)S(1)}, u32[]{:S(2)}, u32[]{:S(2)}) collective-permute-start(bf16[16,32,256]{2,1,0:T(8,128)(2,1)S(1)} %get-tuple-element.30), channel_id=1, source_target_pairs={{0,48},{1,67},{4,52},{5,71},{8,56},{9,75},{12,60},{13,79},{16,0},{... | collective-permute-start | bytes 786440 | tf_op jit(solution)/shard_map/ppermute | solution.py:349
  40.3 5.7 %collective-permute-start.2 = (bf16[16,16,256]{2,1,0:T(8,128)(2,1)S(1)}, bf16[16,16,256]{2,1,0:T(8,128)(2,1)S(1)}, u32[]{:S(2)}, u32[]{:S(2)}) collective-permute-start(bf16[16,16,256]{2,1,0:T(8,128)(2,1)S(1)} %slice.33), channel_id=1, source_target_pairs={{0,16},{1,65},{4,20},{5,69},{8,24},{9,73},{12,28},{13,77},{16,32},... | collective-permute-start | bytes 393224 | tf_op jit(solution)/shard_map/ppermute | solution.py:349
  43.6 6.2 %collective-permute-start.3 = (bf16[16,16,256]{2,1,0:T(8,128)(2,1)S(1)}, bf16[16,16,256]{2,1,0:T(8,128)(2,1)S(1)}, u32[]{:S(2)}, u32[]{:S(2)}) collective-permute-start(bf16[16,16,256]{2,1,0:T(8,128)(2,1)S(1)} %slice.34), channel_id=1, source_target_pairs={{0,48},{1,67},{4,52},{5,71},{8,56},{9,75},{12,60},{13,79},{16,0},{... | collective-permute-start | bytes 393224 | tf_op jit(solution)/shard_map/ppermute | solution.py:349
  50.0 2.9 %copy-start.1 = (bf16[4,16,32,256]{3,2,1,0:T(8,128)(2,1)}, bf16[4,16,32,256]{3,2,1,0:T(8,128)(2,1)S(1)}, u32[]{:S(2)}) copy-start(bf16[4,16,32,256]{3,2,1,0:T(8,128)(2,1)S(1)} %pad_maximum_fusion.refs_4_) | copy-start | bytes 3145732
  50.0 2.9 %collective-permute-start.6 = (bf16[4,16,32,256]{3,2,1,0:T(8,128)(2,1)S(1)}, bf16[4,16,32,256]{3,2,1,0:T(8,128)(2,1)}, u32[]{:S(2)}, u32[]{:S(2)}) collective-permute-start(bf16[4,16,32,256]{3,2,1,0:T(8,128)(2,1)S(1)} %pad_maximum_fusion.refs_4_), channel_id=1, source_target_pairs={{0,1},{1,0},{4,5},{5,4},{8,9},{9,8},{12,13},{13,12},{16,17},{17,16... | collective-permute-start | bytes 3145736 | tf_op jit(solution)/shard_map/ppermute | solution.py:349
  50.1 21.3 %collective-permute-start.5 = (bf16[4,16,32,256]{3,2,1,0:T(8,128)(2,1)S(1)}, bf16[4,16,32,256]{3,2,1,0:T(8,128)(2,1)S(1)}, u32[]{:S(2)}, u32[]{:S(2)}) collective-permute-start(bf16[4,16,32,256]{3,2,1,0:T(8,128)(2,1)S(1)} %pad_maximum_fusion.refs_4_), channel_id=1, source_target_pairs={{0,66},{1,49},{4,70},{5,53},{8,74},{9,57},{12,78},{13,61},{16,82},... | collective-permute-start | bytes 3145736 | tf_op jit(solution)/shard_map/ppermute | solution.py:349
  52.1 19.3 %collective-permute-start.4 = (bf16[4,16,32,256]{3,2,1,0:T(8,128)(2,1)S(1)}, bf16[4,16,32,256]{3,2,1,0:T(8,128)(2,1)}, u32[]{:S(2)}, u32[]{:S(2)}) collective-permute-start(bf16[4,16,32,256]{3,2,1,0:T(8,128)(2,1)S(1)} %pad_maximum_fusion.refs_4_), channel_id=1, source_target_pairs={{0,64},{1,17},{4,68},{5,21},{8,72},{9,25},{12,76},{13,29},{16,80},... | collective-permute-start | bytes 3145736 | tf_op jit(solution)/shard_map/ppermute | solution.py:349
  71.4 5.4 %copy-start.2 = (bf16[4,16,32,256]{3,2,1,0:T(8,128)(2,1)}, bf16[4,16,32,256]{3,2,1,0:T(8,128)(2,1)S(1)}, u32[]{:S(2)}) copy-start(bf16[4,16,32,256]{3,2,1,0:T(8,128)(2,1)S(1)} %collective-permute-done.5.refs_5_) | copy-start | bytes 3145732
  72.9 26.6 %collective-permute-start.7 = (bf16[4,16,32,256]{3,2,1,0:T(8,128)(2,1)}, bf16[4,16,32,256]{3,2,1,0:T(8,128)(2,1)S(1)}, u32[]{:S(2)}, u32[]{:S(2)}) collective-permute-start(bf16[4,16,32,256]{3,2,1,0:T(8,128)(2,1)} %collective-permute-done.4.refs_4_), channel_id=1, source_target_pairs={{0,1},{1,0},{4,5},{5,4},{8,9},{9,8},{12,13},{13,12},{16,17},{17,16... | collective-permute-start | bytes 3145736 | tf_op jit(solution)/shard_map/ppermute | solution.py:349
  74.1 25.4 %collective-permute-start.8 = (bf16[4,16,32,256]{3,2,1,0:T(8,128)(2,1)S(1)}, bf16[4,16,32,256]{3,2,1,0:T(8,128)(2,1)}, u32[]{:S(2)}, u32[]{:S(2)}) collective-permute-start(bf16[4,16,32,256]{3,2,1,0:T(8,128)(2,1)S(1)} %collective-permute-done.5.refs_5_), channel_id=1, source_target_pairs={{0,1},{1,0},{4,5},{5,4},{8,9},{9,8},{12,13},{13,12},{16,17},{17,16... | collective-permute-start | bytes 3145736 | tf_op jit(solution)/shard_map/ppermute | solution.py:349
  74.2 22.3 %collective-permute-start.10 = (bf16[2,16,32,256]{3,2,1,0:T(8,128)(2,1)S(1)}, bf16[2,16,32,256]{3,2,1,0:T(8,128)(2,1)S(1)}, u32[]{:S(2)}, u32[]{:S(2)}) collective-permute-start(bf16[2,16,32,256]{3,2,1,0:T(8,128)(2,1)S(1)} %slice.31), channel_id=1, source_target_pairs={{0,66},{1,49},{4,70},{5,53},{8,74},{9,57},{12,78},{13,61},{16,82},... | collective-permute-start | bytes 1572872 | tf_op jit(solution)/shard_map/ppermute | solution.py:349
  76.8 19.7 %collective-permute-start.9 = (bf16[2,16,32,256]{3,2,1,0:T(8,128)(2,1)S(1)}, bf16[2,16,32,256]{3,2,1,0:T(8,128)(2,1)}, u32[]{:S(2)}, u32[]{:S(2)}) collective-permute-start(bf16[2,16,32,256]{3,2,1,0:T(8,128)(2,1)S(1)} %slice.30), channel_id=1, source_target_pairs={{0,64},{1,17},{4,68},{5,21},{8,72},{9,25},{12,76},{13,29},{16,80},... | collective-permute-start | bytes 1572872 | tf_op jit(solution)/shard_map/ppermute | solution.py:349
  96.5 3.0 %copy-start.4 = (bf16[2,16,32,256]{3,2,1,0:T(8,128)(2,1)}, bf16[2,16,32,256]{3,2,1,0:T(8,128)(2,1)S(1)}, u32[]{:S(2)}) copy-start(bf16[2,16,32,256]{3,2,1,0:T(8,128)(2,1)S(1)} %collective-permute-done.10.refs_7_) | copy-start | bytes 1572868
  96.5 2.4 %collective-permute-start.11 = (bf16[2,16,32,256]{3,2,1,0:T(8,128)(2,1)}, bf16[2,16,32,256]{3,2,1,0:T(8,128)(2,1)S(1)}, u32[]{:S(2)}, u32[]{:S(2)}) collective-permute-start(bf16[2,16,32,256]{3,2,1,0:T(8,128)(2,1)} %collective-permute-done.9.refs_6_), channel_id=1, source_target_pairs={{0,1},{1,0},{4,5},{5,4},{8,9},{9,8},{12,13},{13,12},{16,17},{17,16... | collective-permute-start | bytes 1572872 | tf_op jit(solution)/shard_map/ppermute | solution.py:349
  97.1 2.3 %collective-permute-start.12 = (bf16[2,16,32,256]{3,2,1,0:T(8,128)(2,1)S(1)}, bf16[2,16,32,256]{3,2,1,0:T(8,128)(2,1)S(1)}, u32[]{:S(2)}, u32[]{:S(2)}) collective-permute-start(bf16[2,16,32,256]{3,2,1,0:T(8,128)(2,1)S(1)} %collective-permute-done.10.refs_7_), channel_id=1, source_target_pairs={{0,1},{1,0},{4,5},{5,4},{8,9},{9,8},{12,13},{13,12},{16,17},{17,16... | collective-permute-start | bytes 1572872 | tf_op jit(solution)/shard_map/ppermute | solution.py:349
  98.9 0.8 copy-start.5
  99.4 0.8 copy-start.6
  99.4 1.1 copy-start.3

commit v3 on v1

v3 whole, which is shorter than its diff:
```python
import functools
import math

import jax
import jax.numpy as jnp
import numpy as np
from jax import lax
from jax.experimental import pallas as pl
from jax.experimental.pallas import tpu as pltpu
from jax.sharding import PartitionSpec as P

HD = 128
ROPE_BASE = 1000000.0
bf16 = jnp.bfloat16
f32 = jnp.float32
AXES = ("blk", "head")
NT = (((1,), (1,)), ((), ()))
NEG = -1e30
CHAINS = 4
VMEM_LIMIT = 24 * 2**20


def device_id(x, y, z, core):
    return ((x % 2) * 4 + y) * 16 + z * 4 + (x // 2) * 2 + core


COORDS = [(x, y, z, c) for x in range(4) for y in range(4) for z in range(4) for c in range(2)]
SPREAD_GROUPS = [
    [device_id(xh * 2 + b // 4, b % 4, z, c) for b in range(8) for z in range(4)]
    for xh in range(2)
    for c in range(2)
]


def ring_perm(first_axis_core, shift):
    pairs = []
    for x, y, z, c in COORDS:
        if c == first_axis_core:
            target = device_id(x, (y + shift) % 4, z, c)
        else:
            target = device_id((x + shift) % 4, y, z, c)
        pairs.append((device_id(x, y, z, c), target))
    return pairs


SHIFTS = (0, -1, 1, 2)


def row_offsets(x, y, c):
    start = ((x % 4) // 2 * 2 + c) * 128 + ((x % 2) * 4 + y % 4) * 16
    return [start + half * 512 + r for half in range(2) for r in range(16)]


def line_offsets(x, y, c, shift):
    if c == 0:
        return [o for s in SHIFTS for o in row_offsets(x + shift, y + s, c)]
    return [o for s in SHIFTS for o in row_offsets(x + s, y + shift, c)]


def key_offsets(parts):
    table = np.zeros((128, 128 * len(parts)), np.int32)
    for x, y, z, c in COORDS:
        row = [o for shift, own in parts for o in line_offsets(x, y, c if own else 1 - c, shift)]
        table[device_id(x, y, z, c)] = row
    return table


KEY_OFFSETS = key_offsets(
    [(0, True), (0, False)]
    + [(-1, True), (1, True)]
    + [(-1, False), (1, False), (2, True), (2, False)]
)
SWAP = [(device_id(x, y, z, c), device_id(x, y, z, 1 - c)) for x, y, z, c in COORDS]


def rope_tables(pos_ref):
    lane = lax.broadcasted_iota(jnp.int32, (128, HD), 1) % (HD // 2)
    inverse = jnp.exp(lane.astype(f32) * (-2.0 * math.log(ROPE_BASE) / HD))
    columns = [
        jnp.transpose(jnp.broadcast_to(pos_ref[i : i + 1, :].astype(f32), (128, 128)))
        for i in range(3)
    ]
    angles = jnp.where(lane < 16, columns[0], jnp.where(lane < 40, columns[1], columns[2])) * inverse
    upper = lax.broadcasted_iota(jnp.int32, (128, HD), 1) >= HD // 2
    sin = jnp.sin(angles)
    return jnp.cos(angles), jnp.where(upper, sin, -sin)


def pack_kernel(q_hbm, k_hbm, v_hbm, pos_ref, out_ref, q_ref, k_ref, v_ref, sem):
    copies = [
        pltpu.make_async_copy(k_hbm, k_ref, sem.at[4]),
        pltpu.make_async_copy(v_hbm, v_ref, sem.at[5]),
    ]
    for z in range(4):
        cols = pl.ds(z * 8 * HD, 8 * HD)
        copies.append(pltpu.make_async_copy(q_hbm.at[:, cols], q_ref.at[:, cols], sem.at[z]))
    for c in copies:
        c.start()
    cos, sin = rope_tables(pos_ref)
    fold = math.log2(math.e) / math.sqrt(HD)
    qcos, qsin = cos * fold, sin * fold

    def rotate(x, c, s):
        x = x.astype(f32)
        return (x * c + pltpu.roll(x, HD // 2, 1) * s).astype(bf16).reshape(8, 16, HD)

    copies[0].wait()
    copies[1].wait()
    for z in range(4):
        cols = slice(z * HD, (z + 1) * HD)
        out_ref[:, z, :, 8 * HD : 9 * HD] = rotate(k_ref[:, cols], cos, sin)
        out_ref[:, z, :, 9 * HD :] = v_ref[:, cols].reshape(8, 16, HD)
    for z in range(4):
        copies[2 + z].wait()
        for h in range(8):
            col = (z * 8 + h) * HD
            out_ref[:, z, :, h * HD : (h + 1) * HD] = rotate(q_ref[:, col : col + HD], qcos, qsin)


VMEM = pl.BlockSpec(memory_space=pltpu.VMEM)
HBM = pl.BlockSpec(memory_space=pltpu.HBM)
SMEM = pl.BlockSpec(memory_space=pltpu.SMEM)


def pack(q, k, v, positions):
    return pl.pallas_call(
        pack_kernel,
        out_shape=jax.ShapeDtypeStruct((8, 4, 16, 10 * HD), bf16),
        in_specs=[HBM, HBM, HBM, VMEM],
        out_specs=VMEM,
        scratch_shapes=[
            pltpu.VMEM(q.shape, bf16),
            pltpu.VMEM(k.shape, bf16),
            pltpu.VMEM(v.shape, bf16),
            pltpu.SemaphoreType.DMA((6,)),
        ],
        compiler_params=pltpu.CompilerParams(vmem_limit_bytes=VMEM_LIMIT),
        name="pack",
    )(q, k, v, positions)


def unpack_kernel(*refs):
    *parts, o_hbm, sem = refs
    width = parts[0].shape[3]
    copies = [
        pltpu.make_async_copy(
            part.at[:, z],
            o_hbm.at[:, :, pl.ds((z * len(parts) + i) * width, width)],
            sem.at[i, z],
        )
        for i, part in enumerate(parts)
        for z in range(4)
    ]
    for c in copies:
        c.start()
    for c in copies:
        c.wait()


def unpack(parts):
    out = pl.pallas_call(
        unpack_kernel,
        out_shape=jax.ShapeDtypeStruct((8, 16, 32 * HD), bf16),
        in_specs=[VMEM] * len(parts),
        out_specs=HBM,
        scratch_shapes=[pltpu.SemaphoreType.DMA((len(parts), 4))],
        compiler_params=pltpu.CompilerParams(vmem_limit_bytes=VMEM_LIMIT),
        name="unpack",
    )(*parts)
    return out.reshape(128, 32 * HD)


def attend_kernel(meta, *refs, n_kv, first, last, heads):
    refs = list(refs)
    q_ref = refs.pop(0)
    kv_refs = [refs.pop(0) for _ in range(n_kv)]
    kpos_ref = refs.pop(0)
    if not first:
        m_in, a_in = refs.pop(0), refs.pop(0)
    if last:
        o_ref, m_ref, a_ref = refs
    else:
        m_ref, a_ref = refs
    head0, head_count = heads
    block_rows = 32 * head_count
    span = 256 // block_rows
    tiles = CHAINS * span
    keys = sum(r.shape[0] for r in kv_refs) * 32
    per_unit = max(span, 1024 // keys)
    units = 2 if per_unit <= 2 else 1
    per_body = per_unit * units
    rows = [pl.ds(c * 256, 256) for c in range(CHAINS)]

    def query_tile(order):
        parts = []
        for i in range(span):
            x = q_ref[meta[order + i]]
            parts += [x[:, h * HD : (h + 1) * HD] for h in range(head0, head0 + head_count)]
        return jnp.concatenate(parts, axis=0)

    def key_tile(orders):
        ks, vs = [], []
        for order in orders:
            block = meta[order]
            for r in kv_refs:
                kv = r[:, block].reshape(r.shape[0] * 32, 2 * HD)
                ks.append(kv[:, :HD])
                vs.append(kv[:, HD:])
        k = jnp.concatenate(ks, axis=0) if len(ks) > 1 else ks[0]
        v = jnp.concatenate(vs, axis=0) if len(vs) > 1 else vs[0]
        return k, jnp.concatenate([v, jnp.ones_like(v)], axis=1)

    def step(index, carry):
        base = index * tiles
        if last:
            m_at = [m_ref.at[rows[c]] for c in range(CHAINS)]
            a_at = [a_ref.at[rows[c]] for c in range(CHAINS)]
        else:
            m_at = [m_ref.at[base + c] for c in range(CHAINS)]
            a_at = [a_ref.at[base + c] for c in range(CHAINS)]
        for c in range(CHAINS):
            if first:
                m_at[c][...] = jnp.full((256, HD), NEG, f32)
                a_at[c][...] = jnp.zeros((256, 2 * HD), f32)
            elif last:
                for i in range(span):
                    source = pl.ds(32 * head0, block_rows)
                    target = pl.ds(c * 256 + i * block_rows, block_rows)
                    m_ref[target, :] = m_in[base + c * span + i, source, :]
                    a_ref[target, :] = a_in[base + c * span + i, source, :]
        queries = [query_tile(base + c * span) for c in range(CHAINS)]

        def scores(c, tile, masked):
            s = lax.dot_general(queries[c], tile[0], NT, preferred_element_type=f32)
            if masked:
                row = lax.broadcasted_iota(jnp.int32, (256, HD), 0)
                device = meta[16]
                start = (device % 4) * 128 + (device // 16) * 16
                qpos = start + (row // 16 % 2) * 512 + row % 16 + row // block_rows * 1024
                kpos = jnp.concatenate([kpos_ref[...] + i * 1024 for i in range(span)], axis=1)
                own = span * keys
                allowed = jnp.tile(kpos, (256, 1)) <= jnp.tile(qpos, (1, own // HD))
                rest = s.shape[1] - own
                diagonal = jnp.where(allowed, s[:, rest:], NEG)
                s = jnp.concatenate([s[:, :rest], diagonal], axis=1) if rest else diagonal
            return s

        def weigh(c, s):
            before = m_at[c][...]
            peak = jnp.maximum(before, jnp.max(s, axis=1, keepdims=True))
            p = jnp.exp2(s - jnp.tile(peak, (1, s.shape[1] // HD))).astype(bf16)
            m_at[c][...] = peak
            return p, jnp.exp2(before - peak)

        def add(c, p, factor, vext):
            o = jnp.dot(p, vext, preferred_element_type=f32)
            a_at[c][...] = a_at[c][...] * jnp.tile(factor, (1, 2)) + o

        def run(todo):
            ahead = scores(*todo[0])
            pending = None
            for i, (c, tile, _) in enumerate(todo):
                s = ahead
                if i + 1 < len(todo):
                    ahead = scores(*todo[i + 1])
                p, factor = weigh(c, s)
                if pending is not None:
                    add(*pending)
                pending = (c, p, factor, tile[1])
            add(*pending)

        def body(j, carry):
            found = [
                key_tile([j * per_body + u * per_unit + i for i in range(per_unit)])
                for u in range(units)
            ]
            run([(c, t, False) for t in found for c in range(CHAINS)])
            return carry

        lax.fori_loop(0, base // per_body, body, 0)

        todo = []
        for c in range(CHAINS):
            end = (c + 1) * span
            for begin in range(0, end, per_unit):
                stop = min(begin + per_unit, end)
                todo.append((c, key_tile([base + i for i in range(begin, stop)]), stop == end))
        run(todo)

        if last:
            for c in range(CHAINS):
                a = a_at[c][...]
                o = (a[:, :HD] / a[:, HD:]).astype(bf16)
                for i in range(span):
                    block = meta[base + c * span + i]
                    for h in range(head_count):
                        at = i * block_rows + h * 32
                        o_ref[block, :, h * HD : (h + 1) * HD] = o[at : at + 32]
        return carry

    lax.fori_loop(0, 16 // tiles, step, 0)


def attend(meta, q, kvs, kpos, state, heads, name):
    first, last = state is None, heads is not None
    heads = heads or (0, 8)
    operands = [meta, q, *kvs, kpos]
    in_specs = [SMEM] + [VMEM] * (len(operands) - 1)
    aliases = {}
    if not first:
        if not last:
            aliases = {len(operands): 0, len(operands) + 1: 1}
        operands += list(state)
        in_specs += [VMEM, VMEM]
    pieces = sum(x.shape[0] for x in kvs)
    work = 17 * 16 // 2 * 32 * heads[1] * 32 * pieces
    scratch = []
    if last:
        out_shape = jax.ShapeDtypeStruct((16, 32, heads[1] * HD), bf16)
        scratch = [
            pltpu.VMEM((CHAINS * 256, HD), f32),
            pltpu.VMEM((CHAINS * 256, 2 * HD), f32),
        ]
    else:
        out_shape = (
            jax.ShapeDtypeStruct((16, 256, HD), f32),
            jax.ShapeDtypeStruct((16, 256, 2 * HD), f32),
        )
    return pl.pallas_call(
        functools.partial(attend_kernel, n_kv=len(kvs), first=first, last=last, heads=heads),
        out_shape=out_shape,
        in_specs=in_specs,
        out_specs=VMEM if last else (VMEM, VMEM),
        scratch_shapes=scratch,
        input_output_aliases=aliases,
        compiler_params=pltpu.CompilerParams(vmem_limit_bytes=VMEM_LIMIT),
        cost_estimate=pl.CostEstimate(
            flops=work * 1024, bytes_accessed=8 * 2**20, transcendentals=work
        ),
        name=name,
    )(*operands)


def per_device(queries, keys, values, positions, block_order):
    device = lax.axis_index(AXES).astype(jnp.int32)
    order = jnp.arange(16, dtype=jnp.int32)
    inverse = jnp.sum(jnp.where(block_order[None, :] == order[:, None], order[None, :], 0), axis=1)
    meta = jnp.concatenate([inverse.astype(jnp.int32), device[None]])
    offsets = lax.dynamic_index_in_dim(jnp.asarray(KEY_OFFSETS), device, 0, keepdims=True)
    near_at, next_at, far_at = offsets[:, :256], offsets[:, 256:512], offsets[:, 512:]

    def spread(t):
        return lax.all_to_all(t, AXES, 0, 0, axis_index_groups=SPREAD_GROUPS)

    def send(t, perm):
        return lax.ppermute(t, AXES, perm)

    packed = pack(queries, keys, values, positions)
    q = spread(packed.reshape(32, 16, 10 * HD)).reshape(16, 32, 10 * HD)
    own = q[:, :, 8 * HD :]

    line = jnp.stack([own, *[send(own, ring_perm(0, s)) for s in (1, -1, 2)]])
    line_other = send(line, SWAP)
    line_minus, line_plus = send(line, ring_perm(1, 1)), send(line, ring_perm(1, -1))
    state = attend(meta, q, [line, line_other], near_at, None, None, "attend_near")
    line, line_minus, line_plus, state = lax.optimization_barrier(
        (line, line_minus, line_plus, state)
    )
    line_far = send(line, ring_perm(1, 2))
    minus_other, plus_other = send(line_minus, SWAP), send(line_plus, SWAP)
    state = attend(meta, q, [line_minus, line_plus], next_at, state, None, "attend_next")
    line_far, state = lax.optimization_barrier((line_far, state))
    far = [minus_other, plus_other, line_far, send(line_far, SWAP)]
    outs = []
    for half in range(2):
        mixed = attend(meta, q, far, far_at, state, (half * 4, 4), "attend_far")
        outs.append(spread(mixed.reshape(32, 16, 4 * HD)).reshape(8, 4, 16, 4 * HD))
    return unpack(outs)


def solution(mesh):
    return jax.shard_map(
        per_device,
        mesh=mesh,
        in_specs=(P(AXES, None), P(AXES, None), P(AXES, None), P(None, AXES), P()),
        out_specs=P(AXES, None),
        check_vma=False,
    )
```

time: 167 us -> 155 us (0.928)
  waiting for transfers between devices: 35.3 us -> 10.5 us
  blocking collectives: 23 us -> 45.8 us
  starting transfers between devices: 27.1 us -> 15 us
  local copies, waits for them, and re-layouts: 11.8 us -> 16.2 us
  between operations: 2.57 us -> 0.31 us
    all_to_all x1 -> x2, blocking collectives: 23 us -> 45.8 us  [spread(): return lax.all_to_all(t, AXES, 0, 0, axis_index_groups=SPREAD_GROUPS)]
    ppermute x13 -> x10, waiting for transfers between devices: 30 us -> 10.5 us  [send(): return lax.ppermute(t, AXES, perm)]
    all_to_all x2 -> x1, starting transfers between devices: 14.8 us -> 5.58 us  [spread(): return lax.all_to_all(t, AXES, 0, 0, axis_index_groups=SPREAD_GROUPS)]
    unnamed x13 -> x22, local copies, waits for them, and re-layouts: 7.07 us -> 14.5 us
    all_to_all x2 -> x1, waiting for transfers between devices: 5.37 us -> 0.01 us  [spread(): return lax.all_to_all(t, AXES, 0, 0, axis_index_groups=SPREAD_GROUPS)]
    ppermute x13 -> x10, starting transfers between devices: 12.3 us -> 9.43 us  [send(): return lax.ppermute(t, AXES, perm)]
    pallas_call x3 -> x4, Pallas kernels: 62.6 us -> 62.1 us  [attend(): pl.pallas_call(functools.partial(attend_kernel, n_kv=len(kvs), first=firs...]
  transfers between devices with their start and end apart: 15 -> 11, of which waited for: 5 -> 3; matrix products, arithmetic and copies ran while one was open for 2% -> 1% of each run, Pallas kernels for 21% -> 31%
where the time goes in v3:
time: 155 us; the launch traced here: 153 us
  Pallas kernels  64.8 us (42%)
  blocking collectives  45.8 us (30%)
  local copies, waits for them, and re-layouts  16.2 us (10%)
  starting transfers between devices  15 us (10%)
  waiting for transfers between devices  10.5 us (7%)
    pallas_call x4, Pallas kernels, attend(): pl.pallas_call(functools.partial(attend_kernel, n_kv=len(kvs), first=firs...  62.1 us
    all_to_all x2, blocking collectives, spread(): return lax.all_to_all(t, AXES, 0, 0, axis_index_groups=SPREAD_GROUPS)  45.8 us
    unnamed x22, local copies, waits for them, and re-layouts  14.5 us
    ppermute x10, waiting for transfers between devices, send(): return lax.ppermute(t, AXES, perm)  10.5 us
    ppermute x10, starting transfers between devices, send(): return lax.ppermute(t, AXES, perm)  9.43 us
    all_to_all x1, starting transfers between devices, spread(): return lax.all_to_all(t, AXES, 0, 0, axis_index_groups=SPREAD_GROUPS)  5.58 us
  transfers between devices with their start and end apart: 11, of which 3 were waited for; matrix products, arithmetic and copies ran while one was open for 1% of the time, Pallas kernels for 31%

profile of v3, /device:TPU:24, one launch (start us, length us, event | category | flops | bytes accessed | tf_op | source)
XLA Modules:
  0.0 152.9 jit_solution(6266139848949087285)
XLA Ops:
  0.0 1.2 copy-done
  1.2 0.9 copy-done.1
  3.7 1.7 %pack.1 = bf16[8,4,16,1280]{3,2,1,0:T(8,128)(2,1)S(1)} custom-call(bf16[128,4096]{1,0:T(8,128)(2,1)S(1)} %copy-done, bf16[128,512]{1,0:T(8,128)(2,1)S(1)} %copy-done.1, bf16[128,512]{1,0:T(8,128)(2,1)S(1)} %copy-done.2, s32[3,128]{1,0:T(4,128)S(1)} %copy-done.3), custom_call_target="tpu_custom_call" | custom-call | tf_op jit(solution)/shard_map/pack/pallas_call | solution.py:126
  5.4 27.8 %all_to_all.15 = bf16[32,16,1280]{2,1,0:T(8,128)(2,1)S(1)} all-to-all(bf16[32,16,1280]{2,1,0:T(8,128)(2,1)S(1)} %bitcast.13), channel_id=1, replica_groups={{0,4,8,12,16,20,24,28,32,36,40,44,48,52,56,60,64,68,72,76,80,84,88,92,9..., dimensions={0} | all-to-all | bytes 2621440 | tf_op jit(solution)/shard_map/all_to_all | solution.py:353
  33.2 2.0 %collective-permute-start = (bf16[16,32,256]{2,1,0:T(8,128)(2,1)S(1)}, bf16[16,32,256]{2,1,0:T(8,128)(2,1)S(1)}, u32[]{:S(2)}, u32[]{:S(2)}) collective-permute-start(bf16[16,32,256]{2,1,0:T(8,128)(2,1)S(1)} %get-tuple-element.30), channel_id=1, source_target_pairs={{0,16},{1,65},{4,20},{5,69},{8,24},{9,73},{12,28},{13,77},{16,32},... | collective-permute-start | bytes 786440 | tf_op jit(solution)/shard_map/ppermute | solution.py:356
  35.3 1.9 %collective-permute-start.2 = (bf16[16,32,256]{2,1,0:T(8,128)(2,1)S(1)}, bf16[16,32,256]{2,1,0:T(8,128)(2,1)S(1)}, u32[]{:S(2)}, u32[]{:S(2)}) collective-permute-start(bf16[16,32,256]{2,1,0:T(8,128)(2,1)S(1)} %get-tuple-element.30), channel_id=1, source_target_pairs={{0,32},{1,3},{4,36},{5,7},{8,40},{9,11},{12,44},{13,15},{16,48},{1... | collective-permute-start | bytes 786440 | tf_op jit(solution)/shard_map/ppermute | solution.py:356
  37.2 2.5 %collective-permute-done = bf16[16,32,256]{2,1,0:T(8,128)(2,1)S(1)} collective-permute-done((bf16[16,32,256]{2,1,0:T(8,128)(2,1)S(1)}, bf16[16,32,256]{2,1,0:T(8,128)(2,1)S(1)}, u32[]{:S(2)}, u32[]{:S(2)}) %collective-permute-start) | collective-permute-done | bytes 262176 | tf_op jit(solution)/shard_map/ppermute | solution.py:356
  39.6 5.9 %collective-permute-done.1 = bf16[16,32,256]{2,1,0:T(8,128)(2,1)S(1)} collective-permute-done((bf16[16,32,256]{2,1,0:T(8,128)(2,1)S(1)}, bf16[16,32,256]{2,1,0:T(8,128)(2,1)S(1)}, u32[]{:S(2)}, u32[]{:S(2)}) %collective-permute-start.1) | collective-permute-done | bytes 262176 | tf_op jit(solution)/shard_map/ppermute | solution.py:356
  46.7 2.5 %collective-permute-start.4 = (bf16[4,16,32,256]{3,2,1,0:T(8,128)(2,1)S(1)}, bf16[4,16,32,256]{3,2,1,0:T(8,128)(2,1)}, u32[]{:S(2)}, u32[]{:S(2)}) collective-permute-start(bf16[4,16,32,256]{3,2,1,0:T(8,128)(2,1)S(1)} %pad_maximum_fusion.refs_1_), channel_id=1, source_target_pairs={{0,66},{1,49},{4,70},{5,53},{8,74},{9,57},{12,78},{13,61},{16,82},... | collective-permute-start | bytes 3145736 | tf_op jit(solution)/shard_map/ppermute | solution.py:356
  50.1 16.2 %attend_near.1 = (f32[16,256,128]{2,1,0:T(8,128)S(1)}, f32[16,256,256]{2,1,0:T(8,128)S(1)}) custom-call(s32[17]{0:T(128)S(1)} %pad_add_fusion.meta, bf16[16,32,1280]{2,1,0:T(8,128)(2,1)S(1)} %bitcast.17, bf16[4,16,32,256]{3,2,1,0:T(8,128)(2,1)S(1)} %pad_maximum_fusion.refs_1_, bf16[4,16,32,256]{3,2,1,0:T(8,128)(2,1)} %collective-permute-done.5.refs_2_, ...), custom_call_target="tpu_custom_call" | custom-call | flops 9126805504 | bytes 8388608 | tf_op jit(solution)/shard_map/attend_near/pallas_call | solution.py:329
  66.3 1.6 %collective-permute-start.8 = (bf16[4,16,32,256]{3,2,1,0:T(8,128)(2,1)S(1)}, bf16[4,16,32,256]{3,2,1,0:T(8,128)(2,1)}, u32[]{:S(2)}, u32[]{:S(2)}) collective-permute-start(bf16[4,16,32,256]{3,2,1,0:T(8,128)(2,1)S(1)} %pad_maximum_fusion.refs_1_), channel_id=1, source_target_pairs={{0,2},{1,33},{4,6},{5,37},{8,10},{9,41},{12,14},{13,45},{16,18},{1... | collective-permute-start | bytes 3145736 | tf_op jit(solution)/shard_map/ppermute | solution.py:356
  68.4 16.1 %attend_next.1 = (f32[16,256,128]{2,1,0:T(8,128)S(1)}, f32[16,256,256]{2,1,0:T(8,128)S(1)}) custom-call(s32[17]{0:T(128)S(1)} %pad_add_fusion.meta, bf16[16,32,1280]{2,1,0:T(8,128)(2,1)S(1)} %bitcast.18, bf16[4,16,32,256]{3,2,1,0:T(8,128)(2,1)} %collective-permute-done.3.refs_1_, ...), custom_call_target="tpu_custom_call", output_to_operand_aliasing={{0}: (5, {}), {1}: (6, {})} | custom-call | flops 9126805504 | bytes 8388608 | tf_op jit(solution)/shard_map/attend_next/pallas_call | solution.py:329
  84.5 1.9 %copy-done.4 = f32[16,256,256]{2,1,0:T(8,128)} copy-done((f32[16,256,256]{2,1,0:T(8,128)}, f32[16,256,256]{2,1,0:T(8,128)S(1)}, u32[]{:S(2)}) %copy-start.4) | copy-done | bytes 4194328
  86.4 1.3 copy-done.7
  88.6 2.1 %collective-permute-done.9.refs_4_ = bf16[4,16,32,256]{3,2,1,0:T(8,128)(2,1)S(1)} collective-permute-done((bf16[4,16,32,256]{3,2,1,0:T(8,128)(2,1)}, bf16[4,16,32,256]{3,2,1,0:T(8,128)(2,1)S(1)}, u32[]{:S(2)}, u32[]{:S(2)}) %collective-permute-start.9) | collective-permute-done | bytes 1048608 | tf_op jit(solution)/shard_map/ppermute | solution.py:356
  90.6 2.2 %copy-done.5 = f32[16,256,256]{2,1,0:T(8,128)S(1)} copy-done((f32[16,256,256]{2,1,0:T(8,128)S(1)}, f32[16,256,256]{2,1,0:T(8,128)}, u32[]{:S(2)}) %copy-start.5) | copy-done | bytes 4194328
  92.8 1.6 %copy-done.8 = f32[16,256,128]{2,1,0:T(8,128)S(1)} copy-done((f32[16,256,128]{2,1,0:T(8,128)S(1)}, f32[16,256,128]{2,1,0:T(8,128)}, u32[]{:S(2)}) %copy-start.8) | copy-done | bytes 2097176
  94.4 15.3 %attend_far.3 = bf16[16,32,512]{2,1,0:T(8,128)(2,1)} custom-call(s32[17]{0:T(128)S(1)} %pad_add_fusion.meta, bf16[16,32,1280]{2,1,0:T(8,128)(2,1)S(1)} %bitcast.19, bf16[4,16,32,256]{3,2,1,0:T(8,128)(2,1)} %collective-permute-done.6.refs_1_, bf16[4,16,32,256]{3,2,1,0:T(8,128)(2,1)} %collective-permute-done.7.refs_2_, ...), custom_call_target="tpu_custom_call" | custom-call | flops 9126805504 | bytes 8388608 | tf_op jit(solution)/shard_map/attend_far/pallas_call | solution.py:329
  109.7 5.6 %all-to-all-start.2 = ((bf16[32,16,512]{2,1,0:T(8,128)(2,1)}), bf16[32,16,512]{2,1,0:T(8,128)(2,1)S(1)}, u32[]{:S(2)}, u32[]{:S(2)}) async-start(bf16[32,16,512]{2,1,0:T(8,128)(2,1)} %bitcast.9), calls=%async_computation.2 | async-start | bytes 1048576 | tf_op jit(solution)/shard_map/all_to_all | solution.py:353
  115.3 2.2 %copy-done.6 = f32[16,256,256]{2,1,0:T(8,128)S(1)} copy-done((f32[16,256,256]{2,1,0:T(8,128)S(1)}, f32[16,256,256]{2,1,0:T(8,128)}, u32[]{:S(2)}) %copy-start.6) | copy-done | bytes 4194328
  117.5 1.6 %copy-done.9 = f32[16,256,128]{2,1,0:T(8,128)S(1)} copy-done((f32[16,256,128]{2,1,0:T(8,128)S(1)}, f32[16,256,128]{2,1,0:T(8,128)}, u32[]{:S(2)}) %copy-start.9) | copy-done | bytes 2097176
  119.1 14.6 %attend_far.2 = bf16[16,32,512]{2,1,0:T(8,128)(2,1)S(1)} custom-call(s32[17]{0:T(128)S(1)} %pad_add_fusion.meta, bf16[16,32,1280]{2,1,0:T(8,128)(2,1)S(1)} %bitcast.20, bf16[4,16,32,256]{3,2,1,0:T(8,128)(2,1)} %collective-permute-done.6.refs_1_, bf16[4,16,32,256]{3,2,1,0:T(8,128)(2,1)} %collective-permute-done.7.refs_2_, ...), custom_call_target="tpu_custom_call" | custom-call | flops 9126805504 | bytes 8388608 | tf_op jit(solution)/shard_map/attend_far/pallas_call | solution.py:329
  133.7 18.0 %all_to_all.16 = bf16[32,16,512]{2,1,0:T(8,128)(2,1)S(1)} all-to-all(bf16[32,16,512]{2,1,0:T(8,128)(2,1)S(1)} %bitcast.21), channel_id=1, replica_groups={{0,4,8,12,16,20,24,28,32,36,40,44,48,52,56,60,64,68,72,76,80,84,88,92,9..., dimensions={0} | all-to-all | bytes 1048576 | tf_op jit(solution)/shard_map/all_to_all | solution.py:353
  151.7 1.0 unpack.1
  (34 shorter events, 5.0 us)
Async XLA Ops:
  0.0 1.2 copy-start
  1.2 0.9 copy-start.1
  2.1 0.9 copy-start.2
  3.0 0.7 copy-start.3
  33.2 12.7 %copy-start.10 = (s32[16]{0:T(128)S(1)}, s32[16]{0:T(128)}, u32[]{:S(2)}) copy-start(s32[16]{0:T(128)} %param.10) | copy-start | bytes 196
  33.2 6.4 %collective-permute-start = (bf16[16,32,256]{2,1,0:T(8,128)(2,1)S(1)}, bf16[16,32,256]{2,1,0:T(8,128)(2,1)S(1)}, u32[]{:S(2)}, u32[]{:S(2)}) collective-permute-start(bf16[16,32,256]{2,1,0:T(8,128)(2,1)S(1)} %get-tuple-element.30), channel_id=1, source_target_pairs={{0,16},{1,65},{4,20},{5,69},{8,24},{9,73},{12,28},{13,77},{16,32},... | collective-permute-start | bytes 786440 | tf_op jit(solution)/shard_map/ppermute | solution.py:356
  35.2 10.4 %collective-permute-start.1 = (bf16[16,32,256]{2,1,0:T(8,128)(2,1)S(1)}, bf16[16,32,256]{2,1,0:T(8,128)(2,1)S(1)}, u32[]{:S(2)}, u32[]{:S(2)}) collective-permute-start(bf16[16,32,256]{2,1,0:T(8,128)(2,1)S(1)} %get-tuple-element.30), channel_id=1, source_target_pairs={{0,48},{1,67},{4,52},{5,71},{8,56},{9,75},{12,60},{13,79},{16,0},{... | collective-permute-start | bytes 786440 | tf_op jit(solution)/shard_map/ppermute | solution.py:356
  35.3 10.3 %collective-permute-start.2 = (bf16[16,32,256]{2,1,0:T(8,128)(2,1)S(1)}, bf16[16,32,256]{2,1,0:T(8,128)(2,1)S(1)}, u32[]{:S(2)}, u32[]{:S(2)}) collective-permute-start(bf16[16,32,256]{2,1,0:T(8,128)(2,1)S(1)} %get-tuple-element.30), channel_id=1, source_target_pairs={{0,32},{1,3},{4,36},{5,7},{8,40},{9,11},{12,44},{13,15},{16,48},{1... | collective-permute-start | bytes 786440 | tf_op jit(solution)/shard_map/ppermute | solution.py:356
  45.7 4.4 %collective-permute-start.5 = (bf16[4,16,32,256]{3,2,1,0:T(8,128)(2,1)S(1)}, bf16[4,16,32,256]{3,2,1,0:T(8,128)(2,1)}, u32[]{:S(2)}, u32[]{:S(2)}) collective-permute-start(bf16[4,16,32,256]{3,2,1,0:T(8,128)(2,1)S(1)} %pad_maximum_fusion.refs_1_), channel_id=1, source_target_pairs={{0,1},{1,0},{4,5},{5,4},{8,9},{9,8},{12,13},{13,12},{16,17},{17,16... | collective-permute-start | bytes 3145736 | tf_op jit(solution)/shard_map/ppermute | solution.py:356
  45.9 20.3 %collective-permute-start.3 = (bf16[4,16,32,256]{3,2,1,0:T(8,128)(2,1)S(1)}, bf16[4,16,32,256]{3,2,1,0:T(8,128)(2,1)}, u32[]{:S(2)}, u32[]{:S(2)}) collective-permute-start(bf16[4,16,32,256]{3,2,1,0:T(8,128)(2,1)S(1)} %pad_maximum_fusion.refs_1_), channel_id=1, source_target_pairs={{0,64},{1,17},{4,68},{5,21},{8,72},{9,25},{12,76},{13,29},{16,80},... | collective-permute-start | bytes 3145736 | tf_op jit(solution)/shard_map/ppermute | solution.py:356
  46.7 19.6 %collective-permute-start.4 = (bf16[4,16,32,256]{3,2,1,0:T(8,128)(2,1)S(1)}, bf16[4,16,32,256]{3,2,1,0:T(8,128)(2,1)}, u32[]{:S(2)}, u32[]{:S(2)}) collective-permute-start(bf16[4,16,32,256]{3,2,1,0:T(8,128)(2,1)S(1)} %pad_maximum_fusion.refs_1_), channel_id=1, source_target_pairs={{0,66},{1,49},{4,70},{5,53},{8,74},{9,57},{12,78},{13,61},{16,82},... | collective-permute-start | bytes 3145736 | tf_op jit(solution)/shard_map/ppermute | solution.py:356
  66.3 21.4 %collective-permute-start.8 = (bf16[4,16,32,256]{3,2,1,0:T(8,128)(2,1)S(1)}, bf16[4,16,32,256]{3,2,1,0:T(8,128)(2,1)}, u32[]{:S(2)}, u32[]{:S(2)}) collective-permute-start(bf16[4,16,32,256]{3,2,1,0:T(8,128)(2,1)S(1)} %pad_maximum_fusion.refs_1_), channel_id=1, source_target_pairs={{0,2},{1,33},{4,6},{5,37},{8,10},{9,41},{12,14},{13,45},{16,18},{1... | collective-permute-start | bytes 3145736 | tf_op jit(solution)/shard_map/ppermute | solution.py:356
  67.9 20.7 %collective-permute-start.6 = (bf16[4,16,32,256]{3,2,1,0:T(8,128)(2,1)}, bf16[4,16,32,256]{3,2,1,0:T(8,128)(2,1)}, u32[]{:S(2)}, u32[]{:S(2)}) collective-permute-start(bf16[4,16,32,256]{3,2,1,0:T(8,128)(2,1)} %collective-permute-done.3.refs_1_), channel_id=1, source_target_pairs={{0,1},{1,0},{4,5},{5,4},{8,9},{9,8},{12,13},{13,12},{16,17},{17,16... | collective-permute-start | bytes 3145736 | tf_op jit(solution)/shard_map/ppermute | solution.py:356
  67.9 20.7 %collective-permute-start.7 = (bf16[4,16,32,256]{3,2,1,0:T(8,128)(2,1)}, bf16[4,16,32,256]{3,2,1,0:T(8,128)(2,1)}, u32[]{:S(2)}, u32[]{:S(2)}) collective-permute-start(bf16[4,16,32,256]{3,2,1,0:T(8,128)(2,1)} %collective-permute-done.4.refs_2_), channel_id=1, source_target_pairs={{0,1},{1,0},{4,5},{5,4},{8,9},{9,8},{12,13},{13,12},{16,17},{17,16... | collective-permute-start | bytes 3145736 | tf_op jit(solution)/shard_map/ppermute | solution.py:356
  84.5 1.9 %copy-start.4 = (f32[16,256,256]{2,1,0:T(8,128)}, f32[16,256,256]{2,1,0:T(8,128)S(1)}, u32[]{:S(2)}) copy-start(f32[16,256,256]{2,1,0:T(8,128)S(1)} %get-tuple-element.28.refs_7_) | copy-start | bytes 12582916
  86.4 1.3 copy-start.7
  87.7 2.9 %collective-permute-start.9 = (bf16[4,16,32,256]{3,2,1,0:T(8,128)(2,1)}, bf16[4,16,32,256]{3,2,1,0:T(8,128)(2,1)S(1)}, u32[]{:S(2)}, u32[]{:S(2)}) collective-permute-start(bf16[4,16,32,256]{3,2,1,0:T(8,128)(2,1)} %collective-permute-done.8.refs_3_), channel_id=1, source_target_pairs={{0,1},{1,0},{4,5},{5,4},{8,9},{9,8},{12,13},{13,12},{16,17},{17,16... | collective-permute-start | bytes 3145736 | tf_op jit(solution)/shard_map/ppermute | solution.py:356
  90.6 2.2 %copy-start.5 = (f32[16,256,256]{2,1,0:T(8,128)S(1)}, f32[16,256,256]{2,1,0:T(8,128)}, u32[]{:S(2)}) copy-start(f32[16,256,256]{2,1,0:T(8,128)} %copy-done.4) | copy-start | bytes 12582916
  92.8 1.6 %copy-start.8 = (f32[16,256,128]{2,1,0:T(8,128)S(1)}, f32[16,256,128]{2,1,0:T(8,128)}, u32[]{:S(2)}) copy-start(f32[16,256,128]{2,1,0:T(8,128)} %copy-done.7) | copy-start | bytes 6291460
  109.7 23.9 %all-to-all-start.2 = ((bf16[32,16,512]{2,1,0:T(8,128)(2,1)}), bf16[32,16,512]{2,1,0:T(8,128)(2,1)S(1)}, u32[]{:S(2)}, u32[]{:S(2)}) async-start(bf16[32,16,512]{2,1,0:T(8,128)(2,1)} %bitcast.9), calls=%async_computation.2 | async-start | bytes 1048576 | tf_op jit(solution)/shard_map/all_to_all | solution.py:353
  115.3 2.2 %copy-start.6 = (f32[16,256,256]{2,1,0:T(8,128)S(1)}, f32[16,256,256]{2,1,0:T(8,128)}, u32[]{:S(2)}) copy-start(f32[16,256,256]{2,1,0:T(8,128)} %copy-done.4) | copy-start | bytes 12582916
  117.5 1.6 %copy-start.9 = (f32[16,256,128]{2,1,0:T(8,128)S(1)}, f32[16,256,128]{2,1,0:T(8,128)}, u32[]{:S(2)}) copy-start(f32[16,256,128]{2,1,0:T(8,128)} %copy-done.7) | copy-start | bytes 6291460

commit v4 on v3

v4 whole, which is shorter than its diff:
```python
import functools
import math

import jax
import jax.numpy as jnp
import numpy as np
from jax import lax
from jax.experimental import pallas as pl
from jax.experimental.pallas import tpu as pltpu
from jax.sharding import PartitionSpec as P

HD = 128
ROPE_BASE = 1000000.0
bf16 = jnp.bfloat16
f32 = jnp.float32
AXES = ("blk", "head")
NT = (((1,), (1,)), ((), ()))
NEG = -1e30
CHAINS = 4
VMEM_LIMIT = 24 * 2**20
PACK_LIMIT = 62 * 2**20


def device_id(x, y, z, core):
    return ((x % 2) * 4 + y) * 16 + z * 4 + (x // 2) * 2 + core


COORDS = [(x, y, z, c) for x in range(4) for y in range(4) for z in range(4) for c in range(2)]
SPREAD_GROUPS = [
    [device_id(xh * 2 + b // 4, b % 4, z, c) for b in range(8) for z in range(4)]
    for xh in range(2)
    for c in range(2)
]


def ring_perm(first_axis_core, shift):
    pairs = []
    for x, y, z, c in COORDS:
        if c == first_axis_core:
            target = device_id(x, (y + shift) % 4, z, c)
        else:
            target = device_id((x + shift) % 4, y, z, c)
        pairs.append((device_id(x, y, z, c), target))
    return pairs


SHIFTS = (0, -1, 1, 2)


def row_offsets(x, y, c):
    start = ((x % 4) // 2 * 2 + c) * 128 + ((x % 2) * 4 + y % 4) * 16
    return [start + half * 512 + r for half in range(2) for r in range(16)]


def line_offsets(x, y, c, shift):
    if c == 0:
        return [o for s in SHIFTS for o in row_offsets(x + shift, y + s, c)]
    return [o for s in SHIFTS for o in row_offsets(x + s, y + shift, c)]


def key_offsets(parts):
    table = np.zeros((128, 128 * len(parts)), np.int32)
    for x, y, z, c in COORDS:
        row = [o for shift, own in parts for o in line_offsets(x, y, c if own else 1 - c, shift)]
        table[device_id(x, y, z, c)] = row
    return table


KEY_OFFSETS = key_offsets(
    [(0, True), (0, False)]
    + [(-1, True), (1, True)]
    + [(-1, False), (1, False), (2, True), (2, False)]
)
SWAP = [(device_id(x, y, z, c), device_id(x, y, z, 1 - c)) for x, y, z, c in COORDS]


def rope_tables(pos_ref):
    lane = lax.broadcasted_iota(jnp.int32, (128, HD), 1) % (HD // 2)
    inverse = jnp.exp(lane.astype(f32) * (-2.0 * math.log(ROPE_BASE) / HD))
    columns = [
        jnp.transpose(jnp.broadcast_to(pos_ref[i : i + 1, :].astype(f32), (128, 128)))
        for i in range(3)
    ]
    angles = jnp.where(lane < 16, columns[0], jnp.where(lane < 40, columns[1], columns[2])) * inverse
    upper = lax.broadcasted_iota(jnp.int32, (128, HD), 1) >= HD // 2
    sin = jnp.sin(angles)
    return jnp.cos(angles), jnp.where(upper, sin, -sin)


def rotate(x, cos, sin):
    x = x.astype(f32)
    return (x * cos + pltpu.roll(x, HD // 2, 1) * sin).astype(bf16).reshape(8, 16, HD)


def pack_kv_kernel(k_hbm, v_hbm, pos_hbm, out_ref, cos_ref, sin_ref, k_ref, v_ref, pos_ref, sem):
    copies = [
        pltpu.make_async_copy(source, target, sem.at[i])
        for i, (source, target) in enumerate(((pos_hbm, pos_ref), (k_hbm, k_ref), (v_hbm, v_ref)))
    ]
    for c in copies:
        c.start()
    copies[0].wait()
    cos, sin = rope_tables(pos_ref)
    copies[1].wait()
    copies[2].wait()
    for z in range(4):
        cols = slice(z * HD, (z + 1) * HD)
        out_ref[:, z, :, :HD] = rotate(k_ref[:, cols], cos, sin)
        out_ref[:, z, :, HD:] = v_ref[:, cols].reshape(8, 16, HD)
    fold = math.log2(math.e) / math.sqrt(HD)
    cos_ref[...] = cos * fold
    sin_ref[...] = sin * fold


def pack_q_kernel(q_ref, cos_ref, sin_ref, out_ref):
    cos, sin = cos_ref[...], sin_ref[...]
    for z in range(4):
        for h in range(8):
            col = (z * 8 + h) * HD
            out_ref[:, z, :, h * HD : (h + 1) * HD] = rotate(q_ref[:, col : col + HD], cos, sin)


VMEM = pl.BlockSpec(memory_space=pltpu.VMEM)
HBM = pl.BlockSpec(memory_space=pltpu.HBM)
SMEM = pl.BlockSpec(memory_space=pltpu.SMEM)


def pack_kv(k, v, positions):
    table = jax.ShapeDtypeStruct((128, HD), f32)
    return pl.pallas_call(
        pack_kv_kernel,
        out_shape=(jax.ShapeDtypeStruct((8, 4, 16, 2 * HD), bf16), table, table),
        in_specs=[HBM] * 3,
        out_specs=(VMEM,) * 3,
        scratch_shapes=[
            pltpu.VMEM(k.shape, bf16),
            pltpu.VMEM(v.shape, bf16),
            pltpu.VMEM(positions.shape, jnp.int32),
            pltpu.SemaphoreType.DMA((3,)),
        ],
        compiler_params=pltpu.CompilerParams(vmem_limit_bytes=PACK_LIMIT),
        name="pack_kv",
    )(k, v, positions)


def pack_q(q, cos, sin):
    return pl.pallas_call(
        pack_q_kernel,
        out_shape=jax.ShapeDtypeStruct((8, 4, 16, 8 * HD), bf16),
        in_specs=[VMEM] * 3,
        out_specs=VMEM,
        compiler_params=pltpu.CompilerParams(vmem_limit_bytes=VMEM_LIMIT),
        name="pack_q",
    )(q, cos, sin)


def unpack_kernel(*refs):
    *parts, o_hbm, sem = refs
    width = parts[0].shape[3]
    copies = [
        pltpu.make_async_copy(
            part.at[:, z],
            o_hbm.at[:, :, pl.ds((z * len(parts) + i) * width, width)],
            sem.at[i, z],
        )
        for i, part in enumerate(parts)
        for z in range(4)
    ]
    for c in copies:
        c.start()
    for c in copies:
        c.wait()


def unpack(parts):
    out = pl.pallas_call(
        unpack_kernel,
        out_shape=jax.ShapeDtypeStruct((8, 16, 32 * HD), bf16),
        in_specs=[VMEM] * len(parts),
        out_specs=HBM,
        scratch_shapes=[pltpu.SemaphoreType.DMA((len(parts), 4))],
        compiler_params=pltpu.CompilerParams(vmem_limit_bytes=VMEM_LIMIT),
        name="unpack",
    )(*parts)
    return out.reshape(128, 32 * HD)


def attend_kernel(meta, *refs, n_kv, first, last):
    refs = list(refs)
    q_ref = refs.pop(0)
    kv_refs = [refs.pop(0) for _ in range(n_kv)]
    kpos_ref = refs.pop(0)
    if not first:
        del refs[:2]
    m_ref, a_ref = refs.pop(0), refs.pop(0)
    if last:
        o_ref = refs.pop(0)
    keys = sum(r.shape[0] for r in kv_refs) * 32
    per_unit = max(1, 1024 // keys)
    units = 2 if per_unit <= 2 else 1
    per_body = per_unit * units

    def query_tile(order):
        x = q_ref[meta[order]]
        return jnp.concatenate([x[:, h * HD : (h + 1) * HD] for h in range(8)], axis=0)

    def key_tile(orders):
        ks, vs = [], []
        for order in orders:
            block = meta[order]
            for r in kv_refs:
                kv = r[:, block].reshape(r.shape[0] * 32, 2 * HD)
                ks.append(kv[:, :HD])
                vs.append(kv[:, HD:])
        k = jnp.concatenate(ks, axis=0) if len(ks) > 1 else ks[0]
        v = jnp.concatenate(vs, axis=0) if len(vs) > 1 else vs[0]
        return k, jnp.concatenate([v, jnp.ones_like(v)], axis=1)

    def step(index, carry):
        base = index * CHAINS
        m_at = [m_ref.at[base + c] for c in range(CHAINS)]
        a_at = [a_ref.at[base + c] for c in range(CHAINS)]
        if first:
            for c in range(CHAINS):
                m_at[c][...] = jnp.full((256, HD), NEG, f32)
                a_at[c][...] = jnp.zeros((256, 2 * HD), f32)
        queries = [query_tile(base + c) for c in range(CHAINS)]

        def scores(c, tile, masked):
            s = lax.dot_general(queries[c], tile[0], NT, preferred_element_type=f32)
            if masked:
                row = lax.broadcasted_iota(jnp.int32, (256, HD), 0)
                device = meta[16]
                start = (device % 4) * 128 + (device // 16) * 16
                qpos = start + (row // 16 % 2) * 512 + row % 16
                allowed = jnp.tile(kpos_ref[...], (256, 1)) <= jnp.tile(qpos, (1, keys // HD))
                rest = s.shape[1] - keys
                diagonal = jnp.where(allowed, s[:, rest:], NEG)
                s = jnp.concatenate([s[:, :rest], diagonal], axis=1) if rest else diagonal
            return s

        def weigh(c, s):
            before = m_at[c][...]
            peak = jnp.maximum(before, jnp.max(s, axis=1, keepdims=True))
            p = jnp.exp2(s - jnp.tile(peak, (1, s.shape[1] // HD))).astype(bf16)
            m_at[c][...] = peak
            return p, jnp.exp2(before - peak)

        def add(c, p, factor, vext):
            o = jnp.dot(p, vext, preferred_element_type=f32)
            a_at[c][...] = a_at[c][...] * jnp.tile(factor, (1, 2)) + o

        def run(todo):
            ahead = scores(*todo[0])
            pending = None
            for i, (c, tile, _) in enumerate(todo):
                s = ahead
                if i + 1 < len(todo):
                    ahead = scores(*todo[i + 1])
                p, factor = weigh(c, s)
                if pending is not None:
                    add(*pending)
                pending = (c, p, factor, tile[1])
            add(*pending)

        def body(j, carry):
            found = [
                key_tile([j * per_body + u * per_unit + i for i in range(per_unit)])
                for u in range(units)
            ]
            run([(c, t, False) for t in found for c in range(CHAINS)])
            return carry

        lax.fori_loop(0, base // per_body, body, 0)

        todo = []
        for c in range(CHAINS):
            for begin in range(0, c + 1, per_unit):
                stop = min(begin + per_unit, c + 1)
                todo.append((c, key_tile([base + i for i in range(begin, stop)]), stop == c + 1))
        run(todo)

        if last:
            for c in range(CHAINS):
                a = a_at[c][...]
                o = (a[:, :HD] / a[:, HD:]).astype(bf16)
                block = meta[base + c]
                for h in range(8):
                    o_ref[block, :, h * HD : (h + 1) * HD] = o[h * 32 : (h + 1) * 32]
        return carry

    lax.fori_loop(0, 16 // CHAINS, step, 0)


def attend(meta, q, kvs, kpos, state, last, name):
    operands = [meta, q, *kvs, kpos]
    in_specs = [SMEM] + [VMEM] * (len(operands) - 1)
    aliases = {}
    if state is not None:
        aliases = {len(operands): 0, len(operands) + 1: 1}
        operands += list(state)
        in_specs += [VMEM, VMEM]
    work = 17 * 16 // 2 * 256 * 32 * sum(x.shape[0] for x in kvs)
    out_shape = [
        jax.ShapeDtypeStruct((16, 256, HD), f32),
        jax.ShapeDtypeStruct((16, 256, 2 * HD), f32),
    ]
    if last:
        out_shape.append(jax.ShapeDtypeStruct((16, 32, 8 * HD), bf16))
    return pl.pallas_call(
        functools.partial(attend_kernel, n_kv=len(kvs), first=state is None, last=last),
        out_shape=out_shape,
        in_specs=in_specs,
        out_specs=[VMEM] * len(out_shape),
        input_output_aliases=aliases,
        compiler_params=pltpu.CompilerParams(vmem_limit_bytes=VMEM_LIMIT),
        cost_estimate=pl.CostEstimate(
            flops=work * 1024, bytes_accessed=8 * 2**20, transcendentals=work
        ),
        name=name,
    )(*operands)


def per_device(queries, keys, values, positions, block_order):
    device = lax.axis_index(AXES).astype(jnp.int32)
    order = jnp.arange(16, dtype=jnp.int32)
    inverse = jnp.sum(jnp.where(block_order[None, :] == order[:, None], order[None, :], 0), axis=1)
    meta = jnp.concatenate([inverse.astype(jnp.int32), device[None]])
    offsets = lax.dynamic_index_in_dim(jnp.asarray(KEY_OFFSETS), device, 0, keepdims=True)
    near_at, far_at = offsets[:, :512], offsets[:, 512:]

    def spread(t):
        return lax.all_to_all(t, AXES, 0, 0, axis_index_groups=SPREAD_GROUPS)

    def send(t, perm):
        return lax.ppermute(t, AXES, perm)

    kv_send, cos, sin = pack_kv(keys, values, positions)
    own = spread(kv_send.reshape(32, 16, 2 * HD))
    own, queries = lax.optimization_barrier((own, queries))
    own = own.reshape(16, 32, 2 * HD)
    q_send = pack_q(queries, cos, sin)

    received = [send(own, ring_perm(0, s)) for s in (1, -1, 2)]
    *received, q_send = lax.optimization_barrier((*received, q_send))
    line = jnp.stack([own, *received])
    line_other = send(line, SWAP)
    line_minus, line_plus = send(line, ring_perm(1, 1)), send(line, ring_perm(1, -1))

    line, q_send = lax.optimization_barrier((line, q_send))
    q = spread(q_send.reshape(32, 16, 8 * HD)).reshape(16, 32, 8 * HD)
    q, line, line_other, line_minus, line_plus = lax.optimization_barrier(
        (q, line, line_other, line_minus, line_plus)
    )
    line_far = send(line, ring_perm(1, 2))
    minus_other, plus_other = send(line_minus, SWAP), send(line_plus, SWAP)
    near = [line, line_other, line_minus, line_plus]
    state = attend(meta, q, near, near_at, None, False, "attend_near")
    line_far, minus_other, plus_other, *state = lax.optimization_barrier(
        (line_far, minus_other, plus_other, *state)
    )
    far = [minus_other, plus_other, line_far, send(line_far, SWAP)]
    *_, mixed = attend(meta, q, far, far_at, state, True, "attend_far")
    return unpack([spread(mixed.reshape(32, 16, 8 * HD)).reshape(8, 4, 16, 8 * HD)])


def solution(mesh):
    return jax.shard_map(
        per_device,
        mesh=mesh,
        in_specs=(P(AXES, None), P(AXES, None), P(AXES, None), P(None, AXES), P()),
        out_specs=P(AXES, None),
        check_vma=False,
    )
```

time: 155 us -> 138 us (0.89)
  waiting for transfers between devices: 10.5 us -> 23 us
  local copies, waits for them, and re-layouts: 16.2 us -> 3.72 us
  Pallas kernels: 64.8 us -> 53.4 us
  blocking collectives: 45.8 us -> 39.4 us
    all_to_all x1, waiting for transfers between devices: 0.01 us -> 19.1 us  [spread(): return lax.all_to_all(t, AXES, 0, 0, axis_index_groups=SPREAD_GROUPS)]
    unnamed x22 -> x8, local copies, waits for them, and re-layouts: 14.5 us -> 2.91 us
    pallas_call x5 -> x4, Pallas kernels: 63.8 us -> 52.4 us  [the longest x2 49.1 us: attend(): pl.pallas_call(functools.partial(attend_kernel, n_kv=len(kvs), first=stat...]
    ppermute x10, waiting for transfers between devices: 10.5 us -> 3.86 us  [send(): return lax.ppermute(t, AXES, perm)]
    all_to_all x2, blocking collectives: 45.8 us -> 39.4 us  [spread(): return lax.all_to_all(t, AXES, 0, 0, axis_index_groups=SPREAD_GROUPS)]
  transfers between devices with their start and end apart: 11 -> 11, of which waited for: 3 -> 3; matrix products, arithmetic and copies ran while one was open for 1% -> 1% of each run, Pallas kernels for 31% -> 20%
where the time goes in v4:
time: 138 us; the launch traced here: 137 us
  Pallas kernels  53.4 us (39%)
  blocking collectives  39.4 us (29%)
  waiting for transfers between devices  23 us (17%)
  starting transfers between devices  16.5 us (12%)
  local copies, waits for them, and re-layouts  3.72 us (3%)
    pallas_call x2, Pallas kernels, attend(): pl.pallas_call(functools.partial(attend_kernel, n_kv=len(kvs), first=stat...  49.1 us
    all_to_all x2, blocking collectives, spread(): return lax.all_to_all(t, AXES, 0, 0, axis_index_groups=SPREAD_GROUPS)  39.4 us
    all_to_all x1, waiting for transfers between devices, spread(): return lax.all_to_all(t, AXES, 0, 0, axis_index_groups=SPREAD_GROUPS)  19.1 us
    ppermute x10, starting transfers between devices, send(): return lax.ppermute(t, AXES, perm)  10.8 us
    all_to_all x1, starting transfers between devices, spread(): return lax.all_to_all(t, AXES, 0, 0, axis_index_groups=SPREAD_GROUPS)  5.72 us
    ppermute x10, waiting for transfers between devices, send(): return lax.ppermute(t, AXES, perm)  3.86 us
    unnamed x8, local copies, waits for them, and re-layouts  2.91 us
  transfers between devices with their start and end apart: 11, of which 3 were waited for; matrix products, arithmetic and copies ran while one was open for 1% of the time, Pallas kernels for 20%

profile of v4, /device:TPU:24, one launch (start us, length us, event | category | flops | bytes accessed | tf_op | source)
XLA Modules:
  0.0 136.7 jit_solution(2754512753589354921)
XLA Ops:
  0.0 1.9 %pack_kv.1 = (bf16[8,4,16,256]{3,2,1,0:T(8,128)(2,1)}, f32[128,128]{1,0:T(8,128)}, f32[128,128]{1,0:T(8,128)}) custom-call(bf16[128,512]{1,0:T(8,128)(2,1)} %k_hbm.1, bf16[128,512]{1,0:T(8,128)(2,1)} %v_hbm.1, s32[3,128]{1,0:T(4,128)} %pos_hbm.1), custom_call_target="tpu_custom_call" | custom-call | tf_op jit(solution)/shard_map/pack_kv/pallas_call | solution.py:130
  1.9 16.7 %all_to_all.15 = bf16[32,16,256]{2,1,0:T(8,128)(2,1)S(1)} all-to-all(bf16[32,16,256]{2,1,0:T(8,128)(2,1)} %bitcast.20), channel_id=1, replica_groups={{0,4,8,12,16,20,24,28,32,36,40,44,48,52,56,60,64,68,72,76,80,84,88,92,9..., dimensions={0} | all-to-all | bytes 524288 | tf_op jit(solution)/shard_map/all_to_all | solution.py:333
  18.6 1.9 %collective-permute-start.2 = (bf16[16,32,256]{2,1,0:T(8,128)(2,1)S(1)}, bf16[16,32,256]{2,1,0:T(8,128)(2,1)S(1)}, u32[]{:S(2)}, u32[]{:S(2)}) collective-permute-start(bf16[16,32,256]{2,1,0:T(8,128)(2,1)S(1)} %bitcast.16), channel_id=1, source_target_pairs={{0,32},{1,3},{4,36},{5,7},{8,40},{9,11},{12,44},{13,15},{16,48},{1... | collective-permute-start | bytes 786440 | tf_op jit(solution)/shard_map/ppermute | solution.py:336
  20.5 0.9 collective-permute-start.1
  21.4 2.3 %collective-permute-start = (bf16[16,32,256]{2,1,0:T(8,128)(2,1)S(1)}, bf16[16,32,256]{2,1,0:T(8,128)(2,1)S(1)}, u32[]{:S(2)}, u32[]{:S(2)}) collective-permute-start(bf16[16,32,256]{2,1,0:T(8,128)(2,1)S(1)} %bitcast.18), channel_id=1, source_target_pairs={{0,16},{1,65},{4,20},{5,69},{8,24},{9,73},{12,28},{13,77},{16,32},... | collective-permute-start | bytes 786440 | tf_op jit(solution)/shard_map/ppermute | solution.py:336
  23.7 1.2 copy-done
  24.9 0.8 copy-done.1
  25.8 0.8 copy-done.2
  26.6 1.5 %pack_q.1 = bf16[8,4,16,1024]{3,2,1,0:T(8,128)(2,1)} custom-call(bf16[128,4096]{1,0:T(8,128)(2,1)S(1)} %copy-done, f32[128,128]{1,0:T(8,128)S(1)} %copy-done.1, f32[128,128]{1,0:T(8,128)S(1)} %copy-done.2), custom_call_target="tpu_custom_call" | custom-call | tf_op jit(solution)/shard_map/pack_q/pallas_call | solution.py:147
  28.1 1.2 collective-permute-done.1
  29.3 0.1 pad_maximum_fusion.refs_1_
  29.4 1.9 %collective-permute-start.5 = (bf16[4,16,32,256]{3,2,1,0:T(8,128)(2,1)S(1)}, bf16[4,16,32,256]{3,2,1,0:T(8,128)(2,1)S(1)}, u32[]{:S(2)}, u32[]{:S(2)}) collective-permute-start(bf16[4,16,32,256]{3,2,1,0:T(8,128)(2,1)S(1)} %pad_maximum_fusion.refs_1_), channel_id=1, source_target_pairs={{0,66},{1,49},{4,70},{5,53},{8,74},{9,57},{12,78},{13,61},{16,82},... | collective-permute-start | bytes 3145736 | tf_op jit(solution)/shard_map/ppermute | solution.py:336
  31.3 0.2 collective-permute-start.4
  31.5 5.7 %all-to-all-start.1 = ((bf16[32,16,1024]{2,1,0:T(8,128)(2,1)}), bf16[32,16,1024]{2,1,0:T(8,128)(2,1)S(1)}, u32[]{:S(2)}, u32[]{:S(2)}) async-start(bf16[32,16,1024]{2,1,0:T(8,128)(2,1)} %bitcast.7), calls=%async_computation.1 | async-start | bytes 2097152 | tf_op jit(solution)/shard_map/all_to_all | solution.py:333
  37.5 0.8 fusion
  38.3 19.1 %all-to-all-done.1 = bf16[32,16,1024]{2,1,0:T(8,128)(2,1)S(1)} async-done(((bf16[32,16,1024]{2,1,0:T(8,128)(2,1)}), bf16[32,16,1024]{2,1,0:T(8,128)(2,1)S(1)}, u32[]{:S(2)}, u32[]{:S(2)}) %all-to-all-start.1) | async-done | bytes 1048608 | tf_op jit(solution)/shard_map/all_to_all | solution.py:333
  57.5 2.9 %collective-permute-start.6 = (bf16[4,16,32,256]{3,2,1,0:T(8,128)(2,1)S(1)}, bf16[4,16,32,256]{3,2,1,0:T(8,128)(2,1)S(1)}, u32[]{:S(2)}, u32[]{:S(2)}) collective-permute-start(bf16[4,16,32,256]{3,2,1,0:T(8,128)(2,1)S(1)} %pad_maximum_fusion.refs_1_), channel_id=1, source_target_pairs={{0,2},{1,33},{4,6},{5,37},{8,10},{9,41},{12,14},{13,45},{16,18},{1... | collective-permute-start | bytes 3145736 | tf_op jit(solution)/shard_map/ppermute | solution.py:336
  60.3 0.5 collective-permute-start.8
  60.8 25.5 %attend_near.1 = (f32[16,256,128]{2,1,0:T(8,128)S(1)}, f32[16,256,256]{2,1,0:T(8,128)S(1)}) custom-call(s32[17]{0:T(128)S(1)} %pad_add_fusion.meta, bf16[16,32,1024]{2,1,0:T(8,128)(2,1)S(1)} %bitcast.13, bf16[4,16,32,256]{3,2,1,0:T(8,128)(2,1)S(1)} %pad_maximum_fusion.refs_1_, bf16[4,16,32,256]{3,2,1,0:T(8,128)(2,1)} %collective-permute-done.3.refs_2_, ...), custom_call_target="tpu_custom_call" | custom-call | flops 18253611008 | bytes 8388608 | tf_op jit(solution)/shard_map/attend_near/pallas_call | solution.py:310
  86.3 0.3 collective-permute-start.9
  86.6 2.6 %collective-permute-done.9.refs_4_ = bf16[4,16,32,256]{3,2,1,0:T(8,128)(2,1)S(1)} collective-permute-done((bf16[4,16,32,256]{3,2,1,0:T(8,128)(2,1)S(1)}, bf16[4,16,32,256]{3,2,1,0:T(8,128)(2,1)S(1)}, u32[]{:S(2)}, u32[]{:S(2)}) %collective-permute-start.9) | collective-permute-done | bytes 1048608 | tf_op jit(solution)/shard_map/ppermute | solution.py:336
  89.2 23.6 %attend_far.1 = (f32[16,256,128]{2,1,0:T(8,128)S(1)}, f32[16,256,256]{2,1,0:T(8,128)S(1)}, bf16[16,32,1024]{2,1,0:T(8,128)(2,1)S(1)}) custom-call(s32[17]{0:T(128)S(1)} %pad_add_fusion.meta, bf16[16,32,1024]{2,1,0:T(8,128)(2,1)S(1)} %bitcast.14, ...), custom_call_target="tpu_custom_call", output_to_operand_aliasing={{0}: (7, {}), {1}: (8, {})} | custom-call | flops 18253611008 | bytes 8388608 | tf_op jit(solution)/shard_map/attend_far/pallas_call | solution.py:310
  112.8 22.7 %all_to_all.16 = bf16[32,16,1024]{2,1,0:T(8,128)(2,1)S(1)} all-to-all(bf16[32,16,1024]{2,1,0:T(8,128)(2,1)S(1)} %bitcast.15), channel_id=1, replica_groups={{0,4,8,12,16,20,24,28,32,36,40,44,48,52,56,60,64,68,72,76,80,84,88,92,9..., dimensions={0} | all-to-all | bytes 2097152 | tf_op jit(solution)/shard_map/all_to_all | solution.py:333
  135.6 1.0 unpack.1
  (17 shorter events, 0.2 us)
Async XLA Ops:
  0.0 37.3 %copy-start.3 = (s32[16]{0:T(128)S(1)}, s32[16]{0:T(128)}, u32[]{:S(2)}) copy-start(s32[16]{0:T(128)} %param.10) | copy-start | bytes 196
  18.6 9.5 %collective-permute-start.2 = (bf16[16,32,256]{2,1,0:T(8,128)(2,1)S(1)}, bf16[16,32,256]{2,1,0:T(8,128)(2,1)S(1)}, u32[]{:S(2)}, u32[]{:S(2)}) collective-permute-start(bf16[16,32,256]{2,1,0:T(8,128)(2,1)S(1)} %bitcast.16), channel_id=1, source_target_pairs={{0,32},{1,3},{4,36},{5,7},{8,40},{9,11},{12,44},{13,15},{16,48},{1... | collective-permute-start | bytes 786440 | tf_op jit(solution)/shard_map/ppermute | solution.py:336
  20.5 8.8 %collective-permute-start.1 = (bf16[16,32,256]{2,1,0:T(8,128)(2,1)S(1)}, bf16[16,32,256]{2,1,0:T(8,128)(2,1)S(1)}, u32[]{:S(2)}, u32[]{:S(2)}) collective-permute-start(bf16[16,32,256]{2,1,0:T(8,128)(2,1)S(1)} %bitcast.17), channel_id=1, source_target_pairs={{0,48},{1,67},{4,52},{5,71},{8,56},{9,75},{12,60},{13,79},{16,0},{... | collective-permute-start | bytes 786440 | tf_op jit(solution)/shard_map/ppermute | solution.py:336
  21.4 7.9 %collective-permute-start = (bf16[16,32,256]{2,1,0:T(8,128)(2,1)S(1)}, bf16[16,32,256]{2,1,0:T(8,128)(2,1)S(1)}, u32[]{:S(2)}, u32[]{:S(2)}) collective-permute-start(bf16[16,32,256]{2,1,0:T(8,128)(2,1)S(1)} %bitcast.18), channel_id=1, source_target_pairs={{0,16},{1,65},{4,20},{5,69},{8,24},{9,73},{12,28},{13,77},{16,32},... | collective-permute-start | bytes 786440 | tf_op jit(solution)/shard_map/ppermute | solution.py:336
  23.7 1.2 copy-start
  24.9 0.8 copy-start.1
  25.8 0.8 copy-start.2
  29.4 28.0 %collective-permute-start.5 = (bf16[4,16,32,256]{3,2,1,0:T(8,128)(2,1)S(1)}, bf16[4,16,32,256]{3,2,1,0:T(8,128)(2,1)S(1)}, u32[]{:S(2)}, u32[]{:S(2)}) collective-permute-start(bf16[4,16,32,256]{3,2,1,0:T(8,128)(2,1)S(1)} %pad_maximum_fusion.refs_1_), channel_id=1, source_target_pairs={{0,66},{1,49},{4,70},{5,53},{8,74},{9,57},{12,78},{13,61},{16,82},... | collective-permute-start | bytes 3145736 | tf_op jit(solution)/shard_map/ppermute | solution.py:336
  31.3 26.1 %collective-permute-start.4 = (bf16[4,16,32,256]{3,2,1,0:T(8,128)(2,1)S(1)}, bf16[4,16,32,256]{3,2,1,0:T(8,128)(2,1)}, u32[]{:S(2)}, u32[]{:S(2)}) collective-permute-start(bf16[4,16,32,256]{3,2,1,0:T(8,128)(2,1)S(1)} %pad_maximum_fusion.refs_1_), channel_id=1, source_target_pairs={{0,64},{1,17},{4,68},{5,21},{8,72},{9,25},{12,76},{13,29},{16,80},... | collective-permute-start | bytes 3145736 | tf_op jit(solution)/shard_map/ppermute | solution.py:336
  31.5 25.9 %collective-permute-start.3 = (bf16[4,16,32,256]{3,2,1,0:T(8,128)(2,1)S(1)}, bf16[4,16,32,256]{3,2,1,0:T(8,128)(2,1)}, u32[]{:S(2)}, u32[]{:S(2)}) collective-permute-start(bf16[4,16,32,256]{3,2,1,0:T(8,128)(2,1)S(1)} %pad_maximum_fusion.refs_1_), channel_id=1, source_target_pairs={{0,1},{1,0},{4,5},{5,4},{8,9},{9,8},{12,13},{13,12},{16,17},{17,16... | collective-permute-start | bytes 3145736 | tf_op jit(solution)/shard_map/ppermute | solution.py:336
  31.5 25.9 %all-to-all-start.1 = ((bf16[32,16,1024]{2,1,0:T(8,128)(2,1)}), bf16[32,16,1024]{2,1,0:T(8,128)(2,1)S(1)}, u32[]{:S(2)}, u32[]{:S(2)}) async-start(bf16[32,16,1024]{2,1,0:T(8,128)(2,1)} %bitcast.7), calls=%async_computation.1 | async-start | bytes 2097152 | tf_op jit(solution)/shard_map/all_to_all | solution.py:333
  57.5 28.8 %collective-permute-start.6 = (bf16[4,16,32,256]{3,2,1,0:T(8,128)(2,1)S(1)}, bf16[4,16,32,256]{3,2,1,0:T(8,128)(2,1)S(1)}, u32[]{:S(2)}, u32[]{:S(2)}) collective-permute-start(bf16[4,16,32,256]{3,2,1,0:T(8,128)(2,1)S(1)} %pad_maximum_fusion.refs_1_), channel_id=1, source_target_pairs={{0,2},{1,33},{4,6},{5,37},{8,10},{9,41},{12,14},{13,45},{16,18},{1... | collective-permute-start | bytes 3145736 | tf_op jit(solution)/shard_map/ppermute | solution.py:336
  60.3 26.0 %collective-permute-start.7 = (bf16[4,16,32,256]{3,2,1,0:T(8,128)(2,1)}, bf16[4,16,32,256]{3,2,1,0:T(8,128)(2,1)S(1)}, u32[]{:S(2)}, u32[]{:S(2)}) collective-permute-start(bf16[4,16,32,256]{3,2,1,0:T(8,128)(2,1)} %collective-permute-done.4.refs_3_), channel_id=1, source_target_pairs={{0,1},{1,0},{4,5},{5,4},{8,9},{9,8},{12,13},{13,12},{16,17},{17,16... | collective-permute-start | bytes 3145736 | tf_op jit(solution)/shard_map/ppermute | solution.py:336
  60.3 26.0 %collective-permute-start.8 = (bf16[4,16,32,256]{3,2,1,0:T(8,128)(2,1)S(1)}, bf16[4,16,32,256]{3,2,1,0:T(8,128)(2,1)S(1)}, u32[]{:S(2)}, u32[]{:S(2)}) collective-permute-start(bf16[4,16,32,256]{3,2,1,0:T(8,128)(2,1)S(1)} %collective-permute-done.5.refs_4_), channel_id=1, source_target_pairs={{0,1},{1,0},{4,5},{5,4},{8,9},{9,8},{12,13},{13,12},{16,17},{17,16... | collective-permute-start | bytes 3145736 | tf_op jit(solution)/shard_map/ppermute | solution.py:336
  86.3 2.9 %collective-permute-start.9 = (bf16[4,16,32,256]{3,2,1,0:T(8,128)(2,1)S(1)}, bf16[4,16,32,256]{3,2,1,0:T(8,128)(2,1)S(1)}, u32[]{:S(2)}, u32[]{:S(2)}) collective-permute-start(bf16[4,16,32,256]{3,2,1,0:T(8,128)(2,1)S(1)} %collective-permute-done.6.refs_3_), channel_id=1, source_target_pairs={{0,1},{1,0},{4,5},{5,4},{8,9},{9,8},{12,13},{13,12},{16,17},{17,16... | collective-permute-start | bytes 3145736 | tf_op jit(solution)/shard_map/ppermute | solution.py:336

commit v5 on v4

--- a/solution.py
+++ b/solution.py
@@ -16,8 +16,7 @@
 AXES = ("blk", "head")
 NT = (((1,), (1,)), ((), ()))
 NEG = -1e30
-CHAINS = 4
-VMEM_LIMIT = 24 * 2**20
+VMEM_LIMIT = 12 * 2**20
 PACK_LIMIT = 62 * 2**20
 
 
@@ -92,11 +91,12 @@
     return (x * cos + pltpu.roll(x, HD // 2, 1) * sin).astype(bf16).reshape(8, 16, HD)
 
 
-def pack_kv_kernel(k_hbm, v_hbm, pos_hbm, out_ref, cos_ref, sin_ref, k_ref, v_ref, pos_ref, sem):
-    copies = [
-        pltpu.make_async_copy(source, target, sem.at[i])
-        for i, (source, target) in enumerate(((pos_hbm, pos_ref), (k_hbm, k_ref), (v_hbm, v_ref)))
-    ]
+def pack_kernel(k_hbm, v_hbm, pos_hbm, q_hbm, kv_out, q_out, k_ref, v_ref, pos_ref, q_ref, sem):
+    sources = [(pos_hbm, pos_ref), (k_hbm, k_ref), (v_hbm, v_ref)]
+    for z in range(4):
+        cols = pl.ds(z * 8 * HD, 8 * HD)
+        sources.append((q_hbm.at[:, cols], q_ref.at[:, cols]))
+    copies = [pltpu.make_async_copy(*pair, sem.at[i]) for i, pair in enumerate(sources)]
     for c in copies:
         c.start()
     copies[0].wait()
@@ -105,19 +105,15 @@
     copies[2].wait()
     for z in range(4):
         cols = slice(z * HD, (z + 1) * HD)
-        out_ref[:, z, :, :HD] = rotate(k_ref[:, cols], cos, sin)
-        out_ref[:, z, :, HD:] = v_ref[:, cols].reshape(8, 16, HD)
+        kv_out[:, z, :, :HD] = rotate(k_ref[:, cols], cos, sin)
+        kv_out[:, z, :, HD:] = v_ref[:, cols].reshape(8, 16, HD)
     fold = math.log2(math.e) / math.sqrt(HD)
-    cos_ref[...] = cos * fold
-    sin_ref[...] = sin * fold
-
-
-def pack_q_kernel(q_ref, cos_ref, sin_ref, out_ref):
-    cos, sin = cos_ref[...], sin_ref[...]
+    cos, sin = cos * fold, sin * fold
     for z in range(4):
+        copies[3 + z].wait()
         for h in range(8):
             col = (z * 8 + h) * HD
-            out_ref[:, z, :, h * HD : (h + 1) * HD] = rotate(q_ref[:, col : col + HD], cos, sin)
+            q_out[:, z, :, h * HD : (h + 1) * HD] = rotate(q_ref[:, col : col + HD], cos, sin)
 
 
 VMEM = pl.BlockSpec(memory_space=pltpu.VMEM)
@@ -125,33 +121,25 @@
 SMEM = pl.BlockSpec(memory_space=pltpu.SMEM)
 
 
-def pack_kv(k, v, positions):
-    table = jax.ShapeDtypeStruct((128, HD), f32)
+def pack(k, v, positions, q):
     return pl.pallas_call(
-        pack_kv_kernel,
-        out_shape=(jax.ShapeDtypeStruct((8, 4, 16, 2 * HD), bf16), table, table),
-        in_specs=[HBM] * 3,
-        out_specs=(VMEM,) * 3,
+        pack_kernel,
+        out_shape=(
+            jax.ShapeDtypeStruct((8, 4, 16, 2 * HD), bf16),
+            jax.ShapeDtypeStruct((8, 4, 16, 8 * HD), bf16),
+        ),
+        in_specs=[HBM] * 4,
+        out_specs=(VMEM, VMEM),
         scratch_shapes=[
             pltpu.VMEM(k.shape, bf16),
             pltpu.VMEM(v.shape, bf16),
             pltpu.VMEM(positions.shape, jnp.int32),
-            pltpu.SemaphoreType.DMA((3,)),
+            pltpu.VMEM(q.shape, bf16),
+            pltpu.SemaphoreType.DMA((7,)),
         ],
         compiler_params=pltpu.CompilerParams(vmem_limit_bytes=PACK_LIMIT),
-        name="pack_kv",
-    )(k, v, positions)
-
-
-def pack_q(q, cos, sin):
-    return pl.pallas_call(
-        pack_q_kernel,
-        out_shape=jax.ShapeDtypeStruct((8, 4, 16, 8 * HD), bf16),
-        in_specs=[VMEM] * 3,
-        out_specs=VMEM,
-        compiler_params=pltpu.CompilerParams(vmem_limit_bytes=VMEM_LIMIT),
-        name="pack_q",
-    )(q, cos, sin)
+        name="pack",
+    )(k, v, positions, q)
 
 
 def unpack_kernel(*refs):
@@ -185,7 +173,7 @@
     return out.reshape(128, 32 * HD)
 
 
-def attend_kernel(meta, *refs, n_kv, first, last):
+def attend_kernel(meta, *refs, n_kv, offset_at, chains, first, last):
     refs = list(refs)
     q_ref = refs.pop(0)
     kv_refs = [refs.pop(0) for _ in range(n_kv)]
@@ -217,14 +205,14 @@
         return k, jnp.concatenate([v, jnp.ones_like(v)], axis=1)
 
     def step(index, carry):
-        base = index * CHAINS
-        m_at = [m_ref.at[base + c] for c in range(CHAINS)]
-        a_at = [a_ref.at[base + c] for c in range(CHAINS)]
+        base = index * chains
+        m_at = [m_ref.at[base + c] for c in range(chains)]
+        a_at = [a_ref.at[base + c] for c in range(chains)]
         if first:
-            for c in range(CHAINS):
+            for c in range(chains):
                 m_at[c][...] = jnp.full((256, HD), NEG, f32)
                 a_at[c][...] = jnp.zeros((256, 2 * HD), f32)
-        queries = [query_tile(base + c) for c in range(CHAINS)]
+        queries = [query_tile(base + c) for c in range(chains)]
 
         def scores(c, tile, masked):
             s = lax.dot_general(queries[c], tile[0], NT, preferred_element_type=f32)
@@ -232,8 +220,9 @@
                 row = lax.broadcasted_iota(jnp.int32, (256, HD), 0)
                 device = meta[16]
                 start = (device % 4) * 128 + (device // 16) * 16
+                kpos = kpos_ref[:, offset_at : offset_at + keys]
                 qpos = start + (row // 16 % 2) * 512 + row % 16
-                allowed = jnp.tile(kpos_ref[...], (256, 1)) <= jnp.tile(qpos, (1, keys // HD))
+                allowed = jnp.tile(kpos, (256, 1)) <= jnp.tile(qpos, (1, keys // HD))
                 rest = s.shape[1] - keys
                 diagonal = jnp.where(allowed, s[:, rest:], NEG)
                 s = jnp.concatenate([s[:, :rest], diagonal], axis=1) if rest else diagonal
@@ -268,20 +257,20 @@
                 key_tile([j * per_body + u * per_unit + i for i in range(per_unit)])
                 for u in range(units)
             ]
-            run([(c, t, False) for t in found for c in range(CHAINS)])
+            run([(c, t, False) for t in found for c in range(chains)])
             return carry
 
         lax.fori_loop(0, base // per_body, body, 0)
 
         todo = []
-        for c in range(CHAINS):
+        for c in range(chains):
             for begin in range(0, c + 1, per_unit):
                 stop = min(begin + per_unit, c + 1)
                 todo.append((c, key_tile([base + i for i in range(begin, stop)]), stop == c + 1))
         run(todo)
 
         if last:
-            for c in range(CHAINS):
+            for c in range(chains):
                 a = a_at[c][...]
                 o = (a[:, :HD] / a[:, HD:]).astype(bf16)
                 block = meta[base + c]
@@ -289,11 +278,11 @@
                     o_ref[block, :, h * HD : (h + 1) * HD] = o[h * 32 : (h + 1) * 32]
         return carry
 
-    lax.fori_loop(0, 16 // CHAINS, step, 0)
-
-
-def attend(meta, q, kvs, kpos, state, last, name):
-    operands = [meta, q, *kvs, kpos]
+    lax.fori_loop(0, 16 // chains, step, 0)
+
+
+def attend(meta, q, kvs, offsets, offset_at, state, last, chains, name):
+    operands = [meta, q, *kvs, offsets]
     in_specs = [SMEM] + [VMEM] * (len(operands) - 1)
     aliases = {}
     if state is not None:
@@ -308,7 +297,14 @@
     if last:
         out_shape.append(jax.ShapeDtypeStruct((16, 32, 8 * HD), bf16))
     return pl.pallas_call(
-        functools.partial(attend_kernel, n_kv=len(kvs), first=state is None, last=last),
+        functools.partial(
+            attend_kernel,
+            n_kv=len(kvs),
+            offset_at=offset_at,
+            chains=chains,
+            first=state is None,
+            last=last,
+        ),
         out_shape=out_shape,
         in_specs=in_specs,
         out_specs=[VMEM] * len(out_shape),
@@ -327,7 +323,6 @@
     inverse = jnp.sum(jnp.where(block_order[None, :] == order[:, None], order[None, :], 0), axis=1)
     meta = jnp.concatenate([inverse.astype(jnp.int32), device[None]])
     offsets = lax.dynamic_index_in_dim(jnp.asarray(KEY_OFFSETS), device, 0, keepdims=True)
-    near_at, far_at = offsets[:, :512], offsets[:, 512:]
 
     def spread(t):
         return lax.all_to_all(t, AXES, 0, 0, axis_index_groups=SPREAD_GROUPS)
@@ -335,32 +330,28 @@
     def send(t, perm):
         return lax.ppermute(t, AXES, perm)
 
-    kv_send, cos, sin = pack_kv(keys, values, positions)
-    own = spread(kv_send.reshape(32, 16, 2 * HD))
-    own, queries = lax.optimization_barrier((own, queries))
+    kv_send, q_send = pack(keys, values, positions, queries)
+    own, q_send = lax.optimization_barrier((spread(kv_send.reshape(32, 16, 2 * HD)), q_send))
     own = own.reshape(16, 32, 2 * HD)
-    q_send = pack_q(queries, cos, sin)
+    q = spread(q_send.reshape(32, 16, 8 * HD)).reshape(16, 32, 8 * HD)
 
     received = [send(own, ring_perm(0, s)) for s in (1, -1, 2)]
-    *received, q_send = lax.optimization_barrier((*received, q_send))
+    *received, q = lax.optimization_barrier((*received, q))
     line = jnp.stack([own, *received])
     line_other = send(line, SWAP)
     line_minus, line_plus = send(line, ring_perm(1, 1)), send(line, ring_perm(1, -1))
-
-    line, q_send = lax.optimization_barrier((line, q_send))
-    q = spread(q_send.reshape(32, 16, 8 * HD)).reshape(16, 32, 8 * HD)
-    q, line, line_other, line_minus, line_plus = lax.optimization_barrier(
-        (q, line, line_other, line_minus, line_plus)
+    state = attend(meta, q, [line, line_other], offsets, 0, None, False, 8, "attend_near")
+    line, line_minus, line_plus, *state = lax.optimization_barrier(
+        (line, line_minus, line_plus, *state)
     )
     line_far = send(line, ring_perm(1, 2))
     minus_other, plus_other = send(line_minus, SWAP), send(line_plus, SWAP)
-    near = [line, line_other, line_minus, line_plus]
-    state = attend(meta, q, near, near_at, None, False, "attend_near")
+    state = attend(meta, q, [line_minus, line_plus], offsets, 256, state, False, 8, "attend_next")
     line_far, minus_other, plus_other, *state = lax.optimization_barrier(
         (line_far, minus_other, plus_other, *state)
     )
     far = [minus_other, plus_other, line_far, send(line_far, SWAP)]
-    *_, mixed = attend(meta, q, far, far_at, state, True, "attend_far")
+    *_, mixed = attend(meta, q, far, offsets, 512, state, True, 8, "attend_far")
     return unpack([spread(mixed.reshape(32, 16, 8 * HD)).reshape(8, 4, 16, 8 * HD)])
 
 

time: 138 us -> 132 us (0.957)
  waiting for transfers between devices: 23 us -> 18.8 us
  local copies, waits for them, and re-layouts: 3.72 us -> 0.77 us
  Pallas kernels: 53.4 us -> 56.2 us
  starting transfers between devices: 16.5 us -> 14.2 us
    all_to_all x1, waiting for transfers between devices: 19.1 us -> 0.01 us  [spread(): return lax.all_to_all(t, AXES, 0, 0, axis_index_groups=SPREAD_GROUPS)]
    ppermute x10, waiting for transfers between devices: 3.86 us -> 18.8 us  [send(): return lax.ppermute(t, AXES, perm)]
    unnamed x8 -> x2, local copies, waits for them, and re-layouts: 2.91 us -> 0.01 us
    pallas_call x4, Pallas kernels: 52.4 us -> 55.2 us  [the longest x3 52.3 us: attend(): pl.pallas_call(functools.partial(attend_kernel, n_kv=len(kvs), offset_at=...]
    ppermute x10, starting transfers between devices: 10.8 us -> 8.6 us  [send(): return lax.ppermute(t, AXES, perm)]
  transfers between devices with their start and end apart: 11 -> 11, of which waited for: 3 -> 6; matrix products, arithmetic and copies ran while one was open for 1% -> 1% of each run, Pallas kernels for 20% -> 21%
where the time goes in v5:
time: 132 us; the launch traced here: 130 us
  Pallas kernels  56.2 us (43%)
  blocking collectives  40 us (30%)
  waiting for transfers between devices  18.8 us (14%)
  starting transfers between devices  14.2 us (11%)
    pallas_call x3, Pallas kernels, attend(): pl.pallas_call(functools.partial(attend_kernel, n_kv=len(kvs), offset_at=...  52.3 us
    all_to_all x2, blocking collectives, spread(): return lax.all_to_all(t, AXES, 0, 0, axis_index_groups=SPREAD_GROUPS)  40 us
    ppermute x10, waiting for transfers between devices, send(): return lax.ppermute(t, AXES, perm)  18.8 us
    ppermute x10, starting transfers between devices, send(): return lax.ppermute(t, AXES, perm)  8.6 us
    all_to_all x1, starting transfers between devices, spread(): return lax.all_to_all(t, AXES, 0, 0, axis_index_groups=SPREAD_GROUPS)  5.58 us
    pallas_call x1, Pallas kernels, pack(): pl.pallas_call(pack_kernel, out_shape=(jax.ShapeDtypeStruct((8, 4, 16, 2...  2.98 us
  transfers between devices with their start and end apart: 11, of which 6 were waited for; matrix products, arithmetic and copies ran while one was open for 1% of the time, Pallas kernels for 21%

profile of v5, /device:TPU:24, one launch (start us, length us, event | category | flops | bytes accessed | tf_op | source)
XLA Modules:
  0.0 130.5 jit_solution(12506130859800389984)
XLA Ops:
  0.0 3.0 %pack.1 = (bf16[8,4,16,256]{3,2,1,0:T(8,128)(2,1)}, bf16[8,4,16,1024]{3,2,1,0:T(8,128)(2,1)}) custom-call(bf16[128,512]{1,0:T(8,128)(2,1)} %k_hbm.1, bf16[128,512]{1,0:T(8,128)(2,1)} %v_hbm.1, s32[3,128]{1,0:T(4,128)} %pos_hbm.1, bf16[128,4096]{1,0:T(8,128)(2,1)} %q_hbm.1), custom_call_target="tpu_custom_call" | custom-call | tf_op jit(solution)/shard_map/pack/pallas_call | solution.py:125
  3.0 16.7 %all_to_all.15 = bf16[32,16,256]{2,1,0:T(8,128)(2,1)S(1)} all-to-all(bf16[32,16,256]{2,1,0:T(8,128)(2,1)} %bitcast.22), channel_id=1, replica_groups={{0,4,8,12,16,20,24,28,32,36,40,44,48,52,56,60,64,68,72,76,80,84,88,92,9..., dimensions={0} | all-to-all | bytes 524288 | tf_op jit(solution)/shard_map/all_to_all | solution.py:328
  19.7 5.6 %all-to-all-start.1 = ((bf16[32,16,1024]{2,1,0:T(8,128)(2,1)}), bf16[32,16,1024]{2,1,0:T(8,128)(2,1)S(1)}, u32[]{:S(2)}, u32[]{:S(2)}) async-start(bf16[32,16,1024]{2,1,0:T(8,128)(2,1)} %bitcast.17), calls=%async_computation.1 | async-start | bytes 2097152 | tf_op jit(solution)/shard_map/all_to_all | solution.py:328
  25.3 1.5 %collective-permute-start.2 = (bf16[16,32,256]{2,1,0:T(8,128)(2,1)S(1)}, bf16[16,32,256]{2,1,0:T(8,128)(2,1)S(1)}, u32[]{:S(2)}, u32[]{:S(2)}) collective-permute-start(bf16[16,32,256]{2,1,0:T(8,128)(2,1)S(1)} %bitcast.18), channel_id=1, source_target_pairs={{0,32},{1,3},{4,36},{5,7},{8,40},{9,11},{12,44},{13,15},{16,48},{1... | collective-permute-start | bytes 786440 | tf_op jit(solution)/shard_map/ppermute | solution.py:331
  26.8 3.2 %collective-permute-start = (bf16[16,32,256]{2,1,0:T(8,128)(2,1)S(1)}, bf16[16,32,256]{2,1,0:T(8,128)(2,1)S(1)}, u32[]{:S(2)}, u32[]{:S(2)}) collective-permute-start(bf16[16,32,256]{2,1,0:T(8,128)(2,1)S(1)} %bitcast.20), channel_id=1, source_target_pairs={{0,16},{1,65},{4,20},{5,69},{8,24},{9,73},{12,28},{13,77},{16,32},... | collective-permute-start | bytes 786440 | tf_op jit(solution)/shard_map/ppermute | solution.py:331
  30.0 10.1 %collective-permute-done.2 = bf16[16,32,256]{2,1,0:T(8,128)(2,1)S(1)} collective-permute-done((bf16[16,32,256]{2,1,0:T(8,128)(2,1)S(1)}, bf16[16,32,256]{2,1,0:T(8,128)(2,1)S(1)}, u32[]{:S(2)}, u32[]{:S(2)}) %collective-permute-start.2) | collective-permute-done | bytes 262176 | tf_op jit(solution)/shard_map/ppermute | solution.py:331
  40.2 1.7 %collective-permute-done.1 = bf16[16,32,256]{2,1,0:T(8,128)(2,1)S(1)} collective-permute-done((bf16[16,32,256]{2,1,0:T(8,128)(2,1)S(1)}, bf16[16,32,256]{2,1,0:T(8,128)(2,1)S(1)}, u32[]{:S(2)}, u32[]{:S(2)}) %collective-permute-start.1) | collective-permute-done | bytes 262176 | tf_op jit(solution)/shard_map/ppermute | solution.py:331
  41.8 0.6 collective-permute-done
  42.5 0.1 pad_maximum_fusion.refs_1_
  42.6 0.4 collective-permute-start.5
  43.0 0.1 select_reduce_fusion
  43.1 2.5 %collective-permute-start.4 = (bf16[4,16,32,256]{3,2,1,0:T(8,128)(2,1)S(1)}, bf16[4,16,32,256]{3,2,1,0:T(8,128)(2,1)S(1)}, u32[]{:S(2)}, u32[]{:S(2)}) collective-permute-start(bf16[4,16,32,256]{3,2,1,0:T(8,128)(2,1)S(1)} %pad_maximum_fusion.refs_1_), channel_id=1, source_target_pairs={{0,66},{1,49},{4,70},{5,53},{8,74},{9,57},{12,78},{13,61},{16,82},... | collective-permute-start | bytes 3145736 | tf_op jit(solution)/shard_map/ppermute | solution.py:331
  45.6 0.1 pad_add_fusion.meta
  45.6 0.8 constant_dynamic-slice_fusion.refs_3_.refs_5_
  46.4 13.2 %attend_near.1 = (f32[16,256,128]{2,1,0:T(8,128)S(1)}, f32[16,256,256]{2,1,0:T(8,128)S(1)}) custom-call(s32[17]{0:T(128)S(1)} %pad_add_fusion.meta, bf16[16,32,1024]{2,1,0:T(8,128)(2,1)S(1)} %bitcast.13, bf16[4,16,32,256]{3,2,1,0:T(8,128)(2,1)S(1)} %pad_maximum_fusion.refs_1_, bf16[4,16,32,256]{3,2,1,0:T(8,128)(2,1)S(1)} %collective-permute-done.5.refs_2_, ...), custom_call_target="tpu_custom_call" | custom-call | flops 9126805504 | bytes 8388608 | tf_op jit(solution)/shard_map/attend_near/pallas_call | solution.py:299
  59.7 1.9 %collective-permute-done.3.refs_1_ = bf16[4,16,32,256]{3,2,1,0:T(8,128)(2,1)S(1)} collective-permute-done((bf16[4,16,32,256]{3,2,1,0:T(8,128)(2,1)S(1)}, bf16[4,16,32,256]{3,2,1,0:T(8,128)(2,1)S(1)}, u32[]{:S(2)}, u32[]{:S(2)}) %collective-permute-start.3) | collective-permute-done | bytes 1048608 | tf_op jit(solution)/shard_map/ppermute | solution.py:331
  61.6 0.5 collective-permute-start.6
  62.1 0.5 collective-permute-start.8
  62.6 13.5 %attend_next.1 = (f32[16,256,128]{2,1,0:T(8,128)S(1)}, f32[16,256,256]{2,1,0:T(8,128)S(1)}) custom-call(s32[17]{0:T(128)S(1)} %pad_add_fusion.meta, bf16[16,32,1024]{2,1,0:T(8,128)(2,1)S(1)} %bitcast.14, bf16[4,16,32,256]{3,2,1,0:T(8,128)(2,1)S(1)} %collective-permute-done.3.refs_1_, ...), custom_call_target="tpu_custom_call", output_to_operand_aliasing={{0}: (5, {}), {1}: (6, {})} | custom-call | flops 9126805504 | bytes 8388608 | tf_op jit(solution)/shard_map/attend_next/pallas_call | solution.py:299
  76.1 1.7 %collective-permute-done.6.refs_3_ = bf16[4,16,32,256]{3,2,1,0:T(8,128)(2,1)S(1)} collective-permute-done((bf16[4,16,32,256]{3,2,1,0:T(8,128)(2,1)S(1)}, bf16[4,16,32,256]{3,2,1,0:T(8,128)(2,1)S(1)}, u32[]{:S(2)}, u32[]{:S(2)}) %collective-permute-start.6) | collective-permute-done | bytes 1048608 | tf_op jit(solution)/shard_map/ppermute | solution.py:331
  77.9 2.7 %collective-permute-done.9.refs_4_ = bf16[4,16,32,256]{3,2,1,0:T(8,128)(2,1)S(1)} collective-permute-done((bf16[4,16,32,256]{3,2,1,0:T(8,128)(2,1)S(1)}, bf16[4,16,32,256]{3,2,1,0:T(8,128)(2,1)S(1)}, u32[]{:S(2)}, u32[]{:S(2)}) %collective-permute-start.9) | collective-permute-done | bytes 1048608 | tf_op jit(solution)/shard_map/ppermute | solution.py:331
  80.6 25.5 %attend_far.1 = (f32[16,256,128]{2,1,0:T(8,128)S(1)}, f32[16,256,256]{2,1,0:T(8,128)S(1)}, bf16[16,32,1024]{2,1,0:T(8,128)(2,1)S(1)}) custom-call(s32[17]{0:T(128)S(1)} %pad_add_fusion.meta, bf16[16,32,1024]{2,1,0:T(8,128)(2,1)S(1)} %bitcast.15, ...), custom_call_target="tpu_custom_call", output_to_operand_aliasing={{0}: (7, {}), {1}: (8, {})} | custom-call | flops 18253611008 | bytes 8388608 | tf_op jit(solution)/shard_map/attend_far/pallas_call | solution.py:299
  106.1 23.2 %all_to_all.16 = bf16[32,16,1024]{2,1,0:T(8,128)(2,1)S(1)} all-to-all(bf16[32,16,1024]{2,1,0:T(8,128)(2,1)S(1)} %bitcast.16), channel_id=1, replica_groups={{0,4,8,12,16,20,24,28,32,36,40,44,48,52,56,60,64,68,72,76,80,84,88,92,9..., dimensions={0} | all-to-all | bytes 2097152 | tf_op jit(solution)/shard_map/all_to_all | solution.py:328
  129.3 1.0 unpack.1
  (11 shorter events, 0.0 us)
Async XLA Ops:
  0.0 43.0 %copy-start = (s32[16]{0:T(128)S(1)}, s32[16]{0:T(128)}, u32[]{:S(2)}) copy-start(s32[16]{0:T(128)} %param.10) | copy-start | bytes 196
  19.7 22.8 %all-to-all-start.1 = ((bf16[32,16,1024]{2,1,0:T(8,128)(2,1)}), bf16[32,16,1024]{2,1,0:T(8,128)(2,1)S(1)}, u32[]{:S(2)}, u32[]{:S(2)}) async-start(bf16[32,16,1024]{2,1,0:T(8,128)(2,1)} %bitcast.17), calls=%async_computation.1 | async-start | bytes 2097152 | tf_op jit(solution)/shard_map/all_to_all | solution.py:328
  25.3 14.9 %collective-permute-start.2 = (bf16[16,32,256]{2,1,0:T(8,128)(2,1)S(1)}, bf16[16,32,256]{2,1,0:T(8,128)(2,1)S(1)}, u32[]{:S(2)}, u32[]{:S(2)}) collective-permute-start(bf16[16,32,256]{2,1,0:T(8,128)(2,1)S(1)} %bitcast.18), channel_id=1, source_target_pairs={{0,32},{1,3},{4,36},{5,7},{8,40},{9,11},{12,44},{13,15},{16,48},{1... | collective-permute-start | bytes 786440 | tf_op jit(solution)/shard_map/ppermute | solution.py:331
  26.8 15.0 %collective-permute-start.1 = (bf16[16,32,256]{2,1,0:T(8,128)(2,1)S(1)}, bf16[16,32,256]{2,1,0:T(8,128)(2,1)S(1)}, u32[]{:S(2)}, u32[]{:S(2)}) collective-permute-start(bf16[16,32,256]{2,1,0:T(8,128)(2,1)S(1)} %bitcast.19), channel_id=1, source_target_pairs={{0,48},{1,67},{4,52},{5,71},{8,56},{9,75},{12,60},{13,79},{16,0},{... | collective-permute-start | bytes 786440 | tf_op jit(solution)/shard_map/ppermute | solution.py:331
  26.8 15.7 %collective-permute-start = (bf16[16,32,256]{2,1,0:T(8,128)(2,1)S(1)}, bf16[16,32,256]{2,1,0:T(8,128)(2,1)S(1)}, u32[]{:S(2)}, u32[]{:S(2)}) collective-permute-start(bf16[16,32,256]{2,1,0:T(8,128)(2,1)S(1)} %bitcast.20), channel_id=1, source_target_pairs={{0,16},{1,65},{4,20},{5,69},{8,24},{9,73},{12,28},{13,77},{16,32},... | collective-permute-start | bytes 786440 | tf_op jit(solution)/shard_map/ppermute | solution.py:331
  42.6 3.8 %collective-permute-start.5 = (bf16[4,16,32,256]{3,2,1,0:T(8,128)(2,1)S(1)}, bf16[4,16,32,256]{3,2,1,0:T(8,128)(2,1)S(1)}, u32[]{:S(2)}, u32[]{:S(2)}) collective-permute-start(bf16[4,16,32,256]{3,2,1,0:T(8,128)(2,1)S(1)} %pad_maximum_fusion.refs_1_), channel_id=1, source_target_pairs={{0,1},{1,0},{4,5},{5,4},{8,9},{9,8},{12,13},{13,12},{16,17},{17,16... | collective-permute-start | bytes 3145736 | tf_op jit(solution)/shard_map/ppermute | solution.py:331
  43.1 16.6 %collective-permute-start.4 = (bf16[4,16,32,256]{3,2,1,0:T(8,128)(2,1)S(1)}, bf16[4,16,32,256]{3,2,1,0:T(8,128)(2,1)S(1)}, u32[]{:S(2)}, u32[]{:S(2)}) collective-permute-start(bf16[4,16,32,256]{3,2,1,0:T(8,128)(2,1)S(1)} %pad_maximum_fusion.refs_1_), channel_id=1, source_target_pairs={{0,66},{1,49},{4,70},{5,53},{8,74},{9,57},{12,78},{13,61},{16,82},... | collective-permute-start | bytes 3145736 | tf_op jit(solution)/shard_map/ppermute | solution.py:331
  45.6 16.0 %collective-permute-start.3 = (bf16[4,16,32,256]{3,2,1,0:T(8,128)(2,1)S(1)}, bf16[4,16,32,256]{3,2,1,0:T(8,128)(2,1)S(1)}, u32[]{:S(2)}, u32[]{:S(2)}) collective-permute-start(bf16[4,16,32,256]{3,2,1,0:T(8,128)(2,1)S(1)} %pad_maximum_fusion.refs_1_), channel_id=1, source_target_pairs={{0,64},{1,17},{4,68},{5,21},{8,72},{9,25},{12,76},{13,29},{16,80},... | collective-permute-start | bytes 3145736 | tf_op jit(solution)/shard_map/ppermute | solution.py:331
  61.6 16.3 %collective-permute-start.6 = (bf16[4,16,32,256]{3,2,1,0:T(8,128)(2,1)S(1)}, bf16[4,16,32,256]{3,2,1,0:T(8,128)(2,1)S(1)}, u32[]{:S(2)}, u32[]{:S(2)}) collective-permute-start(bf16[4,16,32,256]{3,2,1,0:T(8,128)(2,1)S(1)} %pad_maximum_fusion.refs_1_), channel_id=1, source_target_pairs={{0,2},{1,33},{4,6},{5,37},{8,10},{9,41},{12,14},{13,45},{16,18},{1... | collective-permute-start | bytes 3145736 | tf_op jit(solution)/shard_map/ppermute | solution.py:331
  62.1 15.8 %collective-permute-start.7 = (bf16[4,16,32,256]{3,2,1,0:T(8,128)(2,1)S(1)}, bf16[4,16,32,256]{3,2,1,0:T(8,128)(2,1)S(1)}, u32[]{:S(2)}, u32[]{:S(2)}) collective-permute-start(bf16[4,16,32,256]{3,2,1,0:T(8,128)(2,1)S(1)} %collective-permute-done.3.refs_1_), channel_id=1, source_target_pairs={{0,1},{1,0},{4,5},{5,4},{8,9},{9,8},{12,13},{13,12},{16,17},{17,16... | collective-permute-start | bytes 3145736 | tf_op jit(solution)/shard_map/ppermute | solution.py:331
  62.1 15.8 %collective-permute-start.8 = (bf16[4,16,32,256]{3,2,1,0:T(8,128)(2,1)S(1)}, bf16[4,16,32,256]{3,2,1,0:T(8,128)(2,1)S(1)}, u32[]{:S(2)}, u32[]{:S(2)}) collective-permute-start(bf16[4,16,32,256]{3,2,1,0:T(8,128)(2,1)S(1)} %collective-permute-done.4.refs_2_), channel_id=1, source_target_pairs={{0,1},{1,0},{4,5},{5,4},{8,9},{9,8},{12,13},{13,12},{16,17},{17,16... | collective-permute-start | bytes 3145736 | tf_op jit(solution)/shard_map/ppermute | solution.py:331
  77.9 2.7 %collective-permute-start.9 = (bf16[4,16,32,256]{3,2,1,0:T(8,128)(2,1)S(1)}, bf16[4,16,32,256]{3,2,1,0:T(8,128)(2,1)S(1)}, u32[]{:S(2)}, u32[]{:S(2)}) collective-permute-start(bf16[4,16,32,256]{3,2,1,0:T(8,128)(2,1)S(1)} %collective-permute-done.6.refs_3_), channel_id=1, source_target_pairs={{0,1},{1,0},{4,5},{5,4},{8,9},{9,8},{12,13},{13,12},{16,17},{17,16... | collective-permute-start | bytes 3145736 | tf_op jit(solution)/shard_map/ppermute | solution.py:331
